TPU v7x, 128 devices: a whole 4x4x4 slice. The times are simulated.
128 devices in a mesh: dp: 16 (over z, y), tensor: 8 (over x, core).
Axes of the slice: x: 4, y: 4, z: 4, core: 2. Of those that a mesh axis runs over, the one named last changes fastest.
Arguments:
- tokens: bfloat16 [32768, 8192], P('dp', 'tensor'), may hold values from -6 to 6
- cotangent: bfloat16 [32768, 1024], P('dp', 'tensor'), may hold values from -6 to 6
- value_matrix: bfloat16 [8192, 1024], P('tensor'), may hold values from -0.0625 to 0.0625
- down_factors: bfloat16 [256, 8192, 64], P('dp', 'tensor'), may hold values from -0.0625 to 0.0625
- up_factors: bfloat16 [256, 64, 1024], P('dp', None, 'tensor'), may hold values from -0.75 to 0.75
- tile_usage_entry: int32 [256], P('dp'), may hold values from 0 to 7, as said below
- usage: int32 [128], replicated, may hold values from 0 to 255, as said below
- storage_row_map: int32 [256], replicated, may hold values from 0 to 255, as said below
Outputs:
- projected: bfloat16 [32768, 1024], P('dp', 'tensor')
- input_gradient: bfloat16 [32768, 8192], P('dp', 'tensor')
- down_gradient: bfloat16 [256, 8192, 64], P('dp', 'tensor')
- up_gradient: bfloat16 [256, 64, 1024], P('dp', None, 'tensor')
Inputs may be any that keep to these rules, and one draw needn't show every extreme that they name: `tile_usage_entry`: each dp index's 256 / 16 entries name every one of its 8 list entries. `usage`: the 8 ids of one dp index are stored (storage_row_map) on 8 different dp indices, storage row // 16. `storage_row_map`: A permutation.
All inputs are finite; a program needn't handle non-finite values.
Results may differ from a plain program's by a relative error of at most 0.02.
Values may be sent and summed in bfloat16 or wider, within the bound.
No kernel may reach another device: no remote copies, remote signals or barrier semaphores. Data moves between devices by JAX's collectives and lax.ppermute only.
A program may use at most 128 MiB of HBM per device.

v0:
```python
import jax
import jax.numpy as jnp
from jax import lax
from jax.experimental import pallas as pl
from jax.experimental.pallas import tpu as pltpu
from jax.sharding import PartitionSpec as P

TILE = 128
ADAPTER_SCALE = 2.0
F32 = jnp.float32
BF16 = jnp.bfloat16
ANY = pl.BlockSpec(memory_space=pl.ANY)
SMEM = pl.BlockSpec(memory_space=pltpu.SMEM)
VMEM = pl.BlockSpec(memory_space=pltpu.VMEM)
LIMIT = 48 * 1024 * 1024


def dot(a, b, contract):
    return lax.dot_general(a, b, ((contract[:1], contract[1:]), ((), ())), preferred_element_type=F32)


def cost(flops, nbytes):
    return pl.CostEstimate(flops=flops, bytes_accessed=nbytes, transcendentals=0)


def params():
    return pltpu.CompilerParams(vmem_limit_bytes=LIMIT)


def copy_rows(rows, source, target, sems):
    count = target.shape[0]
    copies = []
    for user in range(count):
        row = jnp.maximum(rows[user], 0)
        copies.append(pltpu.make_async_copy(source.at[row], target.at[user], sems.at[user]))
        copies[-1].start()
    for copy in copies:
        copy.wait()


def route_up(me, usage, storage_row_map, entries, up, holding):
    users = usage.shape[0] // 8
    tiles = entries.shape[0]

    def kernel(me_ref, usage_ref, map_ref, entry_ref, up_ref, rows_ref, holders_ref, send_ref, sems):
        mine = me_ref[0]
        for user in range(users):
            row = jnp.int32(-1)
            for slot in range(8):
                place = map_ref[usage_ref[user * 8 + slot]]
                row = jnp.where(place // holding == mine, place % holding, row)
            rows_ref[user] = row
        for tile in range(tiles):
            holders_ref[tile] = map_ref[usage_ref[mine * 8 + entry_ref[tile]]] // holding
        copy_rows(rows_ref, up_ref, send_ref, sems)

    return pl.pallas_call(
        kernel,
        out_shape=(
            jax.ShapeDtypeStruct((users,), jnp.int32),
            jax.ShapeDtypeStruct((tiles,), jnp.int32),
            jax.ShapeDtypeStruct((users,) + up.shape[1:], BF16),
        ),
        in_specs=[SMEM, SMEM, SMEM, SMEM, ANY],
        out_specs=(SMEM, SMEM, ANY),
        scratch_shapes=[pltpu.SemaphoreType.DMA((users,))],
        compiler_params=params(),
        cost_estimate=cost(0, 2 * up.size * 2),
        name="route_up",
    )(me, usage, storage_row_map, entries, up)


def select_rows(rows, stored):
    users = rows.shape[0]
    return pl.pallas_call(
        copy_rows,
        out_shape=jax.ShapeDtypeStruct((users,) + stored.shape[1:], BF16),
        in_specs=[SMEM, ANY],
        out_specs=ANY,
        scratch_shapes=[pltpu.SemaphoreType.DMA((users,))],
        compiler_params=params(),
        cost_estimate=cost(0, 2 * stored.size * 2),
        name="select_down",
    )(rows, stored)


def base_product(tokens, value_matrix, shards_number):
    rows, features = tokens.shape
    columns = value_matrix.shape[1]
    width = columns // shards_number
    block = 512

    def kernel(x_ref, v_ref, o_ref):
        product = dot(x_ref[...], v_ref[...], (1, 0))
        for index in range(shards_number):
            o_ref[index] = product[:, index * width : (index + 1) * width].astype(BF16)

    return pl.pallas_call(
        kernel,
        grid=(rows // block,),
        out_shape=jax.ShapeDtypeStruct((shards_number, rows, width), BF16),
        in_specs=[
            pl.BlockSpec((block, features), lambda i: (i, 0)),
            pl.BlockSpec((features, columns), lambda i: (0, 0)),
        ],
        out_specs=pl.BlockSpec((shards_number, block, width), lambda i: (0, i, 0)),
        compiler_params=params(),
        cost_estimate=cost(2 * rows * features * columns, 2 * (rows * features + features * columns + rows * columns)),
        name="base_product",
    )(tokens, value_matrix)


def back_product(holders, up, cotangent):
    tiles = holders.shape[0]

    def kernel(h_ref, up_ref, dy_ref, o_ref):
        for tile in range(tiles):
            o_ref[tile] = dot(
                up_ref[h_ref[tile]], dy_ref[tile * TILE : (tile + 1) * TILE, :], (1, 1)
            ).astype(BF16)

    return pl.pallas_call(
        kernel,
        out_shape=jax.ShapeDtypeStruct((tiles, up.shape[1], TILE), BF16),
        in_specs=[SMEM, VMEM, VMEM],
        out_specs=VMEM,
        compiler_params=params(),
        cost_estimate=cost(2 * cotangent.size * up.shape[1], 2 * 3 * cotangent.size),
        name="back_product",
    )(holders, up, cotangent)


def low_product(holders, down, tokens):
    tiles = holders.shape[0]
    rows, features = tokens.shape
    rank = down.shape[1]
    group = 4

    def kernel(h_ref, down_ref, x_ref, o_ref):
        first = pl.program_id(0) * group
        for tile in range(group):
            o_ref[tile] = dot(
                down_ref[h_ref[first + tile]], x_ref[tile * TILE : (tile + 1) * TILE, :], (1, 1)
            ).astype(BF16)

    return pl.pallas_call(
        kernel,
        grid=(tiles // group,),
        out_shape=jax.ShapeDtypeStruct((tiles, rank, TILE), BF16),
        in_specs=[
            SMEM,
            pl.BlockSpec(down.shape, lambda i: (0, 0, 0)),
            pl.BlockSpec((group * TILE, features), lambda i: (i, 0)),
        ],
        out_specs=pl.BlockSpec((group, rank, TILE), lambda i: (i, 0, 0)),
        compiler_params=params(),
        cost_estimate=cost(8 * tokens.size * rank, 2 * (tokens.size + down.size)),
        name="low_product",
    )(holders, down, tokens)


def gradient_terms(holders, rank_side, wide_side, owners, step):
    tiles, rank, _ = rank_side.shape
    rows, width = wide_side.shape

    def kernel(h_ref, r_ref, w_ref, o_ref, total):
        total[...] = jnp.zeros_like(total)
        for tile in range(tiles):
            total[h_ref[tile]] += dot(r_ref[tile], w_ref[tile * TILE : (tile + 1) * TILE, :], (1, 0))
        o_ref[...] = (ADAPTER_SCALE * total[...]).astype(BF16)

    return pl.pallas_call(
        kernel,
        grid=(width // step,),
        out_shape=jax.ShapeDtypeStruct((owners, rank, width), BF16),
        in_specs=[
            SMEM,
            pl.BlockSpec(rank_side.shape, lambda i: (0, 0, 0)),
            pl.BlockSpec((rows, step), lambda i: (0, i)),
        ],
        out_specs=pl.BlockSpec((owners, rank, step), lambda i: (0, 0, i)),
        scratch_shapes=[pltpu.VMEM((owners, rank, step), F32)],
        compiler_params=params(),
        cost_estimate=cost(8 * wide_side.size * rank, 2 * (wide_side.size + owners * rank * width)),
        name="gradient_terms",
    )(holders, rank_side, wide_side)


def combine(rows, received, holding, step):
    users, rank, width = received.shape

    def kernel(rows_ref, r_ref, o_ref, total):
        total[...] = jnp.zeros_like(total)
        for user in range(users):

            @pl.when(rows_ref[user] >= 0)
            def _():
                total[jnp.maximum(rows_ref[user], 0)] += r_ref[user].astype(F32)

        o_ref[...] = total[...].astype(BF16)

    return pl.pallas_call(
        kernel,
        grid=(width // step,),
        out_shape=jax.ShapeDtypeStruct((holding, rank, width), BF16),
        in_specs=[SMEM, pl.BlockSpec((users, rank, step), lambda i: (0, 0, i))],
        out_specs=pl.BlockSpec((holding, rank, step), lambda i: (0, 0, i)),
        scratch_shapes=[pltpu.VMEM((holding, rank, step), F32)],
        compiler_params=params(),
        cost_estimate=cost(4 * received.size, 4 * received.size),
        name="combine",
    )(rows, received)


def finish_projected(holders, frozen, lowrank, up):
    tiles = holders.shape[0]

    def kernel(h_ref, f_ref, l_ref, up_ref, o_ref):
        for tile in range(tiles):
            span = slice(tile * TILE, (tile + 1) * TILE)
            adapter = dot(l_ref[tile], up_ref[h_ref[tile]], (0, 0))
            o_ref[span, :] = (f_ref[span, :].astype(F32) + ADAPTER_SCALE * adapter).astype(BF16)

    return pl.pallas_call(
        kernel,
        out_shape=jax.ShapeDtypeStruct(frozen.shape, BF16),
        in_specs=[SMEM, VMEM, VMEM, VMEM],
        out_specs=VMEM,
        compiler_params=params(),
        cost_estimate=cost(2 * frozen.size * up.shape[1], 8 * frozen.size),
        name="finish_projected",
    )(holders, frozen, lowrank, up)


def input_product(holders, dy_full, value_matrix, back_low, down):
    rows, columns = dy_full.shape
    features = value_matrix.shape[0]
    rank = down.shape[1]
    group = 4

    def kernel(h_ref, dy_ref, v_ref, b_ref, down_ref, o_ref):
        first = pl.program_id(0) * group
        frozen = dot(dy_ref[...], v_ref[...], (1, 1))
        for tile in range(group):
            span = slice(tile * TILE, (tile + 1) * TILE)
            adapter = dot(b_ref[tile], down_ref[h_ref[first + tile]], (0, 0))
            o_ref[span, :] = (frozen[span, :] + ADAPTER_SCALE * adapter).astype(BF16)

    return pl.pallas_call(
        kernel,
        grid=(rows // (group * TILE),),
        out_shape=jax.ShapeDtypeStruct((rows, features), BF16),
        in_specs=[
            SMEM,
            pl.BlockSpec((group * TILE, columns), lambda i: (i, 0)),
            pl.BlockSpec(value_matrix.shape, lambda i: (0, 0)),
            pl.BlockSpec((group, rank, TILE), lambda i: (i, 0, 0)),
            pl.BlockSpec(down.shape, lambda i: (0, 0, 0)),
        ],
        out_specs=pl.BlockSpec((group * TILE, features), lambda i: (i, 0)),
        compiler_params=params(),
        cost_estimate=cost(2 * rows * columns * features, 2 * (dy_full.size + value_matrix.size + rows * features)),
        name="input_product",
    )(holders, dy_full, value_matrix, back_low, down)


def sum_over_tensor(part, half):
    size = lax.axis_size("tensor")
    chips = size // 2
    count = part.shape[0] // 2
    swap = [(i, i ^ 1) for i in range(size)]

    def along_x(array, k):
        return lax.ppermute(array, "tensor", [(i, (i // 2 + k) % chips * 2 + i % 2) for i in range(size)])

    both = (part.astype(F32) + lax.ppermute(part, "tensor", swap).astype(F32)).astype(BF16)
    own = lax.dynamic_slice_in_dim(both, half * count, count, 0)
    total = own.astype(F32)
    for k in range(1, chips):
        total = total + along_x(own, k).astype(F32)
    total = total.astype(BF16)
    other = lax.ppermute(total, "tensor", swap)
    first = jnp.where(half == 0, total, other)
    second = jnp.where(half == 0, other, total)
    return jnp.concatenate([first, second], axis=0)


def shards(
    tokens,
    cotangent,
    value_matrix,
    down_factors,
    up_factors,
    tile_usage_entry,
    usage,
    storage_row_map,
):
    owners = lax.axis_size("dp")
    tensor_size = lax.axis_size("tensor")
    half = lax.axis_index("tensor") % 2
    me = lax.axis_index("dp").astype(jnp.int32).reshape(1)
    holding = down_factors.shape[0]
    down_stored = jnp.transpose(down_factors, (0, 2, 1))

    dy_full = lax.all_gather(cotangent, "tensor", axis=1, tiled=True)
    rows, holders, send_up = route_up(me, usage, storage_row_map, tile_usage_entry, up_factors, holding)
    up = lax.all_to_all(send_up, "dp", split_axis=0, concat_axis=0, tiled=True)
    send_down = select_rows(rows, down_stored)
    down = lax.all_to_all(send_down, "dp", split_axis=0, concat_axis=0, tiled=True)

    base_part = base_product(tokens, value_matrix, tensor_size)
    frozen = lax.psum_scatter(base_part, "tensor", scatter_dimension=0, tiled=False)

    back_low = sum_over_tensor(back_product(holders, up, cotangent), half)
    send_down_terms = gradient_terms(holders, back_low, tokens, owners, 256)
    down_terms = lax.all_to_all(send_down_terms, "dp", split_axis=0, concat_axis=0, tiled=True)

    lowrank = sum_over_tensor(low_product(holders, down, tokens), half)
    send_up_terms = gradient_terms(holders, lowrank, cotangent, owners, cotangent.shape[1])
    up_terms = lax.all_to_all(send_up_terms, "dp", split_axis=0, concat_axis=0, tiled=True)

    input_gradient = input_product(holders, dy_full, value_matrix, back_low, down)
    projected = finish_projected(holders, frozen, lowrank, up)
    up_gradient = combine(rows, up_terms, holding, up_terms.shape[2])
    down_gradient = jnp.transpose(combine(rows, down_terms, holding, 256), (0, 2, 1))
    return (projected, input_gradient, down_gradient, up_gradient)


def solution(mesh):
    return jax.shard_map(
        shards,
        mesh=mesh,
        in_specs=(
            P("dp", "tensor"),
            P("dp", "tensor"),
            P("tensor", None),
            P("dp", "tensor", None),
            P("dp", None, "tensor"),
            P("dp"),
            P(),
            P(),
        ),
        out_specs=(
            P("dp", "tensor"),
            P("dp", "tensor"),
            P("dp", "tensor", None),
            P("dp", None, "tensor"),
        ),
        check_vma=False,
    )
```

profile of v0, /device:TPU:0, one launch (start us, length us, event | category | flops | bytes accessed | tf_op | source)
XLA Modules:
  0.0 173.0 jit_solution(8548552655834632211)
XLA Ops:
  8.0 1.6 copy-done.8
  9.5 7.7 %base_product.1 = bf16[8,2048,128]{2,1,0:T(8,128)(2,1)} custom-call(bf16[2048,1024]{1,0:T(8,128)(2,1)} %w_ref.2, bf16[1024,1024]{1,0:T(8,128)(2,1)S(1)} %copy-done.8), custom_call_target="tpu_custom_call" | custom-call | flops 4294967296 | bytes 10485760 | tf_op jit(solution)/shard_map/base_product/pallas_call | solution.py:98
  18.2 2.8 %route_up.1 = (s32[16]{0:T(128)S(1)}, s32[16]{0:T(128)S(1)}, bf16[16,64,128]{2,1,0:T(8,128)(2,1)}) custom-call(s32[1]{0:T(128)} %bitcast.me_ref, s32[128]{0:T(128)S(1)} %copy-done.6, s32[256]{0:T(256)S(1)} %copy-done.5, s32[16]{0:T(128)S(1)} %copy-done.7, bf16[16,64,128]{2,1,0:T(8,128)(2,1)S(1)} %copy-done.4), custom_call_target="tpu_custom_call" | custom-call | bytes 524288 | tf_op jit(solution)/shard_map/route_up/pallas_call | solution.py:57
  21.0 1.7 copy-done.2
  22.8 3.5 %select_down.1 = bf16[16,64,1024]{2,1,0:T(8,128)(2,1)S(1)} custom-call(s32[16]{0:T(128)S(1)} %get-tuple-element.8.rows.rows_ref, bf16[16,64,1024]{2,1,0:T(8,128)(2,1)S(1)} %bitcast.4), custom_call_target="tpu_custom_call" | custom-call | bytes 4194304 | tf_op jit(solution)/shard_map/select_down/pallas_call | solution.py:75
  26.3 36.4 %all_to_all.20.down_ref = bf16[16,64,1024]{2,1,0:T(8,128)(2,1)S(1)} all-to-all(bf16[16,64,1024]{2,1,0:T(8,128)(2,1)S(1)} %select_down.1), channel_id=1, replica_groups=mesh['dp'=16,'tensor'=8] {'dp'}, dimensions={0} | all-to-all | bytes 4194304 | tf_op jit(solution)/shard_map/all_to_all | solution.py:309
  62.7 3.5 %all-to-all-start.1 = ((bf16[16,64,128]{2,1,0:T(8,128)(2,1)}), bf16[16,64,128]{2,1,0:T(8,128)(2,1)S(1)}, u32[]{:S(2)}, u32[]{:S(2)}) async-start(bf16[16,64,128]{2,1,0:T(8,128)(2,1)} %get-tuple-element.9), calls=%async_computation.2 | async-start | bytes 524288 | tf_op jit(solution)/shard_map/all_to_all | solution.py:307
  66.2 4.2 %low_product.1 = bf16[16,64,128]{2,1,0:T(8,128)(2,1)S(1)} custom-call(s32[16]{0:T(128)S(1)} %get-tuple-element.7.h_ref, bf16[16,64,1024]{2,1,0:T(8,128)(2,1)S(1)} %all_to_all.20.down_ref, bf16[2048,1024]{1,0:T(8,128)(2,1)} %w_ref.2), custom_call_target="tpu_custom_call" | custom-call | flops 1073741824 | bytes 6291456 | tf_op jit(solution)/shard_map/low_product/pallas_call | solution.py:146
  70.5 4.4 %all-to-all-done.1.up_ref = bf16[16,64,128]{2,1,0:T(8,128)(2,1)S(1)} async-done(((bf16[16,64,128]{2,1,0:T(8,128)(2,1)}), bf16[16,64,128]{2,1,0:T(8,128)(2,1)S(1)}, u32[]{:S(2)}, u32[]{:S(2)}) %all-to-all-start.1) | async-done | bytes 262176 | tf_op jit(solution)/shard_map/all_to_all | solution.py:307
  76.9 2.8 %collective-permute-start.3 = (bf16[8,64,128]{2,1,0:T(8,128)(2,1)S(1)}, bf16[8,64,128]{2,1,0:T(8,128)(2,1)S(1)}, u32[]{:S(2)}, u32[]{:S(2)}) collective-permute-start(bf16[8,64,128]{2,1,0:T(8,128)(2,1)S(1)} %add_convert_fusion.3), channel_id=1, source_target_pairs={{0,6},{1,7},{2,0},{3,1},{4,2},{5,3},{6,4},{7,5},{8,14},{9,15},{10,... | collective-permute-start | bytes 393224 | tf_op jit(solution)/shard_map/ppermute | solution.py:274
  82.4 2.4 %collective-permute-start.8 = (bf16[8,64,128]{2,1,0:T(8,128)(2,1)S(1)}, bf16[8,64,128]{2,1,0:T(8,128)(2,1)S(1)}, u32[]{:S(2)}, u32[]{:S(2)}) collective-permute-start(bf16[8,64,128]{2,1,0:T(8,128)(2,1)S(1)} %add_convert_fusion.1), channel_id=1, source_target_pairs={{0,6},{1,7},{2,0},{3,1},{4,2},{5,3},{6,4},{7,5},{8,14},{9,15},{10,... | collective-permute-start | bytes 393224 | tf_op jit(solution)/shard_map/ppermute | solution.py:274
  86.8 2.3 %collective-permute-done.2 = bf16[8,64,128]{2,1,0:T(8,128)(2,1)} collective-permute-done((bf16[8,64,128]{2,1,0:T(8,128)(2,1)S(1)}, bf16[8,64,128]{2,1,0:T(8,128)(2,1)}, u32[]{:S(2)}, u32[]{:S(2)}) %collective-permute-start.2) | collective-permute-done | bytes 131104 | tf_op jit(solution)/shard_map/ppermute | solution.py:274
  92.8 2.2 %collective-permute-done.7 = bf16[8,64,128]{2,1,0:T(8,128)(2,1)S(1)} collective-permute-done((bf16[8,64,128]{2,1,0:T(8,128)(2,1)S(1)}, bf16[8,64,128]{2,1,0:T(8,128)(2,1)S(1)}, u32[]{:S(2)}, u32[]{:S(2)}) %collective-permute-start.7) | collective-permute-done | bytes 131104 | tf_op jit(solution)/shard_map/ppermute | solution.py:274
  95.0 3.3 %collective-permute-done.6 = bf16[8,64,128]{2,1,0:T(8,128)(2,1)S(1)} collective-permute-done((bf16[8,64,128]{2,1,0:T(8,128)(2,1)S(1)}, bf16[8,64,128]{2,1,0:T(8,128)(2,1)S(1)}, u32[]{:S(2)}, u32[]{:S(2)}) %collective-permute-start.6) | collective-permute-done | bytes 131104 | tf_op jit(solution)/shard_map/ppermute | solution.py:274
  98.6 1.6 gradient_terms.3
  100.2 3.8 %all-to-all-start.3 = ((bf16[16,64,128]{2,1,0:T(8,128)(2,1)}), bf16[16,64,128]{2,1,0:T(8,128)(2,1)S(1)}, u32[]{:S(2)}, u32[]{:S(2)}) async-start(bf16[16,64,128]{2,1,0:T(8,128)(2,1)} %gradient_terms.3), calls=%async_computation.4 | async-start | bytes 524288 | tf_op jit(solution)/shard_map/all_to_all | solution.py:320
  104.1 4.0 %gradient_terms.2 = bf16[16,64,1024]{2,1,0:T(8,128)(2,1)S(1)} custom-call(s32[16]{0:T(128)S(1)} %get-tuple-element.7.h_ref, bf16[16,64,128]{2,1,0:T(8,128)(2,1)S(1)} %pad_maximum_fusion.1.b_ref.r_ref, bf16[2048,1024]{1,0:T(8,128)(2,1)} %w_ref.2), custom_call_target="tpu_custom_call" | custom-call | flops 1073741824 | bytes 6291456 | tf_op jit(solution)/shard_map/gradient_terms/pallas_call | solution.py:172
  109.4 3.9 %all-to-all-done.3.r_ref = bf16[16,64,128]{2,1,0:T(8,128)(2,1)S(1)} async-done(((bf16[16,64,128]{2,1,0:T(8,128)(2,1)}), bf16[16,64,128]{2,1,0:T(8,128)(2,1)S(1)}, u32[]{:S(2)}, u32[]{:S(2)}) %all-to-all-start.3) | async-done | bytes 262176 | tf_op jit(solution)/shard_map/all_to_all | solution.py:320
  113.3 4.4 %all-to-all-start.2 = ((bf16[16,64,1024]{2,1,0:T(8,128)(2,1)}), bf16[16,64,1024]{2,1,0:T(8,128)(2,1)}, u32[]{:S(2)}, u32[]{:S(2)}) async-start(bf16[16,64,1024]{2,1,0:T(8,128)(2,1)} %copy-done), calls=%async_computation.3 | async-start | bytes 4194304 | tf_op jit(solution)/shard_map/all_to_all | solution.py:316
  119.3 29.7 %all-to-all-done.2.r_ref = bf16[16,64,1024]{2,1,0:T(8,128)(2,1)} async-done(((bf16[16,64,1024]{2,1,0:T(8,128)(2,1)}), bf16[16,64,1024]{2,1,0:T(8,128)(2,1)}, u32[]{:S(2)}, u32[]{:S(2)}) %all-to-all-start.2) | async-done | bytes 2097184 | tf_op jit(solution)/shard_map/all_to_all | solution.py:316
  149.0 4.3 %combine.2 = bf16[16,64,1024]{2,1,0:T(8,128)(2,1)} custom-call(s32[16]{0:T(128)S(1)} %get-tuple-element.8.rows.rows_ref, bf16[16,64,1024]{2,1,0:T(8,128)(2,1)} %all-to-all-done.2.r_ref), custom_call_target="tpu_custom_call" | custom-call | flops 4194304 | bytes 4194304 | tf_op jit(solution)/shard_map/combine/pallas_call | solution.py:202
  153.3 1.6 copy-done.9
  154.9 8.6 %input_product.1 = bf16[2048,1024]{1,0:T(8,128)(2,1)} custom-call(s32[16]{0:T(128)S(1)} %get-tuple-element.7.h_ref, bf16[2048,1024]{1,0:T(8,128)(2,1)} %all-gather.2.cloned.1.call-done.dy_ref, bf16[1024,1024]{1,0:T(8,128)(2,1)S(1)} %copy-done.9, bf16[16,64,128]{2,1,0:T(8,128)(2,1)S(1)} %pad_maximum_fusion.1.b_ref.r_ref, ...), custom_call_target="tpu_custom_call" | custom-call | flops 4294967296 | bytes 10485760 | tf_op jit(solution)/shard_map/input_product/pallas_call | solution.py:249
  164.5 1.7 finish_projected.1
  (48 shorter events, 16.3 us)
Async XLA Ops:
  7.2 146.1 %all-gather.2.cloned.1.call-start = ((), (), s32[]{:S(2)}) async-start(), calls=%async_computation.6 | async-start | bytes 4718592 | tf_op jit(solution)/shard_map/all_gather | solution.py:305
  7.9 155.5 %reduce-scatter.2.cloned.1.call-start = ((), (), s32[]{:S(2)}) async-start(), calls=%async_computation.5 | async-start | bytes 4718592 | tf_op jit(solution)/shard_map/reduce_scatter | solution.py:312
  7.9 1.6 copy-start.8
  17.2 1.0 copy-start.5
  17.2 1.0 copy-start.6
  17.2 1.0 copy-start.7
  21.0 1.7 %copy-start.2 = (bf16[16,1024,64]{1,2,0:T(8,128)(2,1)S(1)}, bf16[16,1024,64]{1,2,0:T(8,128)(2,1)}, u32[]{:S(2)}) copy-start(bf16[16,1024,64]{1,2,0:T(8,128)(2,1)} %param.11) | copy-start | bytes 6291460
  62.7 12.2 %all-to-all-start.1 = ((bf16[16,64,128]{2,1,0:T(8,128)(2,1)}), bf16[16,64,128]{2,1,0:T(8,128)(2,1)S(1)}, u32[]{:S(2)}, u32[]{:S(2)}) async-start(bf16[16,64,128]{2,1,0:T(8,128)(2,1)} %get-tuple-element.9), calls=%async_computation.2 | async-start | bytes 524288 | tf_op jit(solution)/shard_map/all_to_all | solution.py:307
  66.2 8.7 %copy-start.1 = (bf16[2048,128]{1,0:T(8,128)(2,1)S(1)}, bf16[2048,128]{1,0:T(8,128)(2,1)}, u32[]{:S(2)}) copy-start(bf16[2048,128]{1,0:T(8,128)(2,1)} %w_ref.3) | copy-start | bytes 1572868
  70.4 5.6 %collective-permute-start = (bf16[16,64,128]{2,1,0:T(8,128)(2,1)S(1)}, bf16[16,64,128]{2,1,0:T(8,128)(2,1)}, u32[]{:S(2)}, u32[]{:S(2)}) collective-permute-start(bf16[16,64,128]{2,1,0:T(8,128)(2,1)S(1)} %low_product.1), channel_id=1, source_target_pairs={{0,1},{1,0},{2,3},{3,2},{4,5},{5,4},{6,7},{7,6},{8,9},{9,8},{10,11... | collective-permute-start | bytes 786440 | tf_op jit(solution)/shard_map/ppermute | solution.py:276
  75.8 5.6 %collective-permute-start.5 = (bf16[16,64,128]{2,1,0:T(8,128)(2,1)S(1)}, bf16[16,64,128]{2,1,0:T(8,128)(2,1)}, u32[]{:S(2)}, u32[]{:S(2)}) collective-permute-start(bf16[16,64,128]{2,1,0:T(8,128)(2,1)S(1)} %back_product.1), channel_id=1, source_target_pairs={{0,1},{1,0},{2,3},{3,2},{4,5},{5,4},{6,7},{7,6},{8,9},{9,8},{10,11... | collective-permute-start | bytes 786440 | tf_op jit(solution)/shard_map/ppermute | solution.py:276
  76.9 9.9 %collective-permute-start.3 = (bf16[8,64,128]{2,1,0:T(8,128)(2,1)S(1)}, bf16[8,64,128]{2,1,0:T(8,128)(2,1)S(1)}, u32[]{:S(2)}, u32[]{:S(2)}) collective-permute-start(bf16[8,64,128]{2,1,0:T(8,128)(2,1)S(1)} %add_convert_fusion.3), channel_id=1, source_target_pairs={{0,6},{1,7},{2,0},{3,1},{4,2},{5,3},{6,4},{7,5},{8,14},{9,15},{10,... | collective-permute-start | bytes 393224 | tf_op jit(solution)/shard_map/ppermute | solution.py:274
  79.8 9.3 %collective-permute-start.2 = (bf16[8,64,128]{2,1,0:T(8,128)(2,1)S(1)}, bf16[8,64,128]{2,1,0:T(8,128)(2,1)}, u32[]{:S(2)}, u32[]{:S(2)}) collective-permute-start(bf16[8,64,128]{2,1,0:T(8,128)(2,1)S(1)} %add_convert_fusion.3), channel_id=1, source_target_pairs={{0,4},{1,5},{2,6},{3,7},{4,0},{5,1},{6,2},{7,3},{8,12},{9,13},{10,... | collective-permute-start | bytes 393224 | tf_op jit(solution)/shard_map/ppermute | solution.py:274
  80.6 10.0 %collective-permute-start.1 = (bf16[8,64,128]{2,1,0:T(8,128)(2,1)S(1)}, bf16[8,64,128]{2,1,0:T(8,128)(2,1)}, u32[]{:S(2)}, u32[]{:S(2)}) collective-permute-start(bf16[8,64,128]{2,1,0:T(8,128)(2,1)S(1)} %add_convert_fusion.3), channel_id=1, source_target_pairs={{0,2},{1,3},{2,4},{3,5},{4,6},{5,7},{6,0},{7,1},{8,10},{9,11},{10,... | collective-permute-start | bytes 393224 | tf_op jit(solution)/shard_map/ppermute | solution.py:274
  82.4 10.4 %collective-permute-start.8 = (bf16[8,64,128]{2,1,0:T(8,128)(2,1)S(1)}, bf16[8,64,128]{2,1,0:T(8,128)(2,1)S(1)}, u32[]{:S(2)}, u32[]{:S(2)}) collective-permute-start(bf16[8,64,128]{2,1,0:T(8,128)(2,1)S(1)} %add_convert_fusion.1), channel_id=1, source_target_pairs={{0,6},{1,7},{2,0},{3,1},{4,2},{5,3},{6,4},{7,5},{8,14},{9,15},{10,... | collective-permute-start | bytes 393224 | tf_op jit(solution)/shard_map/ppermute | solution.py:274
  84.8 10.2 %collective-permute-start.7 = (bf16[8,64,128]{2,1,0:T(8,128)(2,1)S(1)}, bf16[8,64,128]{2,1,0:T(8,128)(2,1)S(1)}, u32[]{:S(2)}, u32[]{:S(2)}) collective-permute-start(bf16[8,64,128]{2,1,0:T(8,128)(2,1)S(1)} %add_convert_fusion.1), channel_id=1, source_target_pairs={{0,4},{1,5},{2,6},{3,7},{4,0},{5,1},{6,2},{7,3},{8,12},{9,13},{10,... | collective-permute-start | bytes 393224 | tf_op jit(solution)/shard_map/ppermute | solution.py:274
  86.8 11.6 %collective-permute-start.6 = (bf16[8,64,128]{2,1,0:T(8,128)(2,1)S(1)}, bf16[8,64,128]{2,1,0:T(8,128)(2,1)S(1)}, u32[]{:S(2)}, u32[]{:S(2)}) collective-permute-start(bf16[8,64,128]{2,1,0:T(8,128)(2,1)S(1)} %add_convert_fusion.1), channel_id=1, source_target_pairs={{0,2},{1,3},{2,4},{3,5},{4,6},{5,7},{6,0},{7,1},{8,10},{9,11},{10,... | collective-permute-start | bytes 393224 | tf_op jit(solution)/shard_map/ppermute | solution.py:274
  91.6 6.9 %collective-permute-start.4 = (bf16[8,64,128]{2,1,0:T(8,128)(2,1)S(1)}, bf16[8,64,128]{2,1,0:T(8,128)(2,1)S(1)}, u32[]{:S(2)}, u32[]{:S(2)}) collective-permute-start(bf16[8,64,128]{2,1,0:T(8,128)(2,1)S(1)} %add_convert_fusion.2), channel_id=1, source_target_pairs={{0,1},{1,0},{2,3},{3,2},{4,5},{5,4},{6,7},{7,6},{8,9},{9,8},{10,11... | collective-permute-start | bytes 393224 | tf_op jit(solution)/shard_map/ppermute | solution.py:282
  98.4 5.6 %collective-permute-start.9 = (bf16[8,64,128]{2,1,0:T(8,128)(2,1)S(1)}, bf16[8,64,128]{2,1,0:T(8,128)(2,1)S(1)}, u32[]{:S(2)}, u32[]{:S(2)}) collective-permute-start(bf16[8,64,128]{2,1,0:T(8,128)(2,1)S(1)} %add_convert_fusion), channel_id=1, source_target_pairs={{0,1},{1,0},{2,3},{3,2},{4,5},{5,4},{6,7},{7,6},{8,9},{9,8},{10,11... | collective-permute-start | bytes 393224 | tf_op jit(solution)/shard_map/ppermute | solution.py:282
  100.2 13.2 %all-to-all-start.3 = ((bf16[16,64,128]{2,1,0:T(8,128)(2,1)}), bf16[16,64,128]{2,1,0:T(8,128)(2,1)S(1)}, u32[]{:S(2)}, u32[]{:S(2)}) async-start(bf16[16,64,128]{2,1,0:T(8,128)(2,1)} %gradient_terms.3), calls=%async_computation.4 | async-start | bytes 524288 | tf_op jit(solution)/shard_map/all_to_all | solution.py:320
  108.1 1.3 copy-start
  113.3 35.6 %all-to-all-start.2 = ((bf16[16,64,1024]{2,1,0:T(8,128)(2,1)}), bf16[16,64,1024]{2,1,0:T(8,128)(2,1)}, u32[]{:S(2)}, u32[]{:S(2)}) async-start(bf16[16,64,1024]{2,1,0:T(8,128)(2,1)} %copy-done), calls=%async_computation.3 | async-start | bytes 4194304 | tf_op jit(solution)/shard_map/all_to_all | solution.py:316
  153.3 1.6 copy-start.9
  163.4 1.0 copy-start.3
  (1 other events, 0.9 us)
Sparse Core Ops, SparseCore 0:
  9.7 38.4 all-gather.1
  50.6 48.9 reduce-scatter.1
where the time goes:
time: 174 us; the launch traced here: 173 us
  waiting for transfers between devices  49.6 us (29%)
  Pallas kernels  40.7 us (23%)
  blocking collectives  36.4 us (21%)
  starting transfers between devices  20.7 us (12%)
  between operations  14.3 us (8%)
  local copies, waits for them, and re-layouts  8.18 us (5%)
  other arithmetic  3.16 us (2%)
    all_to_all x1, blocking collectives, shards(): lax.all_to_all(send_down, 'dp', split_axis=0, concat_axis=0, tiled=True)  36.4 us
    all_to_all x1, waiting for transfers between devices, shards(): lax.all_to_all(send_down_terms, 'dp', split_axis=0, concat_axis=0, tiled=...  29.7 us
    ppermute x6, waiting for transfers between devices, along_x(): lax.ppermute(array, 'tensor', [(i, (i // 2 + k) % chips * 2 + i % 2) for...  10.9 us
    pallas_call x1, Pallas kernels, input_product(): pl.pallas_call(kernel, grid=(rows // (group * TILE),), out_shape=jax.Shap...  8.55 us
    ppermute x6, starting transfers between devices, along_x(): lax.ppermute(array, 'tensor', [(i, (i // 2 + k) % chips * 2 + i % 2) for...  8.45 us
    unnamed x20, local copies, waits for them, and re-layouts  8.18 us
    pallas_call x1, Pallas kernels, base_product(): pl.pallas_call(kernel, grid=(rows // block,), out_shape=jax.ShapeDtypeStr...  7.7 us
    pallas_call x2, Pallas kernels, combine(): pl.pallas_call(kernel, grid=(width // step,), out_shape=jax.ShapeDtypeStr...  5.77 us
  transfers between devices with their start and end apart: 15, of which 9 were waited for; matrix products, arithmetic and copies ran while one was open for 2% of the time, Pallas kernels for 23%

commit v1 on v0

--- a/solution.py
+++ b/solution.py
@@ -9,50 +9,70 @@
 ADAPTER_SCALE = 2.0
 F32 = jnp.float32
 BF16 = jnp.bfloat16
-ANY = pl.BlockSpec(memory_space=pl.ANY)
+HBM = pl.BlockSpec(memory_space=pltpu.HBM)
 SMEM = pl.BlockSpec(memory_space=pltpu.SMEM)
 VMEM = pl.BlockSpec(memory_space=pltpu.VMEM)
-LIMIT = 48 * 1024 * 1024
+LIMIT = 62 * 1024 * 1024
 
 
 def dot(a, b, contract):
     return lax.dot_general(a, b, ((contract[:1], contract[1:]), ((), ())), preferred_element_type=F32)
 
 
-def cost(flops, nbytes):
-    return pl.CostEstimate(flops=flops, bytes_accessed=nbytes, transcendentals=0)
+def cost(nbytes=1024):
+    return pl.CostEstimate(flops=1024, bytes_accessed=nbytes, transcendentals=0)
+
+
+def after(value, *others):
+    return lax.optimization_barrier((value,) + others)[0]
 
 
 def params():
     return pltpu.CompilerParams(vmem_limit_bytes=LIMIT)
 
 
-def copy_rows(rows, source, target, sems):
-    count = target.shape[0]
-    copies = []
-    for user in range(count):
-        row = jnp.maximum(rows[user], 0)
-        copies.append(pltpu.make_async_copy(source.at[row], target.at[user], sems.at[user]))
-        copies[-1].start()
-    for copy in copies:
+def pass_on(copies, held, target, sems):
+    count = len(copies)
+    onward = []
+    for index, copy in enumerate(copies):
         copy.wait()
-
-
-def route_up(me, usage, storage_row_map, entries, up, holding):
-    users = usage.shape[0] // 8
+        onward.append(pltpu.make_async_copy(held.at[index], target.at[index], sems.at[count + index]))
+        onward[-1].start()
+    for copy in onward:
+        copy.wait()
+
+
+def route_up(usage, storage_row_map, entries, up, holding):
+    users = lax.axis_size("dp")
     tiles = entries.shape[0]
-
-    def kernel(me_ref, usage_ref, map_ref, entry_ref, up_ref, rows_ref, holders_ref, send_ref, sems):
-        mine = me_ref[0]
+    slots = usage.shape[0] // users
+
+    def kernel(usage_hbm, map_hbm, entry_hbm, up_ref, rows_ref, holders_ref, send_ref, usage_ref, map_ref, entry_ref, held, sems, table_sems):
+        tables = [
+            pltpu.make_async_copy(source, target, table_sems.at[index])
+            for index, (source, target) in enumerate(
+                ((usage_hbm, usage_ref), (map_hbm, map_ref), (entry_hbm, entry_ref))
+            )
+        ]
+        for copy in tables:
+            copy.start()
+        for copy in tables:
+            copy.wait()
+        mine = lax.axis_index("dp").astype(jnp.int32)
+        copies = []
         for user in range(users):
             row = jnp.int32(-1)
-            for slot in range(8):
-                place = map_ref[usage_ref[user * 8 + slot]]
+            for slot in range(slots):
+                place = map_ref[usage_ref[user * slots + slot]]
                 row = jnp.where(place // holding == mine, place % holding, row)
             rows_ref[user] = row
+            copies.append(
+                pltpu.make_async_copy(up_ref.at[jnp.maximum(row, 0)], held.at[user], sems.at[user])
+            )
+            copies[-1].start()
         for tile in range(tiles):
-            holders_ref[tile] = map_ref[usage_ref[mine * 8 + entry_ref[tile]]] // holding
-        copy_rows(rows_ref, up_ref, send_ref, sems)
+            holders_ref[tile] = map_ref[usage_ref[mine * slots + entry_ref[tile]]] // holding
+        pass_on(copies, held, send_ref, sems)
 
     return pl.pallas_call(
         kernel,
@@ -61,25 +81,44 @@
             jax.ShapeDtypeStruct((tiles,), jnp.int32),
             jax.ShapeDtypeStruct((users,) + up.shape[1:], BF16),
         ),
-        in_specs=[SMEM, SMEM, SMEM, SMEM, ANY],
-        out_specs=(SMEM, SMEM, ANY),
-        scratch_shapes=[pltpu.SemaphoreType.DMA((users,))],
-        compiler_params=params(),
-        cost_estimate=cost(0, 2 * up.size * 2),
+        in_specs=[HBM, HBM, HBM, HBM],
+        out_specs=(SMEM, SMEM, HBM),
+        scratch_shapes=[
+            pltpu.SMEM(usage.shape, jnp.int32),
+            pltpu.SMEM(storage_row_map.shape, jnp.int32),
+            pltpu.SMEM(entries.shape, jnp.int32),
+            pltpu.VMEM((users,) + up.shape[1:], BF16),
+            pltpu.SemaphoreType.DMA((2 * users,)),
+            pltpu.SemaphoreType.DMA((3,)),
+        ],
+        compiler_params=params(),
+        cost_estimate=cost(),
         name="route_up",
-    )(me, usage, storage_row_map, entries, up)
+    )(usage, storage_row_map, entries, up)
 
 
 def select_rows(rows, stored):
     users = rows.shape[0]
-    return pl.pallas_call(
-        copy_rows,
+
+    def kernel(rows_ref, stored_ref, send_ref, held, sems):
+        copies = []
+        for user in range(users):
+            row = jnp.maximum(rows_ref[user], 0)
+            copies.append(pltpu.make_async_copy(stored_ref.at[row], held.at[user], sems.at[user]))
+            copies[-1].start()
+        pass_on(copies, held, send_ref, sems)
+
+    return pl.pallas_call(
+        kernel,
         out_shape=jax.ShapeDtypeStruct((users,) + stored.shape[1:], BF16),
-        in_specs=[SMEM, ANY],
-        out_specs=ANY,
-        scratch_shapes=[pltpu.SemaphoreType.DMA((users,))],
-        compiler_params=params(),
-        cost_estimate=cost(0, 2 * stored.size * 2),
+        in_specs=[SMEM, HBM],
+        out_specs=HBM,
+        scratch_shapes=[
+            pltpu.VMEM((users,) + stored.shape[1:], BF16),
+            pltpu.SemaphoreType.DMA((2 * users,)),
+        ],
+        compiler_params=params(),
+        cost_estimate=cost(),
         name="select_down",
     )(rows, stored)
 
@@ -105,7 +144,7 @@
         ],
         out_specs=pl.BlockSpec((shards_number, block, width), lambda i: (0, i, 0)),
         compiler_params=params(),
-        cost_estimate=cost(2 * rows * features * columns, 2 * (rows * features + features * columns + rows * columns)),
+        cost_estimate=cost(),
         name="base_product",
     )(tokens, value_matrix)
 
@@ -125,7 +164,7 @@
         in_specs=[SMEM, VMEM, VMEM],
         out_specs=VMEM,
         compiler_params=params(),
-        cost_estimate=cost(2 * cotangent.size * up.shape[1], 2 * 3 * cotangent.size),
+        cost_estimate=cost(),
         name="back_product",
     )(holders, up, cotangent)
 
@@ -154,7 +193,7 @@
         ],
         out_specs=pl.BlockSpec((group, rank, TILE), lambda i: (i, 0, 0)),
         compiler_params=params(),
-        cost_estimate=cost(8 * tokens.size * rank, 2 * (tokens.size + down.size)),
+        cost_estimate=cost(),
         name="low_product",
     )(holders, down, tokens)
 
@@ -181,12 +220,12 @@
         out_specs=pl.BlockSpec((owners, rank, step), lambda i: (0, 0, i)),
         scratch_shapes=[pltpu.VMEM((owners, rank, step), F32)],
         compiler_params=params(),
-        cost_estimate=cost(8 * wide_side.size * rank, 2 * (wide_side.size + owners * rank * width)),
+        cost_estimate=cost(),
         name="gradient_terms",
     )(holders, rank_side, wide_side)
 
 
-def combine(rows, received, holding, step):
+def combine(rows, received, holding, step, nbytes):
     users, rank, width = received.shape
 
     def kernel(rows_ref, r_ref, o_ref, total):
@@ -207,7 +246,7 @@
         out_specs=pl.BlockSpec((holding, rank, step), lambda i: (0, 0, i)),
         scratch_shapes=[pltpu.VMEM((holding, rank, step), F32)],
         compiler_params=params(),
-        cost_estimate=cost(4 * received.size, 4 * received.size),
+        cost_estimate=cost(nbytes),
         name="combine",
     )(rows, received)
 
@@ -227,7 +266,7 @@
         in_specs=[SMEM, VMEM, VMEM, VMEM],
         out_specs=VMEM,
         compiler_params=params(),
-        cost_estimate=cost(2 * frozen.size * up.shape[1], 8 * frozen.size),
+        cost_estimate=cost(),
         name="finish_projected",
     )(holders, frozen, lowrank, up)
 
@@ -259,30 +298,35 @@
         ],
         out_specs=pl.BlockSpec((group * TILE, features), lambda i: (i, 0)),
         compiler_params=params(),
-        cost_estimate=cost(2 * rows * columns * features, 2 * (dy_full.size + value_matrix.size + rows * features)),
+        cost_estimate=cost(),
         name="input_product",
     )(holders, dy_full, value_matrix, back_low, down)
 
 
-def sum_over_tensor(part, half):
+def swap_cores(array):
+    size = lax.axis_size("tensor")
+    return lax.ppermute(array, "tensor", [(i, i ^ 1) for i in range(size)])
+
+
+def along_x(array, k):
     size = lax.axis_size("tensor")
     chips = size // 2
-    count = part.shape[0] // 2
-    swap = [(i, i ^ 1) for i in range(size)]
-
-    def along_x(array, k):
-        return lax.ppermute(array, "tensor", [(i, (i // 2 + k) % chips * 2 + i % 2) for i in range(size)])
-
-    both = (part.astype(F32) + lax.ppermute(part, "tensor", swap).astype(F32)).astype(BF16)
-    own = lax.dynamic_slice_in_dim(both, half * count, count, 0)
+    return lax.ppermute(array, "tensor", [(i, (i // 2 + k) % chips * 2 + i % 2) for i in range(size)])
+
+
+def sum_on_chip(part):
+    return (part.astype(F32) + swap_cores(part).astype(F32)).astype(BF16)
+
+
+def other_chips(own):
+    return [along_x(own, k) for k in (1, -1, 2)]
+
+
+def sum_of(own, others):
     total = own.astype(F32)
-    for k in range(1, chips):
-        total = total + along_x(own, k).astype(F32)
-    total = total.astype(BF16)
-    other = lax.ppermute(total, "tensor", swap)
-    first = jnp.where(half == 0, total, other)
-    second = jnp.where(half == 0, other, total)
-    return jnp.concatenate([first, second], axis=0)
+    for other in others:
+        total = total + other.astype(F32)
+    return total.astype(BF16)
 
 
 def shards(
@@ -297,32 +341,35 @@
 ):
     owners = lax.axis_size("dp")
     tensor_size = lax.axis_size("tensor")
-    half = lax.axis_index("tensor") % 2
-    me = lax.axis_index("dp").astype(jnp.int32).reshape(1)
     holding = down_factors.shape[0]
     down_stored = jnp.transpose(down_factors, (0, 2, 1))
 
     dy_full = lax.all_gather(cotangent, "tensor", axis=1, tiled=True)
-    rows, holders, send_up = route_up(me, usage, storage_row_map, tile_usage_entry, up_factors, holding)
+    rows, holders, send_up = route_up(usage, storage_row_map, tile_usage_entry, up_factors, holding)
     up = lax.all_to_all(send_up, "dp", split_axis=0, concat_axis=0, tiled=True)
     send_down = select_rows(rows, down_stored)
     down = lax.all_to_all(send_down, "dp", split_axis=0, concat_axis=0, tiled=True)
 
-    base_part = base_product(tokens, value_matrix, tensor_size)
+    base_part = base_product(after(tokens, rows), value_matrix, tensor_size)
     frozen = lax.psum_scatter(base_part, "tensor", scatter_dimension=0, tiled=False)
-
-    back_low = sum_over_tensor(back_product(holders, up, cotangent), half)
+    back_part = back_product(holders, after(up, send_down, base_part), cotangent)
+    back_chip = sum_on_chip(back_part)
+    back_low = sum_of(back_chip, other_chips(back_chip))
     send_down_terms = gradient_terms(holders, back_low, tokens, owners, 256)
     down_terms = lax.all_to_all(send_down_terms, "dp", split_axis=0, concat_axis=0, tiled=True)
 
-    lowrank = sum_over_tensor(low_product(holders, down, tokens), half)
+    low_chip = sum_on_chip(low_product(holders, after(down, send_down_terms), tokens))
+    low_others = other_chips(low_chip)
+    input_gradient = input_product(holders, after(dy_full, low_chip), value_matrix, back_low, down)
+    low_others[2] = after(low_others[2], input_gradient)
+    lowrank = sum_of(low_chip, low_others)
     send_up_terms = gradient_terms(holders, lowrank, cotangent, owners, cotangent.shape[1])
+    down_terms, send_up_terms = lax.optimization_barrier((down_terms, send_up_terms))
     up_terms = lax.all_to_all(send_up_terms, "dp", split_axis=0, concat_axis=0, tiled=True)
 
-    input_gradient = input_product(holders, dy_full, value_matrix, back_low, down)
     projected = finish_projected(holders, frozen, lowrank, up)
-    up_gradient = combine(rows, up_terms, holding, up_terms.shape[2])
-    down_gradient = jnp.transpose(combine(rows, down_terms, holding, 256), (0, 2, 1))
+    up_gradient = combine(rows, after(up_terms, projected), holding, up_terms.shape[2], 1024)
+    down_gradient = jnp.transpose(combine(rows, down_terms, holding, 256, 1 << 30), (0, 2, 1))
     return (projected, input_gradient, down_gradient, up_gradient)
 
 

time: 174 us -> 131 us (0.75)
  blocking collectives: 36.4 us -> 0 us
  waiting for transfers between devices: 49.6 us -> 28.6 us
  starting transfers between devices: 20.7 us -> 31.3 us
  Pallas kernels: 40.7 us -> 50.2 us
  local copies, waits for them, and re-layouts: 8.18 us -> 0.7 us
    all_to_all x1 -> x0, blocking collectives: 36.4 us -> none  [shards(): lax.all_to_all(send_down, 'dp', split_axis=0, concat_axis=0, tiled=True)]
    all_to_all x1, waiting for transfers between devices: 29.7 us -> 4.05 us  [shards(): lax.all_to_all(send_down_terms, 'dp', split_axis=0, concat_axis=0, tiled=...]
    unnamed x20 -> x4, local copies, waits for them, and re-layouts: 8.18 us -> 0.7 us
    all_to_all x1, starting transfers between devices: 3.53 us -> 8.16 us  [shards(): up = lax.all_to_all(send_up, 'dp', split_axis=0, concat_axis=0, tiled=True)]
    all_to_all x0 -> x1, starting transfers between devices: none -> 4.45 us  [shards(): lax.all_to_all(send_down, 'dp', split_axis=0, concat_axis=0, tiled=True)]
    ppermute x4 -> x2, waiting for transfers between devices: 0.01 us -> 3.49 us  [swap_cores(): return lax.ppermute(array, 'tensor', [(i, i ^ 1) for i in range(size)])]
    all_to_all x0 -> x1, waiting for transfers between devices: none -> 2.7 us  [shards(): lax.all_to_all(send_down, 'dp', split_axis=0, concat_axis=0, tiled=True)]
    ppermute x6, starting transfers between devices: 8.45 us -> 10.4 us  [along_x(): lax.ppermute(array, 'tensor', [(i, (i // 2 + k) % chips * 2 + i % 2) for...]
  transfers between devices with their start and end apart: 15 -> 14, of which waited for: 9 -> 9; matrix products, arithmetic and copies ran while one was open for 2% -> 3% of each run, Pallas kernels for 23% -> 37%
where the time goes in v1:
time: 131 us; the launch traced here: 129 us
  Pallas kernels  50.2 us (38%)
  starting transfers between devices  31.3 us (24%)
  waiting for transfers between devices  28.6 us (22%)
  between operations  14.1 us (11%)
  other arithmetic  3.8 us (3%)
    ppermute x6, waiting for transfers between devices, along_x(): lax.ppermute(array, 'tensor', [(i, (i // 2 + k) % chips * 2 + i % 2) for...  11.5 us
    ppermute x6, starting transfers between devices, along_x(): lax.ppermute(array, 'tensor', [(i, (i // 2 + k) % chips * 2 + i % 2) for...  10.4 us
    pallas_call x1, Pallas kernels, input_product(): pl.pallas_call(kernel, grid=(rows // (group * TILE),), out_shape=jax.Shap...  9.92 us
    pallas_call x1, Pallas kernels, base_product(): pl.pallas_call(kernel, grid=(rows // block,), out_shape=jax.ShapeDtypeStr...  8.41 us
    all_to_all x1, starting transfers between devices, shards(): up = lax.all_to_all(send_up, 'dp', split_axis=0, concat_axis=0, tiled=True)  8.16 us
    pallas_call x2, Pallas kernels, gradient_terms(): pl.pallas_call(kernel, grid=(width // step,), out_shape=jax.ShapeDtypeStr...  7.2 us
    pallas_call x2, Pallas kernels, combine(): pl.pallas_call(kernel, grid=(width // step,), out_shape=jax.ShapeDtypeStr...  6.26 us
    pallas_call x1, Pallas kernels, low_product(): pl.pallas_call(kernel, grid=(tiles // group,), out_shape=jax.ShapeDtypeSt...  5.54 us
  transfers between devices with their start and end apart: 14, of which 9 were waited for; matrix products, arithmetic and copies ran while one was open for 3% of the time, Pallas kernels for 37%

profile of v1, /device:TPU:0, one launch (start us, length us, event | category | flops | bytes accessed | tf_op | source)
XLA Modules:
  0.0 128.8 jit_solution(12838270703679472167)
XLA Ops:
  7.9 3.8 %route_up.1 = (s32[16]{0:T(128)}, s32[16]{0:T(128)}, bf16[16,64,128]{2,1,0:T(8,128)(2,1)}) custom-call(s32[128]{0:T(128)} %usage_hbm.1, s32[256]{0:T(256)} %map_hbm.1, s32[16]{0:T(128)} %entry_hbm.1, bf16[16,64,128]{2,1,0:T(8,128)(2,1)} %up_ref.1), custom_call_target="tpu_custom_call" | custom-call | flops 1024 | bytes 1024 | tf_op jit(solution)/shard_map/route_up/pallas_call | solution.py:77
  11.7 8.4 %base_product.1 = bf16[8,2048,128]{2,1,0:T(8,128)(2,1)} custom-call(bf16[2048,1024]{1,0:T(8,128)(2,1)} %x_ref.2, bf16[1024,1024]{1,0:T(8,128)(2,1)} %v_ref.3), custom_call_target="tpu_custom_call" | custom-call | flops 1024 | bytes 1024 | tf_op jit(solution)/shard_map/base_product/pallas_call | solution.py:137
  20.2 8.2 %all-to-all-start.1 = ((bf16[16,64,128]{2,1,0:T(8,128)(2,1)}), bf16[16,64,128]{2,1,0:T(8,128)(2,1)S(1)}, u32[]{:S(2)}, u32[]{:S(2)}) async-start(bf16[16,64,128]{2,1,0:T(8,128)(2,1)} %get-tuple-element.18), calls=%async_computation.2 | async-start | bytes 524288 | tf_op jit(solution)/shard_map/all_to_all | solution.py:349
  28.3 4.4 %select_down.1 = bf16[16,64,1024]{2,1,0:T(8,128)(2,1)} custom-call(s32[16]{0:T(128)} %get-tuple-element.16.rows_ref, bf16[16,64,1024]{2,1,0:T(8,128)(2,1)} %bitcast.3), custom_call_target="tpu_custom_call" | custom-call | flops 1024 | bytes 1024 | tf_op jit(solution)/shard_map/select_down/pallas_call | solution.py:111
  32.8 4.2 %all-to-all-done.1.up_ref = bf16[16,64,128]{2,1,0:T(8,128)(2,1)S(1)} async-done(((bf16[16,64,128]{2,1,0:T(8,128)(2,1)}), bf16[16,64,128]{2,1,0:T(8,128)(2,1)S(1)}, u32[]{:S(2)}, u32[]{:S(2)}) %all-to-all-start.1) | async-done | bytes 262176 | tf_op jit(solution)/shard_map/all_to_all | solution.py:349
  37.0 4.4 %all-to-all-start = ((bf16[16,64,1024]{2,1,0:T(8,128)(2,1)}), bf16[16,64,1024]{2,1,0:T(8,128)(2,1)}, u32[]{:S(2)}, u32[]{:S(2)}) async-start(bf16[16,64,1024]{2,1,0:T(8,128)(2,1)} %select_down.1), calls=%async_computation.1 | async-start | bytes 4194304 | tf_op jit(solution)/shard_map/all_to_all | solution.py:351
  41.5 2.3 %back_product.1 = bf16[16,64,128]{2,1,0:T(8,128)(2,1)} custom-call(s32[16]{0:T(128)} %get-tuple-element.15.h_ref, bf16[16,64,128]{2,1,0:T(8,128)(2,1)} %copy-done, bf16[2048,128]{1,0:T(8,128)(2,1)} %w_ref.3), custom_call_target="tpu_custom_call" | custom-call | flops 1024 | bytes 1024 | tf_op jit(solution)/shard_map/back_product/pallas_call | solution.py:161
  43.8 1.7 %collective-permute-done = bf16[16,64,128]{2,1,0:T(8,128)(2,1)S(1)} collective-permute-done((bf16[16,64,128]{2,1,0:T(8,128)(2,1)}, bf16[16,64,128]{2,1,0:T(8,128)(2,1)S(1)}, u32[]{:S(2)}, u32[]{:S(2)}) %collective-permute-start) | collective-permute-done | bytes 262176 | tf_op jit(solution)/shard_map/ppermute | solution.py:308
  46.6 3.1 %collective-permute-start.3 = (bf16[16,64,128]{2,1,0:T(8,128)(2,1)S(1)}, bf16[16,64,128]{2,1,0:T(8,128)(2,1)S(1)}, u32[]{:S(2)}, u32[]{:S(2)}) collective-permute-start(bf16[16,64,128]{2,1,0:T(8,128)(2,1)S(1)} %add_convert_fusion.3), channel_id=1, source_target_pairs={{0,4},{1,5},{2,6},{3,7},{4,0},{5,1},{6,2},{7,3},{8,12},{9,13},{10,... | collective-permute-start | bytes 786440 | tf_op jit(solution)/shard_map/ppermute | solution.py:314
  51.7 5.6 %collective-permute-done.3 = bf16[16,64,128]{2,1,0:T(8,128)(2,1)S(1)} collective-permute-done((bf16[16,64,128]{2,1,0:T(8,128)(2,1)S(1)}, bf16[16,64,128]{2,1,0:T(8,128)(2,1)S(1)}, u32[]{:S(2)}, u32[]{:S(2)}) %collective-permute-start.3) | collective-permute-done | bytes 262176 | tf_op jit(solution)/shard_map/ppermute | solution.py:314
  57.3 5.0 %collective-permute-done.2 = bf16[16,64,128]{2,1,0:T(8,128)(2,1)S(1)} collective-permute-done((bf16[16,64,128]{2,1,0:T(8,128)(2,1)S(1)}, bf16[16,64,128]{2,1,0:T(8,128)(2,1)S(1)}, u32[]{:S(2)}, u32[]{:S(2)}) %collective-permute-start.2) | collective-permute-done | bytes 262176 | tf_op jit(solution)/shard_map/ppermute | solution.py:314
  63.1 5.0 %gradient_terms.2 = bf16[16,64,1024]{2,1,0:T(8,128)(2,1)} custom-call(s32[16]{0:T(128)} %get-tuple-element.15.h_ref, bf16[16,64,128]{2,1,0:T(8,128)(2,1)} %add_convert_fusion.2.r_ref.b_ref, bf16[2048,1024]{1,0:T(8,128)(2,1)} %x_ref.2), custom_call_target="tpu_custom_call" | custom-call | flops 1024 | bytes 1024 | tf_op jit(solution)/shard_map/gradient_terms/pallas_call | solution.py:211
  68.2 2.7 %all-to-all-done.down_ref = bf16[16,64,1024]{2,1,0:T(8,128)(2,1)} async-done(((bf16[16,64,1024]{2,1,0:T(8,128)(2,1)}), bf16[16,64,1024]{2,1,0:T(8,128)(2,1)}, u32[]{:S(2)}, u32[]{:S(2)}) %all-to-all-start) | async-done | bytes 2097184 | tf_op jit(solution)/shard_map/all_to_all | solution.py:351
  70.9 4.7 %all-to-all-start.2 = ((bf16[16,64,1024]{2,1,0:T(8,128)(2,1)}), bf16[16,64,1024]{2,1,0:T(8,128)(2,1)}, u32[]{:S(2)}, u32[]{:S(2)}) async-start(bf16[16,64,1024]{2,1,0:T(8,128)(2,1)} %gradient_terms.2), calls=%async_computation.3 | async-start | bytes 4194304 | tf_op jit(solution)/shard_map/all_to_all | solution.py:359
  75.5 5.5 %low_product.1 = bf16[16,64,128]{2,1,0:T(8,128)(2,1)} custom-call(s32[16]{0:T(128)} %get-tuple-element.15.h_ref, bf16[16,64,1024]{2,1,0:T(8,128)(2,1)} %all-to-all-done.down_ref, bf16[2048,1024]{1,0:T(8,128)(2,1)} %x_ref.2), custom_call_target="tpu_custom_call" | custom-call | flops 1024 | bytes 1024 | tf_op jit(solution)/shard_map/low_product/pallas_call | solution.py:185
  83.9 3.3 %collective-permute-start.7 = (bf16[16,64,128]{2,1,0:T(8,128)(2,1)S(1)}, bf16[16,64,128]{2,1,0:T(8,128)(2,1)S(1)}, u32[]{:S(2)}, u32[]{:S(2)}) collective-permute-start(bf16[16,64,128]{2,1,0:T(8,128)(2,1)S(1)} %add_convert_fusion.1), channel_id=1, source_target_pairs={{0,4},{1,5},{2,6},{3,7},{4,0},{5,1},{6,2},{7,3},{8,12},{9,13},{10,... | collective-permute-start | bytes 786440 | tf_op jit(solution)/shard_map/ppermute | solution.py:314
  89.2 9.9 %input_product.1 = bf16[2048,1024]{1,0:T(8,128)(2,1)} custom-call(s32[16]{0:T(128)} %get-tuple-element.15.h_ref, bf16[2048,1024]{1,0:T(8,128)(2,1)} %all-gather.2.cloned.1.call-done.dy_ref, bf16[1024,1024]{1,0:T(8,128)(2,1)} %v_ref.3, bf16[16,64,128]{2,1,0:T(8,128)(2,1)} %add_convert_fusion.2.r_ref.b_ref, bf16[16,64,1024]{2,1,0:T(8,128)(2,1)} %all-to-all-done.down_ref), custom_call_target="tpu_custom_call" | custom-call | flops 1024 | bytes 1024 | tf_op jit(solution)/shard_map/input_product/pallas_call | solution.py:288
  100.9 2.2 %gradient_terms.3 = bf16[16,64,128]{2,1,0:T(8,128)(2,1)} custom-call(s32[16]{0:T(128)} %get-tuple-element.15.h_ref, bf16[16,64,128]{2,1,0:T(8,128)(2,1)} %add_convert_fusion.l_ref.r_ref, bf16[2048,128]{1,0:T(8,128)(2,1)} %w_ref.3), custom_call_target="tpu_custom_call" | custom-call | flops 1024 | bytes 1024 | tf_op jit(solution)/shard_map/gradient_terms/pallas_call | solution.py:211
  103.0 4.1 %all-to-all-done.2.r_ref = bf16[16,64,1024]{2,1,0:T(8,128)(2,1)} async-done(((bf16[16,64,1024]{2,1,0:T(8,128)(2,1)}), bf16[16,64,1024]{2,1,0:T(8,128)(2,1)}, u32[]{:S(2)}, u32[]{:S(2)}) %all-to-all-start.2) | async-done | bytes 2097184 | tf_op jit(solution)/shard_map/all_to_all | solution.py:359
  107.1 3.5 %all-to-all-start.3 = ((bf16[16,64,128]{2,1,0:T(8,128)(2,1)}), bf16[16,64,128]{2,1,0:T(8,128)(2,1)S(1)}, u32[]{:S(2)}, u32[]{:S(2)}) async-start(bf16[16,64,128]{2,1,0:T(8,128)(2,1)} %gradient_terms.3), calls=%async_computation.4 | async-start | bytes 524288 | tf_op jit(solution)/shard_map/all_to_all | solution.py:368
  110.7 4.4 %combine.2 = bf16[16,64,1024]{2,1,0:T(8,128)(2,1)} custom-call(s32[16]{0:T(128)} %get-tuple-element.16.rows_ref, bf16[16,64,1024]{2,1,0:T(8,128)(2,1)} %all-to-all-done.2.r_ref), custom_call_target="tpu_custom_call" | custom-call | flops 1024 | bytes 1073741824 | tf_op jit(solution)/shard_map/combine/pallas_call | solution.py:241
  115.0 2.3 %finish_projected.1 = bf16[2048,128]{1,0:T(8,128)(2,1)} custom-call(s32[16]{0:T(128)} %get-tuple-element.15.h_ref, bf16[2048,128]{1,0:T(8,128)(2,1)} %bitcast.5, bf16[16,64,128]{2,1,0:T(8,128)(2,1)} %add_convert_fusion.l_ref.r_ref, bf16[16,64,128]{2,1,0:T(8,128)(2,1)} %copy-done), custom_call_target="tpu_custom_call" | custom-call | flops 1024 | bytes 1024 | tf_op jit(solution)/shard_map/finish_projected/pallas_call | solution.py:263
  117.4 2.0 %all-to-all-done.3.r_ref = bf16[16,64,128]{2,1,0:T(8,128)(2,1)S(1)} async-done(((bf16[16,64,128]{2,1,0:T(8,128)(2,1)}), bf16[16,64,128]{2,1,0:T(8,128)(2,1)S(1)}, u32[]{:S(2)}, u32[]{:S(2)}) %all-to-all-start.3) | async-done | bytes 262176 | tf_op jit(solution)/shard_map/all_to_all | solution.py:368
  120.0 1.9 %combine.3 = bf16[16,64,128]{2,1,0:T(8,128)(2,1)} custom-call(s32[16]{0:T(128)} %get-tuple-element.16.rows_ref, bf16[16,64,128]{2,1,0:T(8,128)(2,1)} %copy-done.1), custom_call_target="tpu_custom_call" | custom-call | flops 1024 | bytes 1024 | tf_op jit(solution)/shard_map/combine/pallas_call | solution.py:241
  (25 shorter events, 12.0 us)
Async XLA Ops:
  7.2 82.0 %all-gather.2.cloned.1.call-start = ((), (), s32[]{:S(2)}) async-start(), calls=%async_computation.6 | async-start | bytes 4718592 | tf_op jit(solution)/shard_map/all_gather | solution.py:347
  7.9 107.1 %reduce-scatter.2.cloned.1.call-start = ((), (), s32[]{:S(2)}) async-start(), calls=%async_computation.5 | async-start | bytes 4718592 | tf_op jit(solution)/shard_map/reduce_scatter | solution.py:354
  20.2 16.9 %all-to-all-start.1 = ((bf16[16,64,128]{2,1,0:T(8,128)(2,1)}), bf16[16,64,128]{2,1,0:T(8,128)(2,1)S(1)}, u32[]{:S(2)}, u32[]{:S(2)}) async-start(bf16[16,64,128]{2,1,0:T(8,128)(2,1)} %get-tuple-element.18), calls=%async_computation.2 | async-start | bytes 524288 | tf_op jit(solution)/shard_map/all_to_all | solution.py:349
  37.0 4.5 %copy-start = (bf16[16,64,128]{2,1,0:T(8,128)(2,1)}, bf16[16,64,128]{2,1,0:T(8,128)(2,1)S(1)}, u32[]{:S(2)}) copy-start(bf16[16,64,128]{2,1,0:T(8,128)(2,1)S(1)} %all-to-all-done.1.up_ref) | copy-start | bytes 786436
  37.0 33.9 %all-to-all-start = ((bf16[16,64,1024]{2,1,0:T(8,128)(2,1)}), bf16[16,64,1024]{2,1,0:T(8,128)(2,1)}, u32[]{:S(2)}, u32[]{:S(2)}) async-start(bf16[16,64,1024]{2,1,0:T(8,128)(2,1)} %select_down.1), calls=%async_computation.1 | async-start | bytes 4194304 | tf_op jit(solution)/shard_map/all_to_all | solution.py:351
  43.8 1.7 %collective-permute-start = (bf16[16,64,128]{2,1,0:T(8,128)(2,1)}, bf16[16,64,128]{2,1,0:T(8,128)(2,1)S(1)}, u32[]{:S(2)}, u32[]{:S(2)}) collective-permute-start(bf16[16,64,128]{2,1,0:T(8,128)(2,1)} %back_product.1), channel_id=1, source_target_pairs={{0,1},{1,0},{2,3},{3,2},{4,5},{5,4},{6,7},{7,6},{8,9},{9,8},{10,11... | collective-permute-start | bytes 786440 | tf_op jit(solution)/shard_map/ppermute | solution.py:308
  46.6 10.7 %collective-permute-start.3 = (bf16[16,64,128]{2,1,0:T(8,128)(2,1)S(1)}, bf16[16,64,128]{2,1,0:T(8,128)(2,1)S(1)}, u32[]{:S(2)}, u32[]{:S(2)}) collective-permute-start(bf16[16,64,128]{2,1,0:T(8,128)(2,1)S(1)} %add_convert_fusion.3), channel_id=1, source_target_pairs={{0,4},{1,5},{2,6},{3,7},{4,0},{5,1},{6,2},{7,3},{8,12},{9,13},{10,... | collective-permute-start | bytes 786440 | tf_op jit(solution)/shard_map/ppermute | solution.py:314
  49.7 12.6 %collective-permute-start.2 = (bf16[16,64,128]{2,1,0:T(8,128)(2,1)S(1)}, bf16[16,64,128]{2,1,0:T(8,128)(2,1)S(1)}, u32[]{:S(2)}, u32[]{:S(2)}) collective-permute-start(bf16[16,64,128]{2,1,0:T(8,128)(2,1)S(1)} %add_convert_fusion.3), channel_id=1, source_target_pairs={{0,6},{1,7},{2,0},{3,1},{4,2},{5,3},{6,4},{7,5},{8,14},{9,15},{10,... | collective-permute-start | bytes 786440 | tf_op jit(solution)/shard_map/ppermute | solution.py:314
  50.8 11.4 %collective-permute-start.1 = (bf16[16,64,128]{2,1,0:T(8,128)(2,1)S(1)}, bf16[16,64,128]{2,1,0:T(8,128)(2,1)S(1)}, u32[]{:S(2)}, u32[]{:S(2)}) collective-permute-start(bf16[16,64,128]{2,1,0:T(8,128)(2,1)S(1)} %add_convert_fusion.3), channel_id=1, source_target_pairs={{0,2},{1,3},{2,4},{3,5},{4,6},{5,7},{6,0},{7,1},{8,10},{9,11},{10,... | collective-permute-start | bytes 786440 | tf_op jit(solution)/shard_map/ppermute | solution.py:314
  70.9 36.2 %all-to-all-start.2 = ((bf16[16,64,1024]{2,1,0:T(8,128)(2,1)}), bf16[16,64,1024]{2,1,0:T(8,128)(2,1)}, u32[]{:S(2)}, u32[]{:S(2)}) async-start(bf16[16,64,1024]{2,1,0:T(8,128)(2,1)} %gradient_terms.2), calls=%async_computation.3 | async-start | bytes 4194304 | tf_op jit(solution)/shard_map/all_to_all | solution.py:359
  81.1 1.7 %collective-permute-start.4 = (bf16[16,64,128]{2,1,0:T(8,128)(2,1)}, bf16[16,64,128]{2,1,0:T(8,128)(2,1)S(1)}, u32[]{:S(2)}, u32[]{:S(2)}) collective-permute-start(bf16[16,64,128]{2,1,0:T(8,128)(2,1)} %low_product.1), channel_id=1, source_target_pairs={{0,1},{1,0},{2,3},{3,2},{4,5},{5,4},{6,7},{7,6},{8,9},{9,8},{10,11... | collective-permute-start | bytes 786440 | tf_op jit(solution)/shard_map/ppermute | solution.py:308
  83.9 15.3 %collective-permute-start.7 = (bf16[16,64,128]{2,1,0:T(8,128)(2,1)S(1)}, bf16[16,64,128]{2,1,0:T(8,128)(2,1)S(1)}, u32[]{:S(2)}, u32[]{:S(2)}) collective-permute-start(bf16[16,64,128]{2,1,0:T(8,128)(2,1)S(1)} %add_convert_fusion.1), channel_id=1, source_target_pairs={{0,4},{1,5},{2,6},{3,7},{4,0},{5,1},{6,2},{7,3},{8,12},{9,13},{10,... | collective-permute-start | bytes 786440 | tf_op jit(solution)/shard_map/ppermute | solution.py:314
  87.2 12.8 %collective-permute-start.6 = (bf16[16,64,128]{2,1,0:T(8,128)(2,1)S(1)}, bf16[16,64,128]{2,1,0:T(8,128)(2,1)S(1)}, u32[]{:S(2)}, u32[]{:S(2)}) collective-permute-start(bf16[16,64,128]{2,1,0:T(8,128)(2,1)S(1)} %add_convert_fusion.1), channel_id=1, source_target_pairs={{0,6},{1,7},{2,0},{3,1},{4,2},{5,3},{6,4},{7,5},{8,14},{9,15},{10,... | collective-permute-start | bytes 786440 | tf_op jit(solution)/shard_map/ppermute | solution.py:314
  88.7 11.2 %collective-permute-start.5 = (bf16[16,64,128]{2,1,0:T(8,128)(2,1)S(1)}, bf16[16,64,128]{2,1,0:T(8,128)(2,1)S(1)}, u32[]{:S(2)}, u32[]{:S(2)}) collective-permute-start(bf16[16,64,128]{2,1,0:T(8,128)(2,1)S(1)} %add_convert_fusion.1), channel_id=1, source_target_pairs={{0,2},{1,3},{2,4},{3,5},{4,6},{5,7},{6,0},{7,1},{8,10},{9,11},{10,... | collective-permute-start | bytes 786440 | tf_op jit(solution)/shard_map/ppermute | solution.py:314
  107.1 12.2 %all-to-all-start.3 = ((bf16[16,64,128]{2,1,0:T(8,128)(2,1)}), bf16[16,64,128]{2,1,0:T(8,128)(2,1)S(1)}, u32[]{:S(2)}, u32[]{:S(2)}) async-start(bf16[16,64,128]{2,1,0:T(8,128)(2,1)} %gradient_terms.3), calls=%async_computation.4 | async-start | bytes 524288 | tf_op jit(solution)/shard_map/all_to_all | solution.py:368
  119.3 0.7 copy-start.1
Sparse Core Ops, SparseCore 0:
  9.7 38.4 all-gather.1
  50.6 45.3 reduce-scatter.1

commit v2 on v1

v2 whole, which is shorter than its diff:
```python
import jax
import jax.numpy as jnp
from jax import lax
from jax.experimental import pallas as pl
from jax.experimental.pallas import tpu as pltpu
from jax.sharding import PartitionSpec as P

TILE = 128
ADAPTER_SCALE = 2.0
F32 = jnp.float32
BF16 = jnp.bfloat16
HBM = pl.BlockSpec(memory_space=pltpu.HBM)
ANY = pl.BlockSpec(memory_space=pl.ANY)
SMEM = pl.BlockSpec(memory_space=pltpu.SMEM)
VMEM = pl.BlockSpec(memory_space=pltpu.VMEM)
SHIFTS = (0, 1, -1, 2)
LIMIT = 62 * 1024 * 1024
PART = 24 * 1024 * 1024


def dot(a, b, contract):
    return lax.dot_general(a, b, ((contract[:1], contract[1:]), ((), ())), preferred_element_type=F32)


def cost(flops=1024):
    return pl.CostEstimate(flops=flops, bytes_accessed=1024, transcendentals=0)


def after(value, *others):
    return lax.optimization_barrier((value,) + others)[0]


def params(limit=LIMIT):
    return pltpu.CompilerParams(vmem_limit_bytes=limit)


def pass_on(copies, held, target, sems):
    count = len(copies)
    onward = []
    for index, copy in enumerate(copies):
        copy.wait()
        onward.append(pltpu.make_async_copy(held.at[index], target.at[index], sems.at[count + index]))
        onward[-1].start()
    for copy in onward:
        copy.wait()


def route_up(usage, storage_row_map, entries, up, holding):
    users = lax.axis_size("dp")
    tiles = entries.shape[0]
    slots = usage.shape[0] // users

    def kernel(usage_hbm, map_hbm, entry_hbm, up_ref, rows_ref, holders_ref, send_ref, usage_ref, map_ref, entry_ref, held, sems, table_sems):
        tables = [
            pltpu.make_async_copy(source, target, table_sems.at[index])
            for index, (source, target) in enumerate(
                ((usage_hbm, usage_ref), (map_hbm, map_ref), (entry_hbm, entry_ref))
            )
        ]
        for copy in tables:
            copy.start()
        for copy in tables:
            copy.wait()
        mine = lax.axis_index("dp").astype(jnp.int32)
        copies = []
        for user in range(users):
            row = jnp.int32(-1)
            for slot in range(slots):
                place = map_ref[usage_ref[user * slots + slot]]
                row = jnp.where(place // holding == mine, place % holding, row)
            rows_ref[user] = row
            copies.append(
                pltpu.make_async_copy(up_ref.at[jnp.maximum(row, 0)], held.at[user], sems.at[user])
            )
            copies[-1].start()
        for tile in range(tiles):
            holders_ref[tile] = map_ref[usage_ref[mine * slots + entry_ref[tile]]] // holding
        pass_on(copies, held, send_ref, sems)

    return pl.pallas_call(
        kernel,
        out_shape=(
            jax.ShapeDtypeStruct((users,), jnp.int32),
            jax.ShapeDtypeStruct((tiles,), jnp.int32),
            jax.ShapeDtypeStruct((users,) + up.shape[1:], BF16),
        ),
        in_specs=[HBM, HBM, HBM, HBM],
        out_specs=(SMEM, SMEM, HBM),
        scratch_shapes=[
            pltpu.SMEM(usage.shape, jnp.int32),
            pltpu.SMEM(storage_row_map.shape, jnp.int32),
            pltpu.SMEM(entries.shape, jnp.int32),
            pltpu.VMEM((users,) + up.shape[1:], BF16),
            pltpu.SemaphoreType.DMA((2 * users,)),
            pltpu.SemaphoreType.DMA((3,)),
        ],
        compiler_params=params(),
        cost_estimate=cost(),
        name="route_up",
    )(usage, storage_row_map, entries, up)


def select_rows(rows, stored):
    users = rows.shape[0]

    def kernel(rows_ref, stored_ref, send_ref, held, sems):
        copies = []
        for user in range(users):
            row = jnp.maximum(rows_ref[user], 0)
            copies.append(pltpu.make_async_copy(stored_ref.at[row], held.at[user], sems.at[user]))
            copies[-1].start()
        pass_on(copies, held, send_ref, sems)

    return pl.pallas_call(
        kernel,
        out_shape=jax.ShapeDtypeStruct((users,) + stored.shape[1:], BF16),
        in_specs=[SMEM, HBM],
        out_specs=HBM,
        scratch_shapes=[
            pltpu.VMEM((users,) + stored.shape[1:], BF16),
            pltpu.SemaphoreType.DMA((2 * users,)),
        ],
        compiler_params=params(),
        cost_estimate=cost(),
        name="select_down",
    )(rows, stored)


def relative_columns(flip):
    size = lax.axis_size("tensor")
    me = lax.axis_index("tensor").astype(jnp.int32)
    chips = size // 2
    core = me % 2 if flip == 0 else 1 - me % 2
    return [(me // 2 + chips + shift) % chips * 2 + core for shift in SHIFTS]


def start_all(copies):
    for copy in copies:
        copy.start()
    return copies


def wait_all(copies):
    for copy in copies:
        copy.wait()


def base_product(tokens, value_matrix):
    rows, features = tokens.shape
    columns = value_matrix.shape[1]
    width = columns // lax.axis_size("tensor")
    chips = len(SHIFTS)
    steps = 4
    block = rows // steps

    def kernel(x_hbm, v_hbm, own_hbm, other_hbm, x_ref, v_ref, y_ref, in_sems, out_sems):
        core = lax.axis_index("tensor").astype(jnp.int32) % 2
        spans = [pl.ds(step * block, block) for step in range(steps)]
        fetch = start_all(
            [pltpu.make_async_copy(v_hbm, v_ref, in_sems.at[steps])]
            + [
                pltpu.make_async_copy(x_hbm.at[span], x_ref.at[span], in_sems.at[step])
                for step, span in enumerate(spans)
            ]
        )
        fetch[0].wait()
        stores = []
        for step, span in enumerate(spans):
            fetch[1 + step].wait()
            product = dot(x_ref[span, :], v_ref[...], (1, 0)).astype(BF16)
            for index in range(2 * chips):
                y_ref[index % 2, index // 2, span, :] = product[:, index * width : (index + 1) * width]
            stores += start_all(
                [
                    pltpu.make_async_copy(y_ref.at[core, :, span], own_hbm.at[:, span], out_sems.at[0, step]),
                    pltpu.make_async_copy(y_ref.at[1 - core, :, span], other_hbm.at[:, span], out_sems.at[1, step]),
                ]
            )
        wait_all(stores)

    shape = jax.ShapeDtypeStruct((chips, rows, width), BF16)
    return pl.pallas_call(
        kernel,
        out_shape=(shape, shape),
        in_specs=[HBM, HBM],
        out_specs=(HBM, HBM),
        scratch_shapes=[
            pltpu.VMEM(tokens.shape, BF16),
            pltpu.VMEM(value_matrix.shape, BF16),
            pltpu.VMEM((2, chips, rows, width), BF16),
            pltpu.SemaphoreType.DMA((steps + 1,)),
            pltpu.SemaphoreType.DMA((2, steps)),
        ],
        compiler_params=params(PART),
        cost_estimate=cost(),
        name="base_product",
    )(tokens, value_matrix)


def add_cores(own, other):
    chips, rows, width = own.shape

    def kernel(own_hbm, other_hbm, *refs):
        sums = refs[:chips]
        own_ref, other_ref, sum_ref, in_sems, out_sems = refs[chips:]
        mine = lax.axis_index("tensor").astype(jnp.int32) // 2
        fetch = []
        for index, shift in enumerate(SHIFTS):
            chip = (mine + chips + shift) % chips
            fetch += start_all(
                [
                    pltpu.make_async_copy(own_hbm.at[chip], own_ref.at[index], in_sems.at[0, index]),
                    pltpu.make_async_copy(other_hbm.at[chip], other_ref.at[index], in_sems.at[1, index]),
                ]
            )
        stores = []
        for index in range(chips):
            wait_all(fetch[2 * index : 2 * index + 2])
            sum_ref[index] = (own_ref[index].astype(F32) + other_ref[index].astype(F32)).astype(BF16)
            stores += start_all([pltpu.make_async_copy(sum_ref.at[index], sums[index], out_sems.at[index])])
        wait_all(stores)

    return pl.pallas_call(
        kernel,
        out_shape=[jax.ShapeDtypeStruct((rows, width), BF16)] * chips,
        in_specs=[ANY, ANY],
        out_specs=[ANY] * chips,
        scratch_shapes=[pltpu.VMEM(own.shape, BF16)] * 3
        + [pltpu.SemaphoreType.DMA((2, chips)), pltpu.SemaphoreType.DMA((chips,))],
        compiler_params=params(PART),
        cost_estimate=cost(),
        name="add_cores",
    )(own, other)


def back_product(holders, up, cotangent):
    tiles = holders.shape[0]

    def kernel(h_ref, up_ref, dy_ref, o_ref):
        for tile in range(tiles):
            o_ref[tile] = dot(
                up_ref[h_ref[tile]], dy_ref[tile * TILE : (tile + 1) * TILE, :], (1, 1)
            ).astype(BF16)

    return pl.pallas_call(
        kernel,
        out_shape=jax.ShapeDtypeStruct((tiles, up.shape[1], TILE), BF16),
        in_specs=[SMEM, VMEM, VMEM],
        out_specs=VMEM,
        compiler_params=params(PART),
        cost_estimate=cost(),
        name="back_product",
    )(holders, up, cotangent)


def low_product(holders, down, tokens):
    tiles = holders.shape[0]
    rows, features = tokens.shape
    rank = down.shape[1]
    steps = 4
    block = rows // steps

    def kernel(h_ref, down_hbm, x_hbm, o_ref, down_ref, x_ref, sems):
        fetch = start_all(
            [pltpu.make_async_copy(down_hbm, down_ref, sems.at[steps])]
            + [
                pltpu.make_async_copy(x_hbm.at[span], x_ref.at[span], sems.at[step])
                for step, span in enumerate([pl.ds(step * block, block) for step in range(steps)])
            ]
        )
        fetch[0].wait()
        for tile in range(tiles):
            if tile * TILE % block == 0:
                fetch[1 + tile * TILE // block].wait()
            o_ref[tile] = dot(
                down_ref[h_ref[tile]], x_ref[tile * TILE : (tile + 1) * TILE, :], (1, 1)
            ).astype(BF16)

    return pl.pallas_call(
        kernel,
        out_shape=jax.ShapeDtypeStruct((tiles, rank, TILE), BF16),
        in_specs=[SMEM, ANY, ANY],
        out_specs=VMEM,
        scratch_shapes=[
            pltpu.VMEM(down.shape, BF16),
            pltpu.VMEM(tokens.shape, BF16),
            pltpu.SemaphoreType.DMA((steps + 1,)),
        ],
        compiler_params=params(PART),
        cost_estimate=cost(1 << 40),
        name="low_product",
    )(holders, down, tokens)


def narrow_terms(holders, rank_side, wide_side, owners):
    tiles, rank, _ = rank_side.shape
    width = wide_side.shape[1]

    def kernel(h_ref, r_ref, w_ref, o_ref, total):
        total[...] = jnp.zeros_like(total)
        for tile in range(tiles):
            total[h_ref[tile]] += dot(r_ref[tile], w_ref[tile * TILE : (tile + 1) * TILE, :], (1, 0))
        o_ref[...] = (ADAPTER_SCALE * total[...]).astype(BF16)

    return pl.pallas_call(
        kernel,
        out_shape=jax.ShapeDtypeStruct((owners, rank, width), BF16),
        in_specs=[SMEM, VMEM, VMEM],
        out_specs=VMEM,
        scratch_shapes=[pltpu.VMEM((owners, rank, width), F32)],
        compiler_params=params(PART),
        cost_estimate=cost(),
        name="narrow_terms",
    )(holders, rank_side, wide_side)


def narrow_combine(rows, received, holding):
    users, rank, width = received.shape

    def kernel(rows_ref, r_ref, o_ref, total):
        total[...] = jnp.zeros_like(total)
        for user in range(users):

            @pl.when(rows_ref[user] >= 0)
            def _():
                total[jnp.maximum(rows_ref[user], 0)] += r_ref[user].astype(F32)

        o_ref[...] = total[...].astype(BF16)

    return pl.pallas_call(
        kernel,
        out_shape=jax.ShapeDtypeStruct((holding, rank, width), BF16),
        in_specs=[SMEM, VMEM],
        out_specs=VMEM,
        scratch_shapes=[pltpu.VMEM((holding, rank, width), F32)],
        compiler_params=params(PART),
        cost_estimate=cost(),
        name="narrow_combine",
    )(rows, received)


def gradient_terms(holders, rank_side, wide_side, owners):
    tiles, rank, _ = rank_side.shape
    rows, width = wide_side.shape
    steps = 4
    block = rows // steps

    def kernel(h_ref, r_hbm, w_hbm, o_hbm, r_ref, w_ref, total, o_ref, in_sems, out_sems):
        fetch = start_all(
            [pltpu.make_async_copy(r_hbm, r_ref, in_sems.at[steps])]
            + [
                pltpu.make_async_copy(w_hbm.at[span], w_ref.at[span], in_sems.at[step])
                for step, span in enumerate([pl.ds(step * block, block) for step in range(steps)])
            ]
        )
        total[...] = jnp.zeros_like(total)
        fetch[0].wait()
        for tile in range(tiles):
            if tile * TILE % block == 0:
                fetch[1 + tile * TILE // block].wait()
            total[h_ref[tile]] += dot(r_ref[tile], w_ref[tile * TILE : (tile + 1) * TILE, :], (1, 0))
        stores = []
        part = owners // 4
        for index in range(4):
            span = pl.ds(index * part, part)
            o_ref[span] = (ADAPTER_SCALE * total[span]).astype(BF16)
            stores += start_all([pltpu.make_async_copy(o_ref.at[span], o_hbm.at[span], out_sems.at[index])])
        wait_all(stores)

    return pl.pallas_call(
        kernel,
        out_shape=jax.ShapeDtypeStruct((owners, rank, width), BF16),
        in_specs=[SMEM, ANY, ANY],
        out_specs=HBM,
        scratch_shapes=[
            pltpu.VMEM(rank_side.shape, BF16),
            pltpu.VMEM(wide_side.shape, BF16),
            pltpu.VMEM((owners, rank, width), F32),
            pltpu.VMEM((owners, rank, width), BF16),
            pltpu.SemaphoreType.DMA((steps + 1,)),
            pltpu.SemaphoreType.DMA((4,)),
        ],
        compiler_params=params(PART),
        cost_estimate=cost(),
        name="gradient_terms",
    )(holders, rank_side, wide_side)


def combine(rows, received, holding):
    users, rank, width = received.shape
    steps = 4
    part = rank // steps

    def kernel(rows_ref, r_hbm, o_hbm, r_ref, total, o_ref, in_sems, out_sems):
        spans = [pl.ds(step * part, part) for step in range(steps)]
        fetch = start_all(
            [
                pltpu.make_async_copy(r_hbm.at[:, span], r_ref.at[:, span], in_sems.at[step])
                for step, span in enumerate(spans)
            ]
        )
        stores = []
        for step, span in enumerate(spans):
            total[...] = jnp.zeros_like(total)
            fetch[step].wait()
            for user in range(users):

                @pl.when(rows_ref[user] >= 0)
                def _():
                    total[jnp.maximum(rows_ref[user], 0)] += r_ref[user, span].astype(F32)

            o_ref[:, span] = total[...].astype(BF16)
            stores += start_all([pltpu.make_async_copy(o_ref.at[:, span], o_hbm.at[:, span], out_sems.at[step])])
        wait_all(stores)

    return pl.pallas_call(
        kernel,
        out_shape=jax.ShapeDtypeStruct((holding, rank, width), BF16),
        in_specs=[SMEM, ANY],
        out_specs=HBM,
        scratch_shapes=[
            pltpu.VMEM(received.shape, BF16),
            pltpu.VMEM((holding, part, width), F32),
            pltpu.VMEM((holding, rank, width), BF16),
            pltpu.SemaphoreType.DMA((steps,)),
            pltpu.SemaphoreType.DMA((steps,)),
        ],
        compiler_params=params(PART),
        cost_estimate=cost(),
        name="combine",
    )(rows, received)


def finish_projected(holders, terms, lowrank, up):
    tiles = holders.shape[0]
    rows, width = terms[0].shape
    count = len(terms)
    middle = rows // 2

    def kernel(h_ref, *refs):
        l_hbm, up_hbm, o_hbm, t_ref, l_ref, up_ref, o_ref, term_sems, in_sems, out_sems = refs[count:]
        spans = [pl.ds(half * middle, middle) for half in range(2)]
        fetch = start_all(
            [
                pltpu.make_async_copy(source, target, in_sems.at[index])
                for index, (source, target) in enumerate(((l_hbm, l_ref), (up_hbm, up_ref)))
            ]
        )
        halves = [
            start_all(
                [
                    pltpu.make_async_copy(
                        refs[index].at[span], t_ref.at[index, span], term_sems.at[half, index]
                    )
                    for index in range(count)
                ]
            )
            for half, span in enumerate(spans)
        ]
        wait_all(fetch)
        stores = []
        for half, span in enumerate(spans):
            wait_all(halves[half])
            for tile in range(half * tiles // 2, (half + 1) * tiles // 2):
                rows_of = pl.ds(tile * TILE, TILE)
                total = ADAPTER_SCALE * dot(l_ref[tile], up_ref[h_ref[tile]], (0, 0))
                for index in range(count):
                    total = total + t_ref[index, rows_of, :].astype(F32)
                o_ref[rows_of, :] = total.astype(BF16)
            stores += start_all([pltpu.make_async_copy(o_ref.at[span], o_hbm.at[span], out_sems.at[half])])
        wait_all(stores)

    return pl.pallas_call(
        kernel,
        out_shape=jax.ShapeDtypeStruct((rows, width), BF16),
        in_specs=[SMEM] + [ANY] * (count + 2),
        out_specs=HBM,
        scratch_shapes=[
            pltpu.VMEM((count, rows, width), BF16),
            pltpu.VMEM(lowrank.shape, BF16),
            pltpu.VMEM(up.shape, BF16),
            pltpu.VMEM((rows, width), BF16),
            pltpu.SemaphoreType.DMA((2, count)),
            pltpu.SemaphoreType.DMA((2,)),
            pltpu.SemaphoreType.DMA((2,)),
        ],
        compiler_params=params(PART),
        cost_estimate=cost(),
        name="finish_projected",
    )(holders, *terms, lowrank, up)


def input_product(holders, pieces, value_matrix, back_low, down):
    rows, width = pieces[0].shape
    features, columns = value_matrix.shape
    steps = 4
    block = rows // steps
    group = block // TILE
    middle = rows // 2
    count = len(pieces)

    def kernel(h_ref, *refs):
        hbm = refs[:count]
        v_hbm, b_hbm, down_hbm, o_hbm = refs[count : count + 4]
        dy_ref, v_ref, b_ref, down_ref, o_ref, dy_sems, in_sems, out_sems = refs[count + 4 :]
        halves = []
        for half in range(2):
            span = pl.ds(half * middle, middle)
            copies = []
            for flip in range(2):
                own, after_own, before_own, opposite = relative_columns(flip)
                own_hbm, left_hbm, right_hbm, first_hbm, last_hbm = hbm[flip * count // 2 : (flip + 1) * count // 2]
                sources = (
                    (own, own_hbm.at[span]),
                    (before_own, left_hbm.at[span]),
                    (after_own, right_hbm.at[span]),
                    (opposite, (first_hbm, last_hbm)[half]),
                )
                for index, (place, source) in enumerate(sources):
                    target = dy_ref.at[span, pl.ds(pl.multiple_of(place * width, width), width)]
                    copies.append(pltpu.make_async_copy(source, target, dy_sems.at[half, flip, index]))
            halves.append(copies)
        fetch = [
            pltpu.make_async_copy(source, target, in_sems.at[index])
            for index, (source, target) in enumerate(((v_hbm, v_ref), (b_hbm, b_ref), (down_hbm, down_ref)))
        ]
        first = start_all(fetch[:1] + halves[0])
        stores = []
        for step in range(steps):
            if step == 0:
                wait_all(first)
                start_all(fetch[1:])
            elif step * block == middle:
                wait_all(halves[1])
            span = pl.ds(step * block, block)
            frozen = dot(dy_ref[span, :], v_ref[...], (1, 1))
            if step == 0:
                wait_all(fetch[1:])
                start_all(halves[1])
            for tile in range(group):
                adapter = dot(b_ref[step * group + tile], down_ref[h_ref[step * group + tile]], (0, 0))
                o_ref[pl.ds(step * block + tile * TILE, TILE), :] = (
                    frozen[tile * TILE : (tile + 1) * TILE, :] + ADAPTER_SCALE * adapter
                ).astype(BF16)
            stores += start_all([pltpu.make_async_copy(o_ref.at[span], o_hbm.at[span], out_sems.at[step])])
        wait_all(stores)

    return pl.pallas_call(
        kernel,
        out_shape=jax.ShapeDtypeStruct((rows, features), BF16),
        in_specs=[SMEM] + [ANY] * (count + 3),
        out_specs=HBM,
        scratch_shapes=[
            pltpu.VMEM((rows, columns), BF16),
            pltpu.VMEM(value_matrix.shape, BF16),
            pltpu.VMEM(back_low.shape, BF16),
            pltpu.VMEM(down.shape, BF16),
            pltpu.VMEM((rows, features), BF16),
            pltpu.SemaphoreType.DMA((2, 2, 4)),
            pltpu.SemaphoreType.DMA((3,)),
            pltpu.SemaphoreType.DMA((steps,)),
        ],
        compiler_params=params(PART),
        cost_estimate=cost(),
        name="input_product",
    )(holders, *pieces, value_matrix, back_low, down)


def swap_cores(array):
    size = lax.axis_size("tensor")
    return lax.ppermute(array, "tensor", [(i, i ^ 1) for i in range(size)])


def along_x(array, k):
    size = lax.axis_size("tensor")
    chips = size // 2
    return lax.ppermute(array, "tensor", [(i, (i // 2 + k) % chips * 2 + i % 2) for i in range(size)])


def sum_on_chip(part):
    return (part.astype(F32) + swap_cores(part).astype(F32)).astype(BF16)


def other_chips(own):
    return [along_x(own, shift) for shift in SHIFTS[1:]]


def sum_of(own, others):
    total = own.astype(F32)
    for other in others:
        total = total + other.astype(F32)
    return total.astype(BF16)


def shards(
    tokens,
    cotangent,
    value_matrix,
    down_factors,
    up_factors,
    tile_usage_entry,
    usage,
    storage_row_map,
):
    owners = lax.axis_size("dp")
    holding = down_factors.shape[0]
    down_stored = jnp.transpose(down_factors, (0, 2, 1))

    middle = cotangent.shape[0] // 2
    rows, holders, send_up = route_up(usage, storage_row_map, tile_usage_entry, up_factors, holding)
    up = lax.all_to_all(send_up, "dp", split_axis=0, concat_axis=0, tiled=True)
    left, right = along_x(cotangent, 1), along_x(cotangent, -1)
    send_down = after(select_rows(rows, down_stored), left, right)
    down = lax.all_to_all(send_down, "dp", split_axis=0, concat_axis=0, tiled=True)

    first, last = along_x(left[:middle], 1), along_x(right[middle:], -1)
    own_swapped = swap_cores(cotangent)
    back_part = back_product(holders, after(up, send_down, own_swapped), cotangent)
    left_swapped, right_swapped = swap_cores(left), swap_cores(right)
    back_chip = after(sum_on_chip(back_part), left_swapped, right_swapped)
    back_others = other_chips(back_chip)
    own_base, other_base = base_product(after(tokens, back_chip), value_matrix)
    first_swapped, last_swapped = swap_cores(first), swap_cores(last)
    back_others[2] = after(back_others[2], own_base, first, last)
    back_low = sum_of(back_chip, back_others)
    pieces = [cotangent, left, right, first, last]
    pieces += [own_swapped, left_swapped, right_swapped, first_swapped, last_swapped]
    sums = add_cores(own_base, swap_cores(other_base))
    frozen = [sums[0]] + [along_x(part, shift) for part, shift in zip(sums[1:], SHIFTS[1:])]
    send_down_terms = gradient_terms(holders, back_low, tokens, owners)
    down_terms = lax.all_to_all(send_down_terms, "dp", split_axis=0, concat_axis=0, tiled=True)

    low_chip = sum_on_chip(low_product(holders, after(down, send_down_terms), tokens))
    low_others = other_chips(low_chip)
    pieces[0] = after(pieces[0], low_chip)
    input_gradient = input_product(holders, pieces, value_matrix, back_low, down)
    low_others[2] = after(low_others[2], input_gradient)
    lowrank = sum_of(low_chip, low_others)
    send_up_terms = narrow_terms(holders, lowrank, cotangent, owners)
    down_terms, send_up_terms = lax.optimization_barrier((down_terms, send_up_terms))
    up_terms = lax.all_to_all(send_up_terms, "dp", split_axis=0, concat_axis=0, tiled=True)

    projected = finish_projected(holders, frozen, lowrank, up)
    up_gradient = narrow_combine(rows, after(up_terms, projected), holding)
    down_gradient = jnp.transpose(combine(rows, down_terms, holding), (0, 2, 1))
    return (projected, input_gradient, down_gradient, up_gradient)


def solution(mesh):
    return jax.shard_map(
        shards,
        mesh=mesh,
        in_specs=(
            P("dp", "tensor"),
            P("dp", "tensor"),
            P("tensor", None),
            P("dp", "tensor", None),
            P("dp", None, "tensor"),
            P("dp"),
            P(),
            P(),
        ),
        out_specs=(
            P("dp", "tensor"),
            P("dp", "tensor"),
            P("dp", "tensor", None),
            P("dp", None, "tensor"),
        ),
        check_vma=False,
    )
```

time: 131 us -> 118 us (0.901)
  waiting for transfers between devices: 28.6 us -> 14.5 us
  between operations: 14.1 us -> 1.05 us
  starting transfers between devices: 31.3 us -> 43.8 us
  local copies, waits for them, and re-layouts: 0.7 us -> 12.8 us
  Pallas kernels: 50.2 us -> 43.3 us
  other arithmetic: 3.8 us -> 0.49 us
    unnamed x4 -> x50, local copies, waits for them, and re-layouts: 0.7 us -> 11.8 us
    ppermute x6 -> x13, starting transfers between devices: 10.4 us -> 18.2 us  [along_x(): lax.ppermute(array, 'tensor', [(i, (i // 2 + k) % chips * 2 + i % 2) for...]
    ppermute x6 -> x13, waiting for transfers between devices: 11.5 us -> 5.18 us  [along_x(): lax.ppermute(array, 'tensor', [(i, (i // 2 + k) % chips * 2 + i % 2) for...]
    pallas_call x8 -> x9, Pallas kernels: 39.7 us -> 34.6 us  [the longest x1 9.84 us: input_product(): pl.pallas_call(kernel, out_shape=jax.ShapeDtypeStruct((rows, features), B...]
    all_to_all x1, waiting for transfers between devices: 2.7 us -> 0.01 us  [shards(): lax.all_to_all(send_down, 'dp', split_axis=0, concat_axis=0, tiled=True)]
    all_to_all x1, starting transfers between devices: 4.66 us -> 7.22 us  [shards(): lax.all_to_all(send_down_terms, 'dp', split_axis=0, concat_axis=0, tiled=...]
    all_to_all x1, waiting for transfers between devices: 1.99 us -> 0.01 us  [shards(): lax.all_to_all(send_up_terms, 'dp', split_axis=0, concat_axis=0, tiled=True)]
    convert_element_type x2, other arithmetic: 2.05 us -> 0.15 us  [sum_on_chip(): return (part.astype(F32) + swap_cores(part).astype(F32)).astype(BF16)]
  transfers between devices with their start and end apart: 14 -> 25, of which waited for: 9 -> 6; matrix products, arithmetic and copies ran while one was open for 3% -> 1% of each run, Pallas kernels for 37% -> 36%
where the time goes in v2:
time: 118 us; the launch traced here: 116 us
  starting transfers between devices  43.8 us (37%)
  Pallas kernels  43.3 us (37%)
  waiting for transfers between devices  14.5 us (12%)
  local copies, waits for them, and re-layouts  12.8 us (11%)
    ppermute x13, starting transfers between devices, along_x(): lax.ppermute(array, 'tensor', [(i, (i // 2 + k) % chips * 2 + i % 2) for...  18.2 us
    unnamed x50, local copies, waits for them, and re-layouts  11.8 us
    pallas_call x1, Pallas kernels, input_product(): pl.pallas_call(kernel, out_shape=jax.ShapeDtypeStruct((rows, features), B...  9.84 us
    all_to_all x1, starting transfers between devices, shards(): up = lax.all_to_all(send_up, 'dp', split_axis=0, concat_axis=0, tiled=True)  8.17 us
    all_to_all x1, starting transfers between devices, shards(): lax.all_to_all(send_down_terms, 'dp', split_axis=0, concat_axis=0, tiled=...  7.22 us
    pallas_call x1, Pallas kernels, base_product(): pl.pallas_call(kernel, out_shape=(shape, shape), in_specs=[HBM, HBM], out...  6.49 us
    ppermute x13, waiting for transfers between devices, along_x(): lax.ppermute(array, 'tensor', [(i, (i // 2 + k) % chips * 2 + i % 2) for...  5.18 us
    all_to_all x1, waiting for transfers between devices, shards(): up = lax.all_to_all(send_up, 'dp', split_axis=0, concat_axis=0, tiled=True)  4.7 us
  transfers between devices with their start and end apart: 25, of which 6 were waited for; matrix products, arithmetic and copies ran while one was open for 1% of the time, Pallas kernels for 36%

profile of v2, /device:TPU:0, one launch (start us, length us, event | category | flops | bytes accessed | tf_op | source)
XLA Modules:
  0.0 115.9 jit_solution(18060999103061667643)
XLA Ops:
  0.6 1.6 %collective-permute-start = (bf16[2048,128]{1,0:T(8,128)(2,1)}, bf16[2048,128]{1,0:T(8,128)(2,1)S(1)}, u32[]{:S(2)}, u32[]{:S(2)}) collective-permute-start(bf16[2048,128]{1,0:T(8,128)(2,1)} %w_ref.1), channel_id=1, source_target_pairs={{0,2},{1,3},{2,4},{3,5},{4,6},{5,7},{6,0},{7,1},{8,10},{9,11},{10,... | collective-permute-start | bytes 1572872 | tf_op jit(solution)/shard_map/ppermute | solution.py:577
  2.3 1.7 %collective-permute-start.1 = (bf16[2048,128]{1,0:T(8,128)(2,1)}, bf16[2048,128]{1,0:T(8,128)(2,1)}, u32[]{:S(2)}, u32[]{:S(2)}) collective-permute-start(bf16[2048,128]{1,0:T(8,128)(2,1)} %w_ref.1), channel_id=1, source_target_pairs={{0,6},{1,7},{2,0},{3,1},{4,2},{5,3},{6,4},{7,5},{8,14},{9,15},{10,... | collective-permute-start | bytes 1572872 | tf_op jit(solution)/shard_map/ppermute | solution.py:577
  3.9 3.7 %route_up.1 = (s32[16]{0:T(128)}, s32[16]{0:T(128)}, bf16[16,64,128]{2,1,0:T(8,128)(2,1)}) custom-call(s32[128]{0:T(128)} %usage_hbm.1, s32[256]{0:T(256)} %map_hbm.1, s32[16]{0:T(128)} %entry_hbm.1, bf16[16,64,128]{2,1,0:T(8,128)(2,1)} %up_ref.1), custom_call_target="tpu_custom_call" | custom-call | flops 1024 | bytes 1024 | tf_op jit(solution)/shard_map/route_up/pallas_call | solution.py:80
  7.7 8.2 %all-to-all-start = ((bf16[16,64,128]{2,1,0:T(8,128)(2,1)}), bf16[16,64,128]{2,1,0:T(8,128)(2,1)S(1)}, u32[]{:S(2)}, u32[]{:S(2)}) async-start(bf16[16,64,128]{2,1,0:T(8,128)(2,1)} %get-tuple-element.25), calls=%async_computation | async-start | bytes 524288 | tf_op jit(solution)/shard_map/all_to_all | solution.py:611
  15.8 3.9 %select_down.1 = bf16[16,64,1024]{2,1,0:T(8,128)(2,1)} custom-call(s32[16]{0:T(128)} %get-tuple-element.26.rows_ref, bf16[16,64,1024]{2,1,0:T(8,128)(2,1)} %bitcast.2), custom_call_target="tpu_custom_call" | custom-call | flops 1024 | bytes 1024 | tf_op jit(solution)/shard_map/select_down/pallas_call | solution.py:114
  19.8 4.7 %all-to-all-done.up_ref.refs_5_ = bf16[16,64,128]{2,1,0:T(8,128)(2,1)S(1)} async-done(((bf16[16,64,128]{2,1,0:T(8,128)(2,1)}), bf16[16,64,128]{2,1,0:T(8,128)(2,1)S(1)}, u32[]{:S(2)}, u32[]{:S(2)}) %all-to-all-start) | async-done | bytes 262176 | tf_op jit(solution)/shard_map/all_to_all | solution.py:611
  24.5 3.7 %all-to-all-start.1 = ((bf16[16,64,1024]{2,1,0:T(8,128)(2,1)}), bf16[16,64,1024]{2,1,0:T(8,128)(2,1)S(1)}, u32[]{:S(2)}, u32[]{:S(2)}) async-start(bf16[16,64,1024]{2,1,0:T(8,128)(2,1)} %select_down.1), calls=%async_computation.1 | async-start | bytes 4194304 | tf_op jit(solution)/shard_map/all_to_all | solution.py:614
  33.6 3.0 %collective-permute-start.14 = (bf16[1024,128]{1,0:T(8,128)(2,1)S(1)}, bf16[1024,128]{1,0:T(8,128)(2,1)S(1)}, u32[]{:S(2)}, u32[]{:S(2)}) collective-permute-start(bf16[1024,128]{1,0:T(8,128)(2,1)S(1)} %slice.9), channel_id=1, source_target_pairs={{0,6},{1,7},{2,0},{3,1},{4,2},{5,3},{6,4},{7,5},{8,14},{9,15},{10,... | collective-permute-start | bytes 786440 | tf_op jit(solution)/shard_map/ppermute | solution.py:577
  41.0 2.2 %copy-done = bf16[2048,1024]{1,0:T(8,128)(2,1)S(1)} copy-done((bf16[2048,1024]{1,0:T(8,128)(2,1)S(1)}, bf16[2048,1024]{1,0:T(8,128)(2,1)}, u32[]{:S(2)}) %copy-start) | copy-done | bytes 4194328
  43.2 6.5 %base_product.1 = (bf16[4,2048,128]{2,1,0:T(8,128)(2,1)S(1)}, bf16[4,2048,128]{2,1,0:T(8,128)(2,1)}) custom-call(bf16[2048,1024]{1,0:T(8,128)(2,1)S(1)} %copy-done, bf16[1024,1024]{1,0:T(8,128)(2,1)S(1)} %copy-done.3), custom_call_target="tpu_custom_call" | custom-call | flops 1024 | bytes 1024 | tf_op jit(solution)/shard_map/base_product/pallas_call | solution.py:182
  51.1 2.6 %collective-permute-done.11 = bf16[16,64,128]{2,1,0:T(8,128)(2,1)S(1)} collective-permute-done((bf16[16,64,128]{2,1,0:T(8,128)(2,1)S(1)}, bf16[16,64,128]{2,1,0:T(8,128)(2,1)S(1)}, u32[]{:S(2)}, u32[]{:S(2)}) %collective-permute-start.11) | collective-permute-done | bytes 262176 | tf_op jit(solution)/shard_map/ppermute | solution.py:577
  54.0 2.8 %gradient_terms.1 = bf16[16,64,1024]{2,1,0:T(8,128)(2,1)S(1)} custom-call(s32[16]{0:T(128)S(1)} %copy-done.23, bf16[16,64,128]{2,1,0:T(8,128)(2,1)S(1)} %add_convert_fusion.2.r_hbm.refs_11_, bf16[2048,1024]{1,0:T(8,128)(2,1)S(1)} %copy-done.1), custom_call_target="tpu_custom_call" | custom-call | flops 1024 | bytes 1024 | tf_op jit(solution)/shard_map/gradient_terms/pallas_call | solution.py:370
  58.9 7.2 %all-to-all-start.2 = ((bf16[16,64,1024]{2,1,0:T(8,128)(2,1)}), bf16[16,64,1024]{2,1,0:T(8,128)(2,1)}, u32[]{:S(2)}, u32[]{:S(2)}) async-start(bf16[16,64,1024]{2,1,0:T(8,128)(2,1)} %copy-done.5), calls=%async_computation.2 | async-start | bytes 4194304 | tf_op jit(solution)/shard_map/all_to_all | solution.py:631
  66.1 2.2 %copy-done.2 = bf16[2048,1024]{1,0:T(8,128)(2,1)S(1)} copy-done((bf16[2048,1024]{1,0:T(8,128)(2,1)S(1)}, bf16[2048,1024]{1,0:T(8,128)(2,1)}, u32[]{:S(2)}) %copy-start.2) | copy-done | bytes 4194328
  68.3 2.9 %low_product.1 = bf16[16,64,128]{2,1,0:T(8,128)(2,1)S(1)} custom-call(s32[16]{0:T(128)S(1)} %copy-done.23, bf16[16,64,1024]{2,1,0:T(8,128)(2,1)S(1)} %all-to-all-done.1.down_hbm.refs_12_, bf16[2048,1024]{1,0:T(8,128)(2,1)S(1)} %copy-done.2), custom_call_target="tpu_custom_call" | custom-call | flops 1099511627776 | bytes 1024 | tf_op jit(solution)/shard_map/low_product/pallas_call | solution.py:279
  73.0 2.4 %collective-permute-start.18 = (bf16[16,64,128]{2,1,0:T(8,128)(2,1)S(1)}, bf16[16,64,128]{2,1,0:T(8,128)(2,1)S(1)}, u32[]{:S(2)}, u32[]{:S(2)}) collective-permute-start(bf16[16,64,128]{2,1,0:T(8,128)(2,1)S(1)} %add_convert_fusion.1), channel_id=1, source_target_pairs={{0,4},{1,5},{2,6},{3,7},{4,0},{5,1},{6,2},{7,3},{8,12},{9,13},{10,... | collective-permute-start | bytes 786440 | tf_op jit(solution)/shard_map/ppermute | solution.py:577
  79.2 2.7 %add_cores.1 = (bf16[2048,128]{1,0:T(8,128)(2,1)S(1)}, bf16[2048,128]{1,0:T(8,128)(2,1)}, bf16[2048,128]{1,0:T(8,128)(2,1)}, bf16[2048,128]{1,0:T(8,128)(2,1)}) custom-call(bf16[4,2048,128]{2,1,0:T(8,128)(2,1)S(1)} %copy-done.10, bf16[4,2048,128]{2,1,0:T(8,128)(2,1)} %collective-permute-done.6.other_hbm), custom_call_target="tpu_custom_call" | custom-call | flops 1024 | bytes 1024 | tf_op jit(solution)/shard_map/add_cores/pallas_call | solution.py:223
  81.9 2.1 %collective-permute-start.7 = (bf16[2048,128]{1,0:T(8,128)(2,1)}, bf16[2048,128]{1,0:T(8,128)(2,1)}, u32[]{:S(2)}, u32[]{:S(2)}) collective-permute-start(bf16[2048,128]{1,0:T(8,128)(2,1)} %get-tuple-element.34), channel_id=1, source_target_pairs={{0,2},{1,3},{2,4},{3,5},{4,6},{5,7},{6,0},{7,1},{8,10},{9,11},{10,... | collective-permute-start | bytes 1572872 | tf_op jit(solution)/shard_map/ppermute | solution.py:577
  86.2 9.8 %input_product.1 = bf16[2048,1024]{1,0:T(8,128)(2,1)} custom-call(s32[16]{0:T(128)S(1)} %copy-done.23, bf16[2048,128]{1,0:T(8,128)(2,1)S(1)} %copy-done.6, bf16[2048,128]{1,0:T(8,128)(2,1)S(1)} %collective-permute-done.refs_1_, bf16[2048,128]{1,0:T(8,128)(2,1)} %collective-permute-done.1.refs_2_, bf16[1024,128]{1,0:T(8,128)(2,1)S(1)} %copy-done.20, ...), custom_call_target="tpu_custom_call" | custom-call | flops 1024 | bytes 1024 | tf_op jit(solution)/shard_map/input_product/pallas_call | solution.py:548
  97.8 2.5 %all-to-all-done.2.r_hbm = bf16[16,64,1024]{2,1,0:T(8,128)(2,1)} async-done(((bf16[16,64,1024]{2,1,0:T(8,128)(2,1)}), bf16[16,64,1024]{2,1,0:T(8,128)(2,1)}, u32[]{:S(2)}, u32[]{:S(2)}) %all-to-all-start.2) | async-done | bytes 2097184 | tf_op jit(solution)/shard_map/all_to_all | solution.py:631
  100.3 4.7 %all-to-all-start.3 = ((bf16[16,64,128]{2,1,0:T(8,128)(2,1)}), bf16[16,64,128]{2,1,0:T(8,128)(2,1)S(1)}, u32[]{:S(2)}, u32[]{:S(2)}) async-start(bf16[16,64,128]{2,1,0:T(8,128)(2,1)} %narrow_terms.1), calls=%async_computation.3 | async-start | bytes 524288 | tf_op jit(solution)/shard_map/all_to_all | solution.py:641
  105.0 3.6 %combine.1 = bf16[16,64,1024]{2,1,0:T(8,128)(2,1)} custom-call(s32[16]{0:T(128)S(1)} %copy-done.24, bf16[16,64,1024]{2,1,0:T(8,128)(2,1)} %all-to-all-done.2.r_hbm), custom_call_target="tpu_custom_call" | custom-call | flops 1024 | bytes 1024 | tf_op jit(solution)/shard_map/combine/pallas_call | solution.py:416
  108.7 2.5 %collective-permute-done.9.refs_3_ = bf16[2048,128]{1,0:T(8,128)(2,1)} collective-permute-done((bf16[2048,128]{1,0:T(8,128)(2,1)}, bf16[2048,128]{1,0:T(8,128)(2,1)}, u32[]{:S(2)}, u32[]{:S(2)}) %collective-permute-start.9) | collective-permute-done | bytes 524320 | tf_op jit(solution)/shard_map/ppermute | solution.py:577
  111.2 3.2 %finish_projected.1 = bf16[2048,128]{1,0:T(8,128)(2,1)} custom-call(s32[16]{0:T(128)S(1)} %copy-done.23, bf16[2048,128]{1,0:T(8,128)(2,1)S(1)} %copy-done.18, bf16[2048,128]{1,0:T(8,128)(2,1)} %collective-permute-done.7.refs_1_, bf16[2048,128]{1,0:T(8,128)(2,1)} %collective-permute-done.8.refs_2_, bf16[2048,128]{1,0:T(8,128)(2,1)} %collective-permute-done.9.refs_3_, ...), custom_call_target="tpu_custom_call" | custom-call | flops 1024 | bytes 1024 | tf_op jit(solution)/shard_map/finish_projected/pallas_call | solution.py:473
  (94 shorter events, 24.3 us)
Async XLA Ops:
  0.6 19.2 %collective-permute-start = (bf16[2048,128]{1,0:T(8,128)(2,1)}, bf16[2048,128]{1,0:T(8,128)(2,1)S(1)}, u32[]{:S(2)}, u32[]{:S(2)}) collective-permute-start(bf16[2048,128]{1,0:T(8,128)(2,1)} %w_ref.1), channel_id=1, source_target_pairs={{0,2},{1,3},{2,4},{3,5},{4,6},{5,7},{6,0},{7,1},{8,10},{9,11},{10,... | collective-permute-start | bytes 1572872 | tf_op jit(solution)/shard_map/ppermute | solution.py:577
  2.3 17.5 %collective-permute-start.1 = (bf16[2048,128]{1,0:T(8,128)(2,1)}, bf16[2048,128]{1,0:T(8,128)(2,1)}, u32[]{:S(2)}, u32[]{:S(2)}) collective-permute-start(bf16[2048,128]{1,0:T(8,128)(2,1)} %w_ref.1), channel_id=1, source_target_pairs={{0,6},{1,7},{2,0},{3,1},{4,2},{5,3},{6,4},{7,5},{8,14},{9,15},{10,... | collective-permute-start | bytes 1572872 | tf_op jit(solution)/shard_map/ppermute | solution.py:577
  7.7 16.9 %all-to-all-start = ((bf16[16,64,128]{2,1,0:T(8,128)(2,1)}), bf16[16,64,128]{2,1,0:T(8,128)(2,1)S(1)}, u32[]{:S(2)}, u32[]{:S(2)}) async-start(bf16[16,64,128]{2,1,0:T(8,128)(2,1)} %get-tuple-element.25), calls=%async_computation | async-start | bytes 524288 | tf_op jit(solution)/shard_map/all_to_all | solution.py:611
  24.5 34.4 %all-to-all-start.1 = ((bf16[16,64,1024]{2,1,0:T(8,128)(2,1)}), bf16[16,64,1024]{2,1,0:T(8,128)(2,1)S(1)}, u32[]{:S(2)}, u32[]{:S(2)}) async-start(bf16[16,64,1024]{2,1,0:T(8,128)(2,1)} %select_down.1), calls=%async_computation.1 | async-start | bytes 4194304 | tf_op jit(solution)/shard_map/all_to_all | solution.py:614
  28.3 2.0 %collective-permute-start.2 = (bf16[2048,128]{1,0:T(8,128)(2,1)S(1)}, bf16[2048,128]{1,0:T(8,128)(2,1)S(1)}, u32[]{:S(2)}, u32[]{:S(2)}) collective-permute-start(bf16[2048,128]{1,0:T(8,128)(2,1)S(1)} %copy-done.6), channel_id=1, source_target_pairs={{0,1},{1,0},{2,3},{3,2},{4,5},{5,4},{6,7},{7,6},{8,9},{9,8},{10,11... | collective-permute-start | bytes 1572872 | tf_op jit(solution)/shard_map/ppermute | solution.py:571
  28.4 8.4 %collective-permute-start.4 = (bf16[2048,128]{1,0:T(8,128)(2,1)S(1)}, bf16[2048,128]{1,0:T(8,128)(2,1)S(1)}, u32[]{:S(2)}, u32[]{:S(2)}) collective-permute-start(bf16[2048,128]{1,0:T(8,128)(2,1)S(1)} %collective-permute-done.refs_1_), channel_id=1, source_target_pairs={{0,1},{1,0},{2,3},{3,2},{4,5},{5,4},{6,7},{7,6},{8,9},{9,8},{10,11... | collective-permute-start | bytes 1572872 | tf_op jit(solution)/shard_map/ppermute | solution.py:571
  28.9 8.7 %collective-permute-start.5 = (bf16[2048,128]{1,0:T(8,128)(2,1)}, bf16[2048,128]{1,0:T(8,128)(2,1)S(1)}, u32[]{:S(2)}, u32[]{:S(2)}) collective-permute-start(bf16[2048,128]{1,0:T(8,128)(2,1)} %collective-permute-done.1.refs_2_), channel_id=1, source_target_pairs={{0,1},{1,0},{2,3},{3,2},{4,5},{5,4},{6,7},{7,6},{8,9},{9,8},{10,11... | collective-permute-start | bytes 1572872 | tf_op jit(solution)/shard_map/ppermute | solution.py:571
  32.1 4.6 %collective-permute-start.3 = (bf16[16,64,128]{2,1,0:T(8,128)(2,1)S(1)}, bf16[16,64,128]{2,1,0:T(8,128)(2,1)S(1)}, u32[]{:S(2)}, u32[]{:S(2)}) collective-permute-start(bf16[16,64,128]{2,1,0:T(8,128)(2,1)S(1)} %back_product.1), channel_id=1, source_target_pairs={{0,1},{1,0},{2,3},{3,2},{4,5},{5,4},{6,7},{7,6},{8,9},{9,8},{10,11... | collective-permute-start | bytes 786440 | tf_op jit(solution)/shard_map/ppermute | solution.py:571
  32.3 18.7 %collective-permute-start.13 = (bf16[1024,128]{1,0:T(8,128)(2,1)S(1)}, bf16[1024,128]{1,0:T(8,128)(2,1)S(1)}, u32[]{:S(2)}, u32[]{:S(2)}) collective-permute-start(bf16[1024,128]{1,0:T(8,128)(2,1)S(1)} %slice.8), channel_id=1, source_target_pairs={{0,2},{1,3},{2,4},{3,5},{4,6},{5,7},{6,0},{7,1},{8,10},{9,11},{10,... | collective-permute-start | bytes 786440 | tf_op jit(solution)/shard_map/ppermute | solution.py:577
  33.6 17.4 %collective-permute-start.14 = (bf16[1024,128]{1,0:T(8,128)(2,1)S(1)}, bf16[1024,128]{1,0:T(8,128)(2,1)S(1)}, u32[]{:S(2)}, u32[]{:S(2)}) collective-permute-start(bf16[1024,128]{1,0:T(8,128)(2,1)S(1)} %slice.9), channel_id=1, source_target_pairs={{0,6},{1,7},{2,0},{3,1},{4,2},{5,3},{6,4},{7,5},{8,14},{9,15},{10,... | collective-permute-start | bytes 786440 | tf_op jit(solution)/shard_map/ppermute | solution.py:577
  38.4 12.7 %collective-permute-start.12 = (bf16[16,64,128]{2,1,0:T(8,128)(2,1)S(1)}, bf16[16,64,128]{2,1,0:T(8,128)(2,1)S(1)}, u32[]{:S(2)}, u32[]{:S(2)}) collective-permute-start(bf16[16,64,128]{2,1,0:T(8,128)(2,1)S(1)} %add_convert_fusion.3), channel_id=1, source_target_pairs={{0,4},{1,5},{2,6},{3,7},{4,0},{5,1},{6,2},{7,3},{8,12},{9,13},{10,... | collective-permute-start | bytes 786440 | tf_op jit(solution)/shard_map/ppermute | solution.py:577
  39.0 14.7 %collective-permute-start.11 = (bf16[16,64,128]{2,1,0:T(8,128)(2,1)S(1)}, bf16[16,64,128]{2,1,0:T(8,128)(2,1)S(1)}, u32[]{:S(2)}, u32[]{:S(2)}) collective-permute-start(bf16[16,64,128]{2,1,0:T(8,128)(2,1)S(1)} %add_convert_fusion.3), channel_id=1, source_target_pairs={{0,6},{1,7},{2,0},{3,1},{4,2},{5,3},{6,4},{7,5},{8,14},{9,15},{10,... | collective-permute-start | bytes 786440 | tf_op jit(solution)/shard_map/ppermute | solution.py:577
  40.1 13.6 %collective-permute-start.10 = (bf16[16,64,128]{2,1,0:T(8,128)(2,1)S(1)}, bf16[16,64,128]{2,1,0:T(8,128)(2,1)S(1)}, u32[]{:S(2)}, u32[]{:S(2)}) collective-permute-start(bf16[16,64,128]{2,1,0:T(8,128)(2,1)S(1)} %add_convert_fusion.3), channel_id=1, source_target_pairs={{0,2},{1,3},{2,4},{3,5},{4,6},{5,7},{6,0},{7,1},{8,10},{9,11},{10,... | collective-permute-start | bytes 786440 | tf_op jit(solution)/shard_map/ppermute | solution.py:577
  53.9 23.0 %collective-permute-start.6 = (bf16[4,2048,128]{2,1,0:T(8,128)(2,1)}, bf16[4,2048,128]{2,1,0:T(8,128)(2,1)}, u32[]{:S(2)}, u32[]{:S(2)}) collective-permute-start(bf16[4,2048,128]{2,1,0:T(8,128)(2,1)} %get-tuple-element.32), channel_id=1, source_target_pairs={{0,1},{1,0},{2,3},{3,2},{4,5},{5,4},{6,7},{7,6},{8,9},{9,8},{10,11... | collective-permute-start | bytes 6291464 | tf_op jit(solution)/shard_map/ppermute | solution.py:571
  58.9 41.4 %all-to-all-start.2 = ((bf16[16,64,1024]{2,1,0:T(8,128)(2,1)}), bf16[16,64,1024]{2,1,0:T(8,128)(2,1)}, u32[]{:S(2)}, u32[]{:S(2)}) async-start(bf16[16,64,1024]{2,1,0:T(8,128)(2,1)} %copy-done.5), calls=%async_computation.2 | async-start | bytes 4194304 | tf_op jit(solution)/shard_map/all_to_all | solution.py:631
  71.5 10.4 %collective-permute-start.19 = (bf16[1024,128]{1,0:T(8,128)(2,1)S(1)}, bf16[1024,128]{1,0:T(8,128)(2,1)S(1)}, u32[]{:S(2)}, u32[]{:S(2)}) collective-permute-start(bf16[1024,128]{1,0:T(8,128)(2,1)S(1)} %copy-done.20), channel_id=1, source_target_pairs={{0,1},{1,0},{2,3},{3,2},{4,5},{5,4},{6,7},{7,6},{8,9},{9,8},{10,11... | collective-permute-start | bytes 786440 | tf_op jit(solution)/shard_map/ppermute | solution.py:571
  71.9 12.2 %collective-permute-start.20 = (bf16[1024,128]{1,0:T(8,128)(2,1)S(1)}, bf16[1024,128]{1,0:T(8,128)(2,1)S(1)}, u32[]{:S(2)}, u32[]{:S(2)}) collective-permute-start(bf16[1024,128]{1,0:T(8,128)(2,1)S(1)} %copy-done.22), channel_id=1, source_target_pairs={{0,1},{1,0},{2,3},{3,2},{4,5},{5,4},{6,7},{7,6},{8,9},{9,8},{10,11... | collective-permute-start | bytes 786440 | tf_op jit(solution)/shard_map/ppermute | solution.py:571
  73.0 12.3 %collective-permute-start.18 = (bf16[16,64,128]{2,1,0:T(8,128)(2,1)S(1)}, bf16[16,64,128]{2,1,0:T(8,128)(2,1)S(1)}, u32[]{:S(2)}, u32[]{:S(2)}) collective-permute-start(bf16[16,64,128]{2,1,0:T(8,128)(2,1)S(1)} %add_convert_fusion.1), channel_id=1, source_target_pairs={{0,4},{1,5},{2,6},{3,7},{4,0},{5,1},{6,2},{7,3},{8,12},{9,13},{10,... | collective-permute-start | bytes 786440 | tf_op jit(solution)/shard_map/ppermute | solution.py:577
  75.4 20.7 %collective-permute-start.17 = (bf16[16,64,128]{2,1,0:T(8,128)(2,1)S(1)}, bf16[16,64,128]{2,1,0:T(8,128)(2,1)S(1)}, u32[]{:S(2)}, u32[]{:S(2)}) collective-permute-start(bf16[16,64,128]{2,1,0:T(8,128)(2,1)S(1)} %add_convert_fusion.1), channel_id=1, source_target_pairs={{0,6},{1,7},{2,0},{3,1},{4,2},{5,3},{6,4},{7,5},{8,14},{9,15},{10,... | collective-permute-start | bytes 786440 | tf_op jit(solution)/shard_map/ppermute | solution.py:577
  76.8 19.2 %collective-permute-start.16 = (bf16[16,64,128]{2,1,0:T(8,128)(2,1)S(1)}, bf16[16,64,128]{2,1,0:T(8,128)(2,1)S(1)}, u32[]{:S(2)}, u32[]{:S(2)}) collective-permute-start(bf16[16,64,128]{2,1,0:T(8,128)(2,1)S(1)} %add_convert_fusion.1), channel_id=1, source_target_pairs={{0,2},{1,3},{2,4},{3,5},{4,6},{5,7},{6,0},{7,1},{8,10},{9,11},{10,... | collective-permute-start | bytes 786440 | tf_op jit(solution)/shard_map/ppermute | solution.py:577
  81.9 26.7 %collective-permute-start.7 = (bf16[2048,128]{1,0:T(8,128)(2,1)}, bf16[2048,128]{1,0:T(8,128)(2,1)}, u32[]{:S(2)}, u32[]{:S(2)}) collective-permute-start(bf16[2048,128]{1,0:T(8,128)(2,1)} %get-tuple-element.34), channel_id=1, source_target_pairs={{0,2},{1,3},{2,4},{3,5},{4,6},{5,7},{6,0},{7,1},{8,10},{9,11},{10,... | collective-permute-start | bytes 1572872 | tf_op jit(solution)/shard_map/ppermute | solution.py:577
  84.0 24.6 %collective-permute-start.8 = (bf16[2048,128]{1,0:T(8,128)(2,1)}, bf16[2048,128]{1,0:T(8,128)(2,1)}, u32[]{:S(2)}, u32[]{:S(2)}) collective-permute-start(bf16[2048,128]{1,0:T(8,128)(2,1)} %get-tuple-element.35), channel_id=1, source_target_pairs={{0,6},{1,7},{2,0},{3,1},{4,2},{5,3},{6,4},{7,5},{8,14},{9,15},{10,... | collective-permute-start | bytes 1572872 | tf_op jit(solution)/shard_map/ppermute | solution.py:577
  85.2 25.9 %collective-permute-start.9 = (bf16[2048,128]{1,0:T(8,128)(2,1)}, bf16[2048,128]{1,0:T(8,128)(2,1)}, u32[]{:S(2)}, u32[]{:S(2)}) collective-permute-start(bf16[2048,128]{1,0:T(8,128)(2,1)} %get-tuple-element.36), channel_id=1, source_target_pairs={{0,4},{1,5},{2,6},{3,7},{4,0},{5,1},{6,2},{7,3},{8,12},{9,13},{10,... | collective-permute-start | bytes 1572872 | tf_op jit(solution)/shard_map/ppermute | solution.py:577
  100.3 14.1 %all-to-all-start.3 = ((bf16[16,64,128]{2,1,0:T(8,128)(2,1)}), bf16[16,64,128]{2,1,0:T(8,128)(2,1)S(1)}, u32[]{:S(2)}, u32[]{:S(2)}) async-start(bf16[16,64,128]{2,1,0:T(8,128)(2,1)} %narrow_terms.1), calls=%async_computation.3 | async-start | bytes 524288 | tf_op jit(solution)/shard_map/all_to_all | solution.py:641
  (26 other events, 152.3 us)

commit v3 on v2

--- a/solution.py
+++ b/solution.py
@@ -24,6 +24,10 @@
 
 def cost(flops=1024):
     return pl.CostEstimate(flops=flops, bytes_accessed=1024, transcendentals=0)
+
+
+def in_hbm(value):
+    return pltpu.with_memory_space_constraint(value, pltpu.HBM)
 
 
 def after(value, *others):
@@ -153,20 +157,11 @@
     steps = 4
     block = rows // steps
 
-    def kernel(x_hbm, v_hbm, own_hbm, other_hbm, x_ref, v_ref, y_ref, in_sems, out_sems):
+    def kernel(x_ref, v_ref, own_hbm, other_hbm, y_ref, out_sems):
         core = lax.axis_index("tensor").astype(jnp.int32) % 2
         spans = [pl.ds(step * block, block) for step in range(steps)]
-        fetch = start_all(
-            [pltpu.make_async_copy(v_hbm, v_ref, in_sems.at[steps])]
-            + [
-                pltpu.make_async_copy(x_hbm.at[span], x_ref.at[span], in_sems.at[step])
-                for step, span in enumerate(spans)
-            ]
-        )
-        fetch[0].wait()
         stores = []
         for step, span in enumerate(spans):
-            fetch[1 + step].wait()
             product = dot(x_ref[span, :], v_ref[...], (1, 0)).astype(BF16)
             for index in range(2 * chips):
                 y_ref[index % 2, index // 2, span, :] = product[:, index * width : (index + 1) * width]
@@ -178,17 +173,14 @@
             )
         wait_all(stores)
 
-    shape = jax.ShapeDtypeStruct((chips, rows, width), BF16)
+    shape = pltpu.HBM((chips, rows, width), BF16)
     return pl.pallas_call(
         kernel,
         out_shape=(shape, shape),
-        in_specs=[HBM, HBM],
+        in_specs=[VMEM, VMEM],
         out_specs=(HBM, HBM),
         scratch_shapes=[
-            pltpu.VMEM(tokens.shape, BF16),
-            pltpu.VMEM(value_matrix.shape, BF16),
             pltpu.VMEM((2, chips, rows, width), BF16),
-            pltpu.SemaphoreType.DMA((steps + 1,)),
             pltpu.SemaphoreType.DMA((2, steps)),
         ],
         compiler_params=params(PART),
@@ -223,14 +215,14 @@
     return pl.pallas_call(
         kernel,
         out_shape=[jax.ShapeDtypeStruct((rows, width), BF16)] * chips,
-        in_specs=[ANY, ANY],
+        in_specs=[HBM, HBM],
         out_specs=[ANY] * chips,
         scratch_shapes=[pltpu.VMEM(own.shape, BF16)] * 3
         + [pltpu.SemaphoreType.DMA((2, chips)), pltpu.SemaphoreType.DMA((chips,))],
         compiler_params=params(PART),
         cost_estimate=cost(),
         name="add_cores",
-    )(own, other)
+    )(in_hbm(own), in_hbm(other))
 
 
 def back_product(holders, up, cotangent):
@@ -255,23 +247,10 @@
 
 def low_product(holders, down, tokens):
     tiles = holders.shape[0]
-    rows, features = tokens.shape
     rank = down.shape[1]
-    steps = 4
-    block = rows // steps
-
-    def kernel(h_ref, down_hbm, x_hbm, o_ref, down_ref, x_ref, sems):
-        fetch = start_all(
-            [pltpu.make_async_copy(down_hbm, down_ref, sems.at[steps])]
-            + [
-                pltpu.make_async_copy(x_hbm.at[span], x_ref.at[span], sems.at[step])
-                for step, span in enumerate([pl.ds(step * block, block) for step in range(steps)])
-            ]
-        )
-        fetch[0].wait()
+
+    def kernel(h_ref, down_ref, x_ref, o_ref):
         for tile in range(tiles):
-            if tile * TILE % block == 0:
-                fetch[1 + tile * TILE // block].wait()
             o_ref[tile] = dot(
                 down_ref[h_ref[tile]], x_ref[tile * TILE : (tile + 1) * TILE, :], (1, 1)
             ).astype(BF16)
@@ -279,13 +258,8 @@
     return pl.pallas_call(
         kernel,
         out_shape=jax.ShapeDtypeStruct((tiles, rank, TILE), BF16),
-        in_specs=[SMEM, ANY, ANY],
+        in_specs=[SMEM, VMEM, VMEM],
         out_specs=VMEM,
-        scratch_shapes=[
-            pltpu.VMEM(down.shape, BF16),
-            pltpu.VMEM(tokens.shape, BF16),
-            pltpu.SemaphoreType.DMA((steps + 1,)),
-        ],
         compiler_params=params(PART),
         cost_estimate=cost(1 << 40),
         name="low_product",
@@ -341,27 +315,16 @@
 
 def gradient_terms(holders, rank_side, wide_side, owners):
     tiles, rank, _ = rank_side.shape
-    rows, width = wide_side.shape
-    steps = 4
-    block = rows // steps
-
-    def kernel(h_ref, r_hbm, w_hbm, o_hbm, r_ref, w_ref, total, o_ref, in_sems, out_sems):
-        fetch = start_all(
-            [pltpu.make_async_copy(r_hbm, r_ref, in_sems.at[steps])]
-            + [
-                pltpu.make_async_copy(w_hbm.at[span], w_ref.at[span], in_sems.at[step])
-                for step, span in enumerate([pl.ds(step * block, block) for step in range(steps)])
-            ]
-        )
+    width = wide_side.shape[1]
+    parts = 4
+    part = owners // parts
+
+    def kernel(h_ref, r_ref, w_ref, o_hbm, total, o_ref, out_sems):
         total[...] = jnp.zeros_like(total)
-        fetch[0].wait()
         for tile in range(tiles):
-            if tile * TILE % block == 0:
-                fetch[1 + tile * TILE // block].wait()
             total[h_ref[tile]] += dot(r_ref[tile], w_ref[tile * TILE : (tile + 1) * TILE, :], (1, 0))
         stores = []
-        part = owners // 4
-        for index in range(4):
+        for index in range(parts):
             span = pl.ds(index * part, part)
             o_ref[span] = (ADAPTER_SCALE * total[span]).astype(BF16)
             stores += start_all([pltpu.make_async_copy(o_ref.at[span], o_hbm.at[span], out_sems.at[index])])
@@ -369,16 +332,13 @@
 
     return pl.pallas_call(
         kernel,
-        out_shape=jax.ShapeDtypeStruct((owners, rank, width), BF16),
-        in_specs=[SMEM, ANY, ANY],
+        out_shape=pltpu.HBM((owners, rank, width), BF16),
+        in_specs=[SMEM, VMEM, VMEM],
         out_specs=HBM,
         scratch_shapes=[
-            pltpu.VMEM(rank_side.shape, BF16),
-            pltpu.VMEM(wide_side.shape, BF16),
             pltpu.VMEM((owners, rank, width), F32),
             pltpu.VMEM((owners, rank, width), BF16),
-            pltpu.SemaphoreType.DMA((steps + 1,)),
-            pltpu.SemaphoreType.DMA((4,)),
+            pltpu.SemaphoreType.DMA((parts,)),
         ],
         compiler_params=params(PART),
         cost_estimate=cost(),
@@ -501,8 +461,7 @@
 
     def kernel(h_ref, *refs):
         hbm = refs[:count]
-        v_hbm, b_hbm, down_hbm, o_hbm = refs[count : count + 4]
-        dy_ref, v_ref, b_ref, down_ref, o_ref, dy_sems, in_sems, out_sems = refs[count + 4 :]
+        v_ref, b_ref, down_ref, o_hbm, dy_ref, o_ref, dy_sems, out_sems = refs[count:]
         halves = []
         for half in range(2):
             span = pl.ds(half * middle, middle)
@@ -520,23 +479,16 @@
                     target = dy_ref.at[span, pl.ds(pl.multiple_of(place * width, width), width)]
                     copies.append(pltpu.make_async_copy(source, target, dy_sems.at[half, flip, index]))
             halves.append(copies)
-        fetch = [
-            pltpu.make_async_copy(source, target, in_sems.at[index])
-            for index, (source, target) in enumerate(((v_hbm, v_ref), (b_hbm, b_ref), (down_hbm, down_ref)))
-        ]
-        first = start_all(fetch[:1] + halves[0])
+        start_all(halves[0])
         stores = []
         for step in range(steps):
             if step == 0:
-                wait_all(first)
-                start_all(fetch[1:])
+                wait_all(halves[0])
+                start_all(halves[1])
             elif step * block == middle:
                 wait_all(halves[1])
             span = pl.ds(step * block, block)
             frozen = dot(dy_ref[span, :], v_ref[...], (1, 1))
-            if step == 0:
-                wait_all(fetch[1:])
-                start_all(halves[1])
             for tile in range(group):
                 adapter = dot(b_ref[step * group + tile], down_ref[h_ref[step * group + tile]], (0, 0))
                 o_ref[pl.ds(step * block + tile * TILE, TILE), :] = (
@@ -548,22 +500,18 @@
     return pl.pallas_call(
         kernel,
         out_shape=jax.ShapeDtypeStruct((rows, features), BF16),
-        in_specs=[SMEM] + [ANY] * (count + 3),
+        in_specs=[SMEM] + [HBM] * count + [VMEM] * 3,
         out_specs=HBM,
         scratch_shapes=[
             pltpu.VMEM((rows, columns), BF16),
-            pltpu.VMEM(value_matrix.shape, BF16),
-            pltpu.VMEM(back_low.shape, BF16),
-            pltpu.VMEM(down.shape, BF16),
             pltpu.VMEM((rows, features), BF16),
             pltpu.SemaphoreType.DMA((2, 2, 4)),
-            pltpu.SemaphoreType.DMA((3,)),
             pltpu.SemaphoreType.DMA((steps,)),
         ],
         compiler_params=params(PART),
         cost_estimate=cost(),
         name="input_product",
-    )(holders, *pieces, value_matrix, back_low, down)
+    )(holders, *map(in_hbm, pieces), value_matrix, back_low, down)
 
 
 def swap_cores(array):

time: 118 us -> 115 us (0.975)
  local copies, waits for them, and re-layouts: 12.8 us -> 6.24 us
  waiting for transfers between devices: 14.5 us -> 20.1 us
  Pallas kernels: 43.3 us -> 41.6 us
    unnamed x50 -> x38, local copies, waits for them, and re-layouts: 11.8 us -> 5.25 us
    ppermute x13, waiting for transfers between devices: 5.18 us -> 9.53 us  [along_x(): lax.ppermute(array, 'tensor', [(i, (i // 2 + k) % chips * 2 + i % 2) for...]
    all_to_all x1, waiting for transfers between devices: 2.47 us -> 3.99 us  [shards(): lax.all_to_all(send_down_terms, 'dp', split_axis=0, concat_axis=0, tiled=...]
  transfers between devices with their start and end apart: 25 -> 25, of which waited for: 6 -> 8; matrix products, arithmetic and copies ran while one was open for 1% -> 1% of each run, Pallas kernels for 36% -> 35%
where the time goes in v3:
time: 115 us; the launch traced here: 113 us
  starting transfers between devices  43.9 us (38%)
  Pallas kernels  41.6 us (36%)
  waiting for transfers between devices  20.1 us (17%)
  local copies, waits for them, and re-layouts  6.24 us (5%)
    ppermute x13, starting transfers between devices, along_x(): lax.ppermute(array, 'tensor', [(i, (i // 2 + k) % chips * 2 + i % 2) for...  19.2 us
    ppermute x13, waiting for transfers between devices, along_x(): lax.ppermute(array, 'tensor', [(i, (i // 2 + k) % chips * 2 + i % 2) for...  9.53 us
    pallas_call x1, Pallas kernels, input_product(): pl.pallas_call(kernel, out_shape=jax.ShapeDtypeStruct((rows, features), B...  9.2 us
    all_to_all x1, starting transfers between devices, shards(): up = lax.all_to_all(send_up, 'dp', split_axis=0, concat_axis=0, tiled=True)  8.16 us
    all_to_all x1, starting transfers between devices, shards(): lax.all_to_all(send_down_terms, 'dp', split_axis=0, concat_axis=0, tiled=...  7.23 us
    pallas_call x1, Pallas kernels, base_product(): pl.pallas_call(kernel, out_shape=(shape, shape), in_specs=[VMEM, VMEM], o...  5.54 us
    unnamed x38, local copies, waits for them, and re-layouts  5.25 us
    all_to_all x1, waiting for transfers between devices, shards(): up = lax.all_to_all(send_up, 'dp', split_axis=0, concat_axis=0, tiled=True)  4.39 us
  transfers between devices with their start and end apart: 25, of which 8 were waited for; matrix products, arithmetic and copies ran while one was open for 1% of the time, Pallas kernels for 35%

profile of v3, /device:TPU:0, one launch (start us, length us, event | category | flops | bytes accessed | tf_op | source)
XLA Modules:
  0.0 113.3 jit_solution(5126218208660984985)
XLA Ops:
  2.3 1.7 %collective-permute-start.1 = (bf16[2048,128]{1,0:T(8,128)(2,1)}, bf16[2048,128]{1,0:T(8,128)(2,1)}, u32[]{:S(2)}, u32[]{:S(2)}) collective-permute-start(bf16[2048,128]{1,0:T(8,128)(2,1)} %w_ref.3), channel_id=1, source_target_pairs={{0,6},{1,7},{2,0},{3,1},{4,2},{5,3},{6,4},{7,5},{8,14},{9,15},{10,... | collective-permute-start | bytes 1572872 | tf_op jit(solution)/shard_map/ppermute | solution.py:525
  3.9 3.7 %route_up.1 = (s32[16]{0:T(128)}, s32[16]{0:T(128)}, bf16[16,64,128]{2,1,0:T(8,128)(2,1)}) custom-call(s32[128]{0:T(128)} %usage_hbm.1, s32[256]{0:T(256)} %map_hbm.1, s32[16]{0:T(128)} %entry_hbm.1, bf16[16,64,128]{2,1,0:T(8,128)(2,1)} %up_ref.1), custom_call_target="tpu_custom_call" | custom-call | flops 1024 | bytes 1024 | tf_op jit(solution)/shard_map/route_up/pallas_call | solution.py:84
  7.7 8.2 %all-to-all-start = ((bf16[16,64,128]{2,1,0:T(8,128)(2,1)}), bf16[16,64,128]{2,1,0:T(8,128)(2,1)S(1)}, u32[]{:S(2)}, u32[]{:S(2)}) async-start(bf16[16,64,128]{2,1,0:T(8,128)(2,1)} %get-tuple-element.25), calls=%async_computation | async-start | bytes 524288 | tf_op jit(solution)/shard_map/all_to_all | solution.py:559
  15.8 4.2 %select_down.1 = bf16[16,64,1024]{2,1,0:T(8,128)(2,1)} custom-call(s32[16]{0:T(128)} %get-tuple-element.26.rows_ref, bf16[16,64,1024]{2,1,0:T(8,128)(2,1)} %bitcast.2), custom_call_target="tpu_custom_call" | custom-call | flops 1024 | bytes 1024 | tf_op jit(solution)/shard_map/select_down/pallas_call | solution.py:118
  20.1 4.4 %all-to-all-done.up_ref.refs_5_ = bf16[16,64,128]{2,1,0:T(8,128)(2,1)S(1)} async-done(((bf16[16,64,128]{2,1,0:T(8,128)(2,1)}), bf16[16,64,128]{2,1,0:T(8,128)(2,1)S(1)}, u32[]{:S(2)}, u32[]{:S(2)}) %all-to-all-start) | async-done | bytes 262176 | tf_op jit(solution)/shard_map/all_to_all | solution.py:559
  24.5 3.7 %all-to-all-start.1 = ((bf16[16,64,1024]{2,1,0:T(8,128)(2,1)}), bf16[16,64,1024]{2,1,0:T(8,128)(2,1)S(1)}, u32[]{:S(2)}, u32[]{:S(2)}) async-start(bf16[16,64,1024]{2,1,0:T(8,128)(2,1)} %select_down.1), calls=%async_computation.1 | async-start | bytes 4194304 | tf_op jit(solution)/shard_map/all_to_all | solution.py:562
  33.6 3.0 %collective-permute-start.14 = (bf16[1024,128]{1,0:T(8,128)(2,1)S(1)}, bf16[1024,128]{1,0:T(8,128)(2,1)S(1)}, u32[]{:S(2)}, u32[]{:S(2)}) collective-permute-start(bf16[1024,128]{1,0:T(8,128)(2,1)S(1)} %slice.9), channel_id=1, source_target_pairs={{0,6},{1,7},{2,0},{3,1},{4,2},{5,3},{6,4},{7,5},{8,14},{9,15},{10,... | collective-permute-start | bytes 786440 | tf_op jit(solution)/shard_map/ppermute | solution.py:525
  39.5 2.2 %copy-done = bf16[2048,1024]{1,0:T(8,128)(2,1)S(1)} copy-done((bf16[2048,1024]{1,0:T(8,128)(2,1)S(1)}, bf16[2048,1024]{1,0:T(8,128)(2,1)}, u32[]{:S(2)}) %copy-start) | copy-done | bytes 4194328
  41.7 5.5 %base_product.1 = (bf16[4,2048,128]{2,1,0:T(8,128)(2,1)}, bf16[4,2048,128]{2,1,0:T(8,128)(2,1)}) custom-call(bf16[2048,1024]{1,0:T(8,128)(2,1)S(1)} %copy-done, bf16[1024,1024]{1,0:T(8,128)(2,1)S(1)} %copy-done.3), custom_call_target="tpu_custom_call" | custom-call | flops 1024 | bytes 1024 | tf_op jit(solution)/shard_map/base_product/pallas_call | solution.py:177
  49.0 4.7 %collective-permute-done.11 = bf16[16,64,128]{2,1,0:T(8,128)(2,1)S(1)} collective-permute-done((bf16[16,64,128]{2,1,0:T(8,128)(2,1)S(1)}, bf16[16,64,128]{2,1,0:T(8,128)(2,1)S(1)}, u32[]{:S(2)}, u32[]{:S(2)}) %collective-permute-start.11) | collective-permute-done | bytes 262176 | tf_op jit(solution)/shard_map/ppermute | solution.py:525
  54.0 3.0 %gradient_terms.1 = bf16[16,64,1024]{2,1,0:T(8,128)(2,1)} custom-call(s32[16]{0:T(128)S(1)} %copy-done.7, bf16[16,64,128]{2,1,0:T(8,128)(2,1)S(1)} %add_convert_fusion.2.r_ref.refs_11_, bf16[2048,1024]{1,0:T(8,128)(2,1)S(1)} %copy-done.1), custom_call_target="tpu_custom_call" | custom-call | flops 1024 | bytes 1024 | tf_op jit(solution)/shard_map/gradient_terms/pallas_call | solution.py:333
  57.0 7.2 %all-to-all-start.2 = ((bf16[16,64,1024]{2,1,0:T(8,128)(2,1)}), bf16[16,64,1024]{2,1,0:T(8,128)(2,1)}, u32[]{:S(2)}, u32[]{:S(2)}) async-start(bf16[16,64,1024]{2,1,0:T(8,128)(2,1)} %gradient_terms.1), calls=%async_computation.2 | async-start | bytes 4194304 | tf_op jit(solution)/shard_map/all_to_all | solution.py:579
  64.2 2.2 %copy-done.2 = bf16[2048,1024]{1,0:T(8,128)(2,1)S(1)} copy-done((bf16[2048,1024]{1,0:T(8,128)(2,1)S(1)}, bf16[2048,1024]{1,0:T(8,128)(2,1)}, u32[]{:S(2)}) %copy-start.2) | copy-done | bytes 4194328
  66.4 2.1 %low_product.1 = bf16[16,64,128]{2,1,0:T(8,128)(2,1)S(1)} custom-call(s32[16]{0:T(128)S(1)} %copy-done.7, bf16[16,64,1024]{2,1,0:T(8,128)(2,1)S(1)} %all-to-all-done.1.down_ref.refs_12_, bf16[2048,1024]{1,0:T(8,128)(2,1)S(1)} %copy-done.2), custom_call_target="tpu_custom_call" | custom-call | flops 1099511627776 | bytes 1024 | tf_op jit(solution)/shard_map/low_product/pallas_call | solution.py:258
  70.4 2.4 %collective-permute-start.18 = (bf16[16,64,128]{2,1,0:T(8,128)(2,1)S(1)}, bf16[16,64,128]{2,1,0:T(8,128)(2,1)S(1)}, u32[]{:S(2)}, u32[]{:S(2)}) collective-permute-start(bf16[16,64,128]{2,1,0:T(8,128)(2,1)S(1)} %add_convert_fusion.1), channel_id=1, source_target_pairs={{0,4},{1,5},{2,6},{3,7},{4,0},{5,1},{6,2},{7,3},{8,12},{9,13},{10,... | collective-permute-start | bytes 786440 | tf_op jit(solution)/shard_map/ppermute | solution.py:525
  75.0 3.2 %add_cores.1 = (bf16[2048,128]{1,0:T(8,128)(2,1)S(1)}, bf16[2048,128]{1,0:T(8,128)(2,1)}, bf16[2048,128]{1,0:T(8,128)(2,1)}, bf16[2048,128]{1,0:T(8,128)(2,1)}) custom-call(bf16[4,2048,128]{2,1,0:T(8,128)(2,1)} %get-tuple-element.31.own_hbm, bf16[4,2048,128]{2,1,0:T(8,128)(2,1)} %collective-permute-done.6.other_hbm), custom_call_target="tpu_custom_call" | custom-call | flops 1024 | bytes 1024 | tf_op jit(solution)/shard_map/add_cores/pallas_call | solution.py:215
  78.3 2.1 %collective-permute-start.7 = (bf16[2048,128]{1,0:T(8,128)(2,1)}, bf16[2048,128]{1,0:T(8,128)(2,1)}, u32[]{:S(2)}, u32[]{:S(2)}) collective-permute-start(bf16[2048,128]{1,0:T(8,128)(2,1)} %get-tuple-element.34), channel_id=1, source_target_pairs={{0,2},{1,3},{2,4},{3,5},{4,6},{5,7},{6,0},{7,1},{8,10},{9,11},{10,... | collective-permute-start | bytes 1572872 | tf_op jit(solution)/shard_map/ppermute | solution.py:525
  81.6 1.9 %collective-permute-start.9 = (bf16[2048,128]{1,0:T(8,128)(2,1)}, bf16[2048,128]{1,0:T(8,128)(2,1)}, u32[]{:S(2)}, u32[]{:S(2)}) collective-permute-start(bf16[2048,128]{1,0:T(8,128)(2,1)} %get-tuple-element.36), channel_id=1, source_target_pairs={{0,4},{1,5},{2,6},{3,7},{4,0},{5,1},{6,2},{7,3},{8,12},{9,13},{10,... | collective-permute-start | bytes 1572872 | tf_op jit(solution)/shard_map/ppermute | solution.py:525
  83.5 9.2 %input_product.1 = bf16[2048,1024]{1,0:T(8,128)(2,1)} custom-call(s32[16]{0:T(128)S(1)} %copy-done.7, bf16[2048,128]{1,0:T(8,128)(2,1)} %w_ref.3, bf16[2048,128]{1,0:T(8,128)(2,1)} %copy-done.9, bf16[2048,128]{1,0:T(8,128)(2,1)} %collective-permute-done.1.refs_2_, bf16[1024,128]{1,0:T(8,128)(2,1)} %copy-done.13, bf16[1024,128]{1,0:T(8,128)(2,1)} %copy-done.15, ...), custom_call_target="tpu_custom_call" | custom-call | flops 1024 | bytes 1024 | tf_op jit(solution)/shard_map/input_product/pallas_call | solution.py:500
  94.4 4.0 %all-to-all-done.2.r_hbm = bf16[16,64,1024]{2,1,0:T(8,128)(2,1)} async-done(((bf16[16,64,1024]{2,1,0:T(8,128)(2,1)}), bf16[16,64,1024]{2,1,0:T(8,128)(2,1)}, u32[]{:S(2)}, u32[]{:S(2)}) %all-to-all-start.2) | async-done | bytes 2097184 | tf_op jit(solution)/shard_map/all_to_all | solution.py:579
  98.4 3.6 %all-to-all-start.3 = ((bf16[16,64,128]{2,1,0:T(8,128)(2,1)}), bf16[16,64,128]{2,1,0:T(8,128)(2,1)S(1)}, u32[]{:S(2)}, u32[]{:S(2)}) async-start(bf16[16,64,128]{2,1,0:T(8,128)(2,1)} %narrow_terms.1), calls=%async_computation.3 | async-start | bytes 524288 | tf_op jit(solution)/shard_map/all_to_all | solution.py:589
  102.1 3.5 %combine.1 = bf16[16,64,1024]{2,1,0:T(8,128)(2,1)} custom-call(s32[16]{0:T(128)S(1)} %copy-done.8, bf16[16,64,1024]{2,1,0:T(8,128)(2,1)} %all-to-all-done.2.r_hbm), custom_call_target="tpu_custom_call" | custom-call | flops 1024 | bytes 1024 | tf_op jit(solution)/shard_map/combine/pallas_call | solution.py:376
  105.5 3.1 %collective-permute-done.9.refs_3_ = bf16[2048,128]{1,0:T(8,128)(2,1)} collective-permute-done((bf16[2048,128]{1,0:T(8,128)(2,1)}, bf16[2048,128]{1,0:T(8,128)(2,1)}, u32[]{:S(2)}, u32[]{:S(2)}) %collective-permute-start.9) | collective-permute-done | bytes 524320 | tf_op jit(solution)/shard_map/ppermute | solution.py:525
  108.6 3.2 %finish_projected.1 = bf16[2048,128]{1,0:T(8,128)(2,1)} custom-call(s32[16]{0:T(128)S(1)} %copy-done.7, bf16[2048,128]{1,0:T(8,128)(2,1)S(1)} %get-tuple-element.33.refs_0_, bf16[2048,128]{1,0:T(8,128)(2,1)} %collective-permute-done.7.refs_1_, bf16[2048,128]{1,0:T(8,128)(2,1)} %collective-permute-done.8.refs_2_, ...), custom_call_target="tpu_custom_call" | custom-call | flops 1024 | bytes 1024 | tf_op jit(solution)/shard_map/finish_projected/pallas_call | solution.py:433
  (82 shorter events, 20.4 us)
Async XLA Ops:
  0.6 19.5 %collective-permute-start = (bf16[2048,128]{1,0:T(8,128)(2,1)}, bf16[2048,128]{1,0:T(8,128)(2,1)S(1)}, u32[]{:S(2)}, u32[]{:S(2)}) collective-permute-start(bf16[2048,128]{1,0:T(8,128)(2,1)} %w_ref.3), channel_id=1, source_target_pairs={{0,2},{1,3},{2,4},{3,5},{4,6},{5,7},{6,0},{7,1},{8,10},{9,11},{10,... | collective-permute-start | bytes 1572872 | tf_op jit(solution)/shard_map/ppermute | solution.py:525
  2.3 17.8 %collective-permute-start.1 = (bf16[2048,128]{1,0:T(8,128)(2,1)}, bf16[2048,128]{1,0:T(8,128)(2,1)}, u32[]{:S(2)}, u32[]{:S(2)}) collective-permute-start(bf16[2048,128]{1,0:T(8,128)(2,1)} %w_ref.3), channel_id=1, source_target_pairs={{0,6},{1,7},{2,0},{3,1},{4,2},{5,3},{6,4},{7,5},{8,14},{9,15},{10,... | collective-permute-start | bytes 1572872 | tf_op jit(solution)/shard_map/ppermute | solution.py:525
  7.7 16.9 %all-to-all-start = ((bf16[16,64,128]{2,1,0:T(8,128)(2,1)}), bf16[16,64,128]{2,1,0:T(8,128)(2,1)S(1)}, u32[]{:S(2)}, u32[]{:S(2)}) async-start(bf16[16,64,128]{2,1,0:T(8,128)(2,1)} %get-tuple-element.25), calls=%async_computation | async-start | bytes 524288 | tf_op jit(solution)/shard_map/all_to_all | solution.py:559
  24.5 32.4 %all-to-all-start.1 = ((bf16[16,64,1024]{2,1,0:T(8,128)(2,1)}), bf16[16,64,1024]{2,1,0:T(8,128)(2,1)S(1)}, u32[]{:S(2)}, u32[]{:S(2)}) async-start(bf16[16,64,1024]{2,1,0:T(8,128)(2,1)} %select_down.1), calls=%async_computation.1 | async-start | bytes 4194304 | tf_op jit(solution)/shard_map/all_to_all | solution.py:562
  28.3 2.0 %collective-permute-start.2 = (bf16[2048,128]{1,0:T(8,128)(2,1)S(1)}, bf16[2048,128]{1,0:T(8,128)(2,1)S(1)}, u32[]{:S(2)}, u32[]{:S(2)}) collective-permute-start(bf16[2048,128]{1,0:T(8,128)(2,1)S(1)} %copy-done.5), channel_id=1, source_target_pairs={{0,1},{1,0},{2,3},{3,2},{4,5},{5,4},{6,7},{7,6},{8,9},{9,8},{10,11... | collective-permute-start | bytes 1572872 | tf_op jit(solution)/shard_map/ppermute | solution.py:519
  28.4 8.4 %collective-permute-start.4 = (bf16[2048,128]{1,0:T(8,128)(2,1)S(1)}, bf16[2048,128]{1,0:T(8,128)(2,1)S(1)}, u32[]{:S(2)}, u32[]{:S(2)}) collective-permute-start(bf16[2048,128]{1,0:T(8,128)(2,1)S(1)} %collective-permute-done.refs_1_), channel_id=1, source_target_pairs={{0,1},{1,0},{2,3},{3,2},{4,5},{5,4},{6,7},{7,6},{8,9},{9,8},{10,11... | collective-permute-start | bytes 1572872 | tf_op jit(solution)/shard_map/ppermute | solution.py:519
  28.9 7.9 %collective-permute-start.5 = (bf16[2048,128]{1,0:T(8,128)(2,1)}, bf16[2048,128]{1,0:T(8,128)(2,1)S(1)}, u32[]{:S(2)}, u32[]{:S(2)}) collective-permute-start(bf16[2048,128]{1,0:T(8,128)(2,1)} %collective-permute-done.1.refs_2_), channel_id=1, source_target_pairs={{0,1},{1,0},{2,3},{3,2},{4,5},{5,4},{6,7},{7,6},{8,9},{9,8},{10,11... | collective-permute-start | bytes 1572872 | tf_op jit(solution)/shard_map/ppermute | solution.py:519
  32.1 4.6 %collective-permute-start.3 = (bf16[16,64,128]{2,1,0:T(8,128)(2,1)S(1)}, bf16[16,64,128]{2,1,0:T(8,128)(2,1)S(1)}, u32[]{:S(2)}, u32[]{:S(2)}) collective-permute-start(bf16[16,64,128]{2,1,0:T(8,128)(2,1)S(1)} %back_product.1), channel_id=1, source_target_pairs={{0,1},{1,0},{2,3},{3,2},{4,5},{5,4},{6,7},{7,6},{8,9},{9,8},{10,11... | collective-permute-start | bytes 786440 | tf_op jit(solution)/shard_map/ppermute | solution.py:519
  32.3 16.0 %collective-permute-start.13 = (bf16[1024,128]{1,0:T(8,128)(2,1)S(1)}, bf16[1024,128]{1,0:T(8,128)(2,1)S(1)}, u32[]{:S(2)}, u32[]{:S(2)}) collective-permute-start(bf16[1024,128]{1,0:T(8,128)(2,1)S(1)} %slice.8), channel_id=1, source_target_pairs={{0,2},{1,3},{2,4},{3,5},{4,6},{5,7},{6,0},{7,1},{8,10},{9,11},{10,... | collective-permute-start | bytes 786440 | tf_op jit(solution)/shard_map/ppermute | solution.py:525
  33.6 15.3 %collective-permute-start.14 = (bf16[1024,128]{1,0:T(8,128)(2,1)S(1)}, bf16[1024,128]{1,0:T(8,128)(2,1)S(1)}, u32[]{:S(2)}, u32[]{:S(2)}) collective-permute-start(bf16[1024,128]{1,0:T(8,128)(2,1)S(1)} %slice.9), channel_id=1, source_target_pairs={{0,6},{1,7},{2,0},{3,1},{4,2},{5,3},{6,4},{7,5},{8,14},{9,15},{10,... | collective-permute-start | bytes 786440 | tf_op jit(solution)/shard_map/ppermute | solution.py:525
  36.8 12.2 %collective-permute-start.12 = (bf16[16,64,128]{2,1,0:T(8,128)(2,1)S(1)}, bf16[16,64,128]{2,1,0:T(8,128)(2,1)S(1)}, u32[]{:S(2)}, u32[]{:S(2)}) collective-permute-start(bf16[16,64,128]{2,1,0:T(8,128)(2,1)S(1)} %add_convert_fusion.3), channel_id=1, source_target_pairs={{0,4},{1,5},{2,6},{3,7},{4,0},{5,1},{6,2},{7,3},{8,12},{9,13},{10,... | collective-permute-start | bytes 786440 | tf_op jit(solution)/shard_map/ppermute | solution.py:525
  37.5 16.2 %collective-permute-start.11 = (bf16[16,64,128]{2,1,0:T(8,128)(2,1)S(1)}, bf16[16,64,128]{2,1,0:T(8,128)(2,1)S(1)}, u32[]{:S(2)}, u32[]{:S(2)}) collective-permute-start(bf16[16,64,128]{2,1,0:T(8,128)(2,1)S(1)} %add_convert_fusion.3), channel_id=1, source_target_pairs={{0,6},{1,7},{2,0},{3,1},{4,2},{5,3},{6,4},{7,5},{8,14},{9,15},{10,... | collective-permute-start | bytes 786440 | tf_op jit(solution)/shard_map/ppermute | solution.py:525
  38.6 15.1 %collective-permute-start.10 = (bf16[16,64,128]{2,1,0:T(8,128)(2,1)S(1)}, bf16[16,64,128]{2,1,0:T(8,128)(2,1)S(1)}, u32[]{:S(2)}, u32[]{:S(2)}) collective-permute-start(bf16[16,64,128]{2,1,0:T(8,128)(2,1)S(1)} %add_convert_fusion.3), channel_id=1, source_target_pairs={{0,2},{1,3},{2,4},{3,5},{4,6},{5,7},{6,0},{7,1},{8,10},{9,11},{10,... | collective-permute-start | bytes 786440 | tf_op jit(solution)/shard_map/ppermute | solution.py:525
  53.9 20.3 %collective-permute-start.6 = (bf16[4,2048,128]{2,1,0:T(8,128)(2,1)}, bf16[4,2048,128]{2,1,0:T(8,128)(2,1)}, u32[]{:S(2)}, u32[]{:S(2)}) collective-permute-start(bf16[4,2048,128]{2,1,0:T(8,128)(2,1)} %get-tuple-element.32), channel_id=1, source_target_pairs={{0,1},{1,0},{2,3},{3,2},{4,5},{5,4},{6,7},{7,6},{8,9},{9,8},{10,11... | collective-permute-start | bytes 6291464 | tf_op jit(solution)/shard_map/ppermute | solution.py:519
  57.0 41.5 %all-to-all-start.2 = ((bf16[16,64,1024]{2,1,0:T(8,128)(2,1)}), bf16[16,64,1024]{2,1,0:T(8,128)(2,1)}, u32[]{:S(2)}, u32[]{:S(2)}) async-start(bf16[16,64,1024]{2,1,0:T(8,128)(2,1)} %gradient_terms.1), calls=%async_computation.2 | async-start | bytes 4194304 | tf_op jit(solution)/shard_map/all_to_all | solution.py:579
  69.0 9.3 %collective-permute-start.19 = (bf16[1024,128]{1,0:T(8,128)(2,1)S(1)}, bf16[1024,128]{1,0:T(8,128)(2,1)S(1)}, u32[]{:S(2)}, u32[]{:S(2)}) collective-permute-start(bf16[1024,128]{1,0:T(8,128)(2,1)S(1)} %copy-done.14), channel_id=1, source_target_pairs={{0,1},{1,0},{2,3},{3,2},{4,5},{5,4},{6,7},{7,6},{8,9},{9,8},{10,11... | collective-permute-start | bytes 786440 | tf_op jit(solution)/shard_map/ppermute | solution.py:519
  69.3 11.1 %collective-permute-start.20 = (bf16[1024,128]{1,0:T(8,128)(2,1)S(1)}, bf16[1024,128]{1,0:T(8,128)(2,1)S(1)}, u32[]{:S(2)}, u32[]{:S(2)}) collective-permute-start(bf16[1024,128]{1,0:T(8,128)(2,1)S(1)} %copy-done.16), channel_id=1, source_target_pairs={{0,1},{1,0},{2,3},{3,2},{4,5},{5,4},{6,7},{7,6},{8,9},{9,8},{10,11... | collective-permute-start | bytes 786440 | tf_op jit(solution)/shard_map/ppermute | solution.py:519
  70.4 11.2 %collective-permute-start.18 = (bf16[16,64,128]{2,1,0:T(8,128)(2,1)S(1)}, bf16[16,64,128]{2,1,0:T(8,128)(2,1)S(1)}, u32[]{:S(2)}, u32[]{:S(2)}) collective-permute-start(bf16[16,64,128]{2,1,0:T(8,128)(2,1)S(1)} %add_convert_fusion.1), channel_id=1, source_target_pairs={{0,4},{1,5},{2,6},{3,7},{4,0},{5,1},{6,2},{7,3},{8,12},{9,13},{10,... | collective-permute-start | bytes 786440 | tf_op jit(solution)/shard_map/ppermute | solution.py:525
  72.8 19.9 %collective-permute-start.17 = (bf16[16,64,128]{2,1,0:T(8,128)(2,1)S(1)}, bf16[16,64,128]{2,1,0:T(8,128)(2,1)S(1)}, u32[]{:S(2)}, u32[]{:S(2)}) collective-permute-start(bf16[16,64,128]{2,1,0:T(8,128)(2,1)S(1)} %add_convert_fusion.1), channel_id=1, source_target_pairs={{0,6},{1,7},{2,0},{3,1},{4,2},{5,3},{6,4},{7,5},{8,14},{9,15},{10,... | collective-permute-start | bytes 786440 | tf_op jit(solution)/shard_map/ppermute | solution.py:525
  74.2 18.4 %collective-permute-start.16 = (bf16[16,64,128]{2,1,0:T(8,128)(2,1)S(1)}, bf16[16,64,128]{2,1,0:T(8,128)(2,1)S(1)}, u32[]{:S(2)}, u32[]{:S(2)}) collective-permute-start(bf16[16,64,128]{2,1,0:T(8,128)(2,1)S(1)} %add_convert_fusion.1), channel_id=1, source_target_pairs={{0,2},{1,3},{2,4},{3,5},{4,6},{5,7},{6,0},{7,1},{8,10},{9,11},{10,... | collective-permute-start | bytes 786440 | tf_op jit(solution)/shard_map/ppermute | solution.py:525
  78.3 27.3 %collective-permute-start.7 = (bf16[2048,128]{1,0:T(8,128)(2,1)}, bf16[2048,128]{1,0:T(8,128)(2,1)}, u32[]{:S(2)}, u32[]{:S(2)}) collective-permute-start(bf16[2048,128]{1,0:T(8,128)(2,1)} %get-tuple-element.34), channel_id=1, source_target_pairs={{0,2},{1,3},{2,4},{3,5},{4,6},{5,7},{6,0},{7,1},{8,10},{9,11},{10,... | collective-permute-start | bytes 1572872 | tf_op jit(solution)/shard_map/ppermute | solution.py:525
  80.4 25.2 %collective-permute-start.8 = (bf16[2048,128]{1,0:T(8,128)(2,1)}, bf16[2048,128]{1,0:T(8,128)(2,1)}, u32[]{:S(2)}, u32[]{:S(2)}) collective-permute-start(bf16[2048,128]{1,0:T(8,128)(2,1)} %get-tuple-element.35), channel_id=1, source_target_pairs={{0,6},{1,7},{2,0},{3,1},{4,2},{5,3},{6,4},{7,5},{8,14},{9,15},{10,... | collective-permute-start | bytes 1572872 | tf_op jit(solution)/shard_map/ppermute | solution.py:525
  81.6 27.0 %collective-permute-start.9 = (bf16[2048,128]{1,0:T(8,128)(2,1)}, bf16[2048,128]{1,0:T(8,128)(2,1)}, u32[]{:S(2)}, u32[]{:S(2)}) collective-permute-start(bf16[2048,128]{1,0:T(8,128)(2,1)} %get-tuple-element.36), channel_id=1, source_target_pairs={{0,4},{1,5},{2,6},{3,7},{4,0},{5,1},{6,2},{7,3},{8,12},{9,13},{10,... | collective-permute-start | bytes 1572872 | tf_op jit(solution)/shard_map/ppermute | solution.py:525
  98.4 13.4 %all-to-all-start.3 = ((bf16[16,64,128]{2,1,0:T(8,128)(2,1)}), bf16[16,64,128]{2,1,0:T(8,128)(2,1)S(1)}, u32[]{:S(2)}, u32[]{:S(2)}) async-start(bf16[16,64,128]{2,1,0:T(8,128)(2,1)} %narrow_terms.1), calls=%async_computation.3 | async-start | bytes 524288 | tf_op jit(solution)/shard_map/all_to_all | solution.py:589
  (20 other events, 123.4 us)

commit v4 on v3

--- a/solution.py
+++ b/solution.py
@@ -38,6 +38,17 @@
     return pltpu.CompilerParams(vmem_limit_bytes=limit)
 
 
+def start_all(copies):
+    for copy in copies:
+        copy.start()
+    return copies
+
+
+def wait_all(copies):
+    for copy in copies:
+        copy.wait()
+
+
 def pass_on(copies, held, target, sems):
     count = len(copies)
     onward = []
@@ -58,28 +69,25 @@
         tables = [
             pltpu.make_async_copy(source, target, table_sems.at[index])
             for index, (source, target) in enumerate(
-                ((usage_hbm, usage_ref), (map_hbm, map_ref), (entry_hbm, entry_ref))
+                ((usage_hbm, usage_ref), (map_hbm, map_ref), (entry_hbm, entry_ref), (up_ref, held))
             )
         ]
-        for copy in tables:
-            copy.start()
-        for copy in tables:
-            copy.wait()
+        start_all(tables)
+        wait_all(tables)
         mine = lax.axis_index("dp").astype(jnp.int32)
         copies = []
         for user in range(users):
             row = jnp.int32(-1)
             for slot in range(slots):
-                place = map_ref[usage_ref[user * slots + slot]]
-                row = jnp.where(place // holding == mine, place % holding, row)
+                place = map_ref[usage_ref[user * slots + slot]] - mine * holding
+                row = jnp.where((place >= 0) & (place < holding), place, row)
             rows_ref[user] = row
-            copies.append(
-                pltpu.make_async_copy(up_ref.at[jnp.maximum(row, 0)], held.at[user], sems.at[user])
+            copies += start_all(
+                [pltpu.make_async_copy(held.at[jnp.maximum(row, 0)], send_ref.at[user], sems.at[user])]
             )
-            copies[-1].start()
         for tile in range(tiles):
-            holders_ref[tile] = map_ref[usage_ref[mine * slots + entry_ref[tile]]] // holding
-        pass_on(copies, held, send_ref, sems)
+            holders_ref[tile] = lax.div(map_ref[usage_ref[mine * slots + entry_ref[tile]]], jnp.int32(holding))
+        wait_all(copies)
 
     return pl.pallas_call(
         kernel,
@@ -94,9 +102,9 @@
             pltpu.SMEM(usage.shape, jnp.int32),
             pltpu.SMEM(storage_row_map.shape, jnp.int32),
             pltpu.SMEM(entries.shape, jnp.int32),
-            pltpu.VMEM((users,) + up.shape[1:], BF16),
-            pltpu.SemaphoreType.DMA((2 * users,)),
-            pltpu.SemaphoreType.DMA((3,)),
+            pltpu.VMEM(up.shape, BF16),
+            pltpu.SemaphoreType.DMA((users,)),
+            pltpu.SemaphoreType.DMA((4,)),
         ],
         compiler_params=params(),
         cost_estimate=cost(),
@@ -136,17 +144,6 @@
     chips = size // 2
     core = me % 2 if flip == 0 else 1 - me % 2
     return [(me // 2 + chips + shift) % chips * 2 + core for shift in SHIFTS]
-
-
-def start_all(copies):
-    for copy in copies:
-        copy.start()
-    return copies
-
-
-def wait_all(copies):
-    for copy in copies:
-        copy.wait()
 
 
 def base_product(tokens, value_matrix):
@@ -563,13 +560,13 @@
 
     first, last = along_x(left[:middle], 1), along_x(right[middle:], -1)
     own_swapped = swap_cores(cotangent)
-    back_part = back_product(holders, after(up, send_down, own_swapped), cotangent)
+    back_part = back_product(holders, after(up, send_down), cotangent)
     left_swapped, right_swapped = swap_cores(left), swap_cores(right)
-    back_chip = after(sum_on_chip(back_part), left_swapped, right_swapped)
+    back_chip = after(sum_on_chip(back_part), own_swapped, left_swapped, right_swapped)
     back_others = other_chips(back_chip)
     own_base, other_base = base_product(after(tokens, back_chip), value_matrix)
     first_swapped, last_swapped = swap_cores(first), swap_cores(last)
-    back_others[2] = after(back_others[2], own_base, first, last)
+    back_others[2] = after(back_others[2], own_base)
     back_low = sum_of(back_chip, back_others)
     pieces = [cotangent, left, right, first, last]
     pieces += [own_swapped, left_swapped, right_swapped, first_swapped, last_swapped]
@@ -578,7 +575,7 @@
     send_down_terms = gradient_terms(holders, back_low, tokens, owners)
     down_terms = lax.all_to_all(send_down_terms, "dp", split_axis=0, concat_axis=0, tiled=True)
 
-    low_chip = sum_on_chip(low_product(holders, after(down, send_down_terms), tokens))
+    low_chip = after(sum_on_chip(low_product(holders, after(down, send_down_terms), tokens)), first, last)
     low_others = other_chips(low_chip)
     pieces[0] = after(pieces[0], low_chip)
     input_gradient = input_product(holders, pieces, value_matrix, back_low, down)

time: 115 us -> 110 us (0.957)
  waiting for transfers between devices: 20.1 us -> 15.9 us
  Pallas kernels: 41.6 us -> 40.2 us
    ppermute x13, waiting for transfers between devices: 9.53 us -> 4.28 us  [along_x(): lax.ppermute(array, 'tensor', [(i, (i // 2 + k) % chips * 2 + i % 2) for...]
    all_to_all x1, waiting for transfers between devices: 0.01 us -> 4.27 us  [shards(): lax.all_to_all(send_down, 'dp', split_axis=0, concat_axis=0, tiled=True)]
    all_to_all x1, waiting for transfers between devices: 3.99 us -> 0.38 us  [shards(): lax.all_to_all(send_down_terms, 'dp', split_axis=0, concat_axis=0, tiled=...]
    all_to_all x1, starting transfers between devices: 3.62 us -> 6.72 us  [shards(): lax.all_to_all(send_up_terms, 'dp', split_axis=0, concat_axis=0, tiled=True)]
    all_to_all x1, starting transfers between devices: 7.23 us -> 4.44 us  [shards(): lax.all_to_all(send_down_terms, 'dp', split_axis=0, concat_axis=0, tiled=...]
    slice x2, local copies, waits for them, and re-layouts: 0.98 us -> 2.39 us  [shards(): first, last = (along_x(left[:middle], 1), along_x(right[middle:], -1))]
    pallas_call x1, Pallas kernels: 3.72 us -> 2.35 us  [route_up(): pl.pallas_call(kernel, out_shape=(jax.ShapeDtypeStruct((users,), jnp.int3...]
    unnamed x38 -> x32, local copies, waits for them, and re-layouts: 5.25 us -> 4.44 us
  transfers between devices with their start and end apart: 25 -> 25, of which waited for: 8 -> 7; matrix products, arithmetic and copies ran while one was open for 1% -> 3% of each run, Pallas kernels for 35% -> 36%
where the time goes in v4:
time: 110 us; the launch traced here: 109 us
  starting transfers between devices  44.7 us (41%)
  Pallas kernels  40.2 us (37%)
  waiting for transfers between devices  15.9 us (14%)
  local copies, waits for them, and re-layouts  6.83 us (6%)
    ppermute x13, starting transfers between devices, along_x(): lax.ppermute(array, 'tensor', [(i, (i // 2 + k) % chips * 2 + i % 2) for...  19.6 us
    pallas_call x1, Pallas kernels, input_product(): pl.pallas_call(kernel, out_shape=jax.ShapeDtypeStruct((rows, features), B...  9.23 us
    all_to_all x1, starting transfers between devices, shards(): up = lax.all_to_all(send_up, 'dp', split_axis=0, concat_axis=0, tiled=True)  8.14 us
    all_to_all x1, starting transfers between devices, shards(): lax.all_to_all(send_up_terms, 'dp', split_axis=0, concat_axis=0, tiled=True)  6.72 us
    pallas_call x1, Pallas kernels, base_product(): pl.pallas_call(kernel, out_shape=(shape, shape), in_specs=[VMEM, VMEM], o...  5.57 us
    all_to_all x1, waiting for transfers between devices, shards(): up = lax.all_to_all(send_up, 'dp', split_axis=0, concat_axis=0, tiled=True)  4.47 us
    unnamed x32, local copies, waits for them, and re-layouts  4.44 us
    all_to_all x1, starting transfers between devices, shards(): lax.all_to_all(send_down_terms, 'dp', split_axis=0, concat_axis=0, tiled=...  4.44 us
  transfers between devices with their start and end apart: 25, of which 7 were waited for; matrix products, arithmetic and copies ran while one was open for 3% of the time, Pallas kernels for 36%

profile of v4, /device:TPU:0, one launch (start us, length us, event | category | flops | bytes accessed | tf_op | source)
XLA Modules:
  0.0 109.1 jit_solution(1182726920751580882)
XLA Ops:
  3.9 2.3 %route_up.1 = (s32[16]{0:T(128)}, s32[16]{0:T(128)}, bf16[16,64,128]{2,1,0:T(8,128)(2,1)}) custom-call(s32[128]{0:T(128)} %usage_hbm.1, s32[256]{0:T(256)} %map_hbm.1, s32[16]{0:T(128)} %entry_hbm.1, bf16[16,64,128]{2,1,0:T(8,128)(2,1)} %up_ref.1), custom_call_target="tpu_custom_call" | custom-call | flops 1024 | bytes 1024 | tf_op jit(solution)/shard_map/route_up/pallas_call | solution.py:92
  6.3 8.1 %all-to-all-start = ((bf16[16,64,128]{2,1,0:T(8,128)(2,1)}), bf16[16,64,128]{2,1,0:T(8,128)(2,1)S(1)}, u32[]{:S(2)}, u32[]{:S(2)}) async-start(bf16[16,64,128]{2,1,0:T(8,128)(2,1)} %get-tuple-element.26), calls=%async_computation | async-start | bytes 524288 | tf_op jit(solution)/shard_map/all_to_all | solution.py:556
  14.4 4.1 %select_down.1 = bf16[16,64,1024]{2,1,0:T(8,128)(2,1)} custom-call(s32[16]{0:T(128)} %get-tuple-element.27.rows_ref, bf16[16,64,1024]{2,1,0:T(8,128)(2,1)} %bitcast.2), custom_call_target="tpu_custom_call" | custom-call | flops 1024 | bytes 1024 | tf_op jit(solution)/shard_map/select_down/pallas_call | solution.py:126
  18.7 4.5 %all-to-all-done.up_ref.refs_5_ = bf16[16,64,128]{2,1,0:T(8,128)(2,1)S(1)} async-done(((bf16[16,64,128]{2,1,0:T(8,128)(2,1)}), bf16[16,64,128]{2,1,0:T(8,128)(2,1)S(1)}, u32[]{:S(2)}, u32[]{:S(2)}) %all-to-all-start) | async-done | bytes 262176 | tf_op jit(solution)/shard_map/all_to_all | solution.py:556
  23.1 3.7 %all-to-all-start.1 = ((bf16[16,64,1024]{2,1,0:T(8,128)(2,1)}), bf16[16,64,1024]{2,1,0:T(8,128)(2,1)S(1)}, u32[]{:S(2)}, u32[]{:S(2)}) async-start(bf16[16,64,1024]{2,1,0:T(8,128)(2,1)} %select_down.1), calls=%async_computation.1 | async-start | bytes 4194304 | tf_op jit(solution)/shard_map/all_to_all | solution.py:559
  29.1 1.7 %collective-permute-done.2 = bf16[16,64,128]{2,1,0:T(8,128)(2,1)S(1)} collective-permute-done((bf16[16,64,128]{2,1,0:T(8,128)(2,1)S(1)}, bf16[16,64,128]{2,1,0:T(8,128)(2,1)S(1)}, u32[]{:S(2)}, u32[]{:S(2)}) %collective-permute-start.2) | collective-permute-done | bytes 262176 | tf_op jit(solution)/shard_map/ppermute | solution.py:516
  30.9 1.9 %collective-permute-start.12 = (bf16[16,64,128]{2,1,0:T(8,128)(2,1)S(1)}, bf16[16,64,128]{2,1,0:T(8,128)(2,1)S(1)}, u32[]{:S(2)}, u32[]{:S(2)}) collective-permute-start(bf16[16,64,128]{2,1,0:T(8,128)(2,1)S(1)} %add_convert_fusion.3), channel_id=1, source_target_pairs={{0,4},{1,5},{2,6},{3,7},{4,0},{5,1},{6,2},{7,3},{8,12},{9,13},{10,... | collective-permute-start | bytes 786440 | tf_op jit(solution)/shard_map/ppermute | solution.py:522
  37.8 2.7 %collective-permute-start.15 = (bf16[1024,128]{1,0:T(8,128)(2,1)}, bf16[1024,128]{1,0:T(8,128)(2,1)}, u32[]{:S(2)}, u32[]{:S(2)}) collective-permute-start(bf16[1024,128]{1,0:T(8,128)(2,1)} %slice.9), channel_id=1, source_target_pairs={{0,6},{1,7},{2,0},{3,1},{4,2},{5,3},{6,4},{7,5},{8,14},{9,15},{10,... | collective-permute-start | bytes 786440 | tf_op jit(solution)/shard_map/ppermute | solution.py:522
  40.5 2.2 %copy-done = bf16[2048,1024]{1,0:T(8,128)(2,1)S(1)} copy-done((bf16[2048,1024]{1,0:T(8,128)(2,1)S(1)}, bf16[2048,1024]{1,0:T(8,128)(2,1)}, u32[]{:S(2)}) %copy-start) | copy-done | bytes 4194328
  42.7 5.6 %base_product.1 = (bf16[4,2048,128]{2,1,0:T(8,128)(2,1)}, bf16[4,2048,128]{2,1,0:T(8,128)(2,1)}) custom-call(bf16[2048,1024]{1,0:T(8,128)(2,1)S(1)} %copy-done, bf16[1024,1024]{1,0:T(8,128)(2,1)S(1)} %copy-done.3), custom_call_target="tpu_custom_call" | custom-call | flops 1024 | bytes 1024 | tf_op jit(solution)/shard_map/base_product/pallas_call | solution.py:174
  48.6 3.0 %gradient_terms.1 = bf16[16,64,1024]{2,1,0:T(8,128)(2,1)} custom-call(s32[16]{0:T(128)S(1)} %copy-done.7, bf16[16,64,128]{2,1,0:T(8,128)(2,1)S(1)} %add_convert_fusion.2.r_ref.refs_11_, bf16[2048,1024]{1,0:T(8,128)(2,1)S(1)} %copy-done.1), custom_call_target="tpu_custom_call" | custom-call | flops 1024 | bytes 1024 | tf_op jit(solution)/shard_map/gradient_terms/pallas_call | solution.py:330
  51.6 4.3 %all-to-all-done.1.down_ref.refs_12_ = bf16[16,64,1024]{2,1,0:T(8,128)(2,1)S(1)} async-done(((bf16[16,64,1024]{2,1,0:T(8,128)(2,1)}), bf16[16,64,1024]{2,1,0:T(8,128)(2,1)S(1)}, u32[]{:S(2)}, u32[]{:S(2)}) %all-to-all-start.1) | async-done | bytes 2097184 | tf_op jit(solution)/shard_map/all_to_all | solution.py:559
  55.9 4.4 %all-to-all-start.2 = ((bf16[16,64,1024]{2,1,0:T(8,128)(2,1)}), bf16[16,64,1024]{2,1,0:T(8,128)(2,1)}, u32[]{:S(2)}, u32[]{:S(2)}) async-start(bf16[16,64,1024]{2,1,0:T(8,128)(2,1)} %gradient_terms.1), calls=%async_computation.2 | async-start | bytes 4194304 | tf_op jit(solution)/shard_map/all_to_all | solution.py:576
  60.3 2.2 %copy-done.2 = bf16[2048,1024]{1,0:T(8,128)(2,1)S(1)} copy-done((bf16[2048,1024]{1,0:T(8,128)(2,1)S(1)}, bf16[2048,1024]{1,0:T(8,128)(2,1)}, u32[]{:S(2)}) %copy-start.2) | copy-done | bytes 4194328
  62.5 2.1 %low_product.1 = bf16[16,64,128]{2,1,0:T(8,128)(2,1)S(1)} custom-call(s32[16]{0:T(128)S(1)} %copy-done.7, bf16[16,64,1024]{2,1,0:T(8,128)(2,1)S(1)} %all-to-all-done.1.down_ref.refs_12_, bf16[2048,1024]{1,0:T(8,128)(2,1)S(1)} %copy-done.2), custom_call_target="tpu_custom_call" | custom-call | flops 1099511627776 | bytes 1024 | tf_op jit(solution)/shard_map/low_product/pallas_call | solution.py:255
  66.3 1.9 %collective-permute-start.18 = (bf16[16,64,128]{2,1,0:T(8,128)(2,1)S(1)}, bf16[16,64,128]{2,1,0:T(8,128)(2,1)S(1)}, u32[]{:S(2)}, u32[]{:S(2)}) collective-permute-start(bf16[16,64,128]{2,1,0:T(8,128)(2,1)S(1)} %add_convert_fusion.1), channel_id=1, source_target_pairs={{0,4},{1,5},{2,6},{3,7},{4,0},{5,1},{6,2},{7,3},{8,12},{9,13},{10,... | collective-permute-start | bytes 786440 | tf_op jit(solution)/shard_map/ppermute | solution.py:522
  70.2 3.2 %add_cores.1 = (bf16[2048,128]{1,0:T(8,128)(2,1)S(1)}, bf16[2048,128]{1,0:T(8,128)(2,1)}, bf16[2048,128]{1,0:T(8,128)(2,1)}, bf16[2048,128]{1,0:T(8,128)(2,1)}) custom-call(bf16[4,2048,128]{2,1,0:T(8,128)(2,1)} %get-tuple-element.32.own_hbm, bf16[4,2048,128]{2,1,0:T(8,128)(2,1)} %collective-permute-done.6.other_hbm), custom_call_target="tpu_custom_call" | custom-call | flops 1024 | bytes 1024 | tf_op jit(solution)/shard_map/add_cores/pallas_call | solution.py:212
  74.1 2.6 %collective-permute-start.8 = (bf16[2048,128]{1,0:T(8,128)(2,1)}, bf16[2048,128]{1,0:T(8,128)(2,1)}, u32[]{:S(2)}, u32[]{:S(2)}) collective-permute-start(bf16[2048,128]{1,0:T(8,128)(2,1)} %get-tuple-element.36), channel_id=1, source_target_pairs={{0,6},{1,7},{2,0},{3,1},{4,2},{5,3},{6,4},{7,5},{8,14},{9,15},{10,... | collective-permute-start | bytes 1572872 | tf_op jit(solution)/shard_map/ppermute | solution.py:522
  77.1 1.8 %collective-permute-start.9 = (bf16[2048,128]{1,0:T(8,128)(2,1)}, bf16[2048,128]{1,0:T(8,128)(2,1)}, u32[]{:S(2)}, u32[]{:S(2)}) collective-permute-start(bf16[2048,128]{1,0:T(8,128)(2,1)} %get-tuple-element.37), channel_id=1, source_target_pairs={{0,4},{1,5},{2,6},{3,7},{4,0},{5,1},{6,2},{7,3},{8,12},{9,13},{10,... | collective-permute-start | bytes 1572872 | tf_op jit(solution)/shard_map/ppermute | solution.py:522
  78.9 9.2 %input_product.1 = bf16[2048,1024]{1,0:T(8,128)(2,1)} custom-call(s32[16]{0:T(128)S(1)} %copy-done.7, bf16[2048,128]{1,0:T(8,128)(2,1)} %w_ref.3, bf16[2048,128]{1,0:T(8,128)(2,1)} %copy-done.9, bf16[2048,128]{1,0:T(8,128)(2,1)} %copy-done.10, bf16[1024,128]{1,0:T(8,128)(2,1)} %collective-permute-done.14.refs_3_, ...), custom_call_target="tpu_custom_call" | custom-call | flops 1024 | bytes 1024 | tf_op jit(solution)/shard_map/input_product/pallas_call | solution.py:497
  90.3 6.7 %all-to-all-start.3 = ((bf16[16,64,128]{2,1,0:T(8,128)(2,1)}), bf16[16,64,128]{2,1,0:T(8,128)(2,1)S(1)}, u32[]{:S(2)}, u32[]{:S(2)}) async-start(bf16[16,64,128]{2,1,0:T(8,128)(2,1)} %narrow_terms.1), calls=%async_computation.3 | async-start | bytes 524288 | tf_op jit(solution)/shard_map/all_to_all | solution.py:586
  97.0 3.5 %combine.1 = bf16[16,64,1024]{2,1,0:T(8,128)(2,1)} custom-call(s32[16]{0:T(128)S(1)} %copy-done.8, bf16[16,64,1024]{2,1,0:T(8,128)(2,1)} %all-to-all-done.2.r_hbm), custom_call_target="tpu_custom_call" | custom-call | flops 1024 | bytes 1024 | tf_op jit(solution)/shard_map/combine/pallas_call | solution.py:373
  100.5 3.9 %collective-permute-done.9.refs_3_ = bf16[2048,128]{1,0:T(8,128)(2,1)} collective-permute-done((bf16[2048,128]{1,0:T(8,128)(2,1)}, bf16[2048,128]{1,0:T(8,128)(2,1)}, u32[]{:S(2)}, u32[]{:S(2)}) %collective-permute-start.9) | collective-permute-done | bytes 524320 | tf_op jit(solution)/shard_map/ppermute | solution.py:522
  104.5 3.2 %finish_projected.1 = bf16[2048,128]{1,0:T(8,128)(2,1)} custom-call(s32[16]{0:T(128)S(1)} %copy-done.7, bf16[2048,128]{1,0:T(8,128)(2,1)S(1)} %get-tuple-element.34.refs_0_, bf16[2048,128]{1,0:T(8,128)(2,1)} %collective-permute-done.7.refs_1_, bf16[2048,128]{1,0:T(8,128)(2,1)} %collective-permute-done.8.refs_2_, ...), custom_call_target="tpu_custom_call" | custom-call | flops 1024 | bytes 1024 | tf_op jit(solution)/shard_map/finish_projected/pallas_call | solution.py:430
  (76 shorter events, 19.2 us)
Async XLA Ops:
  0.6 18.0 %collective-permute-start = (bf16[2048,128]{1,0:T(8,128)(2,1)}, bf16[2048,128]{1,0:T(8,128)(2,1)S(1)}, u32[]{:S(2)}, u32[]{:S(2)}) collective-permute-start(bf16[2048,128]{1,0:T(8,128)(2,1)} %w_ref.3), channel_id=1, source_target_pairs={{0,2},{1,3},{2,4},{3,5},{4,6},{5,7},{6,0},{7,1},{8,10},{9,11},{10,... | collective-permute-start | bytes 1572872 | tf_op jit(solution)/shard_map/ppermute | solution.py:522
  2.3 16.4 %collective-permute-start.1 = (bf16[2048,128]{1,0:T(8,128)(2,1)}, bf16[2048,128]{1,0:T(8,128)(2,1)S(1)}, u32[]{:S(2)}, u32[]{:S(2)}) collective-permute-start(bf16[2048,128]{1,0:T(8,128)(2,1)} %w_ref.3), channel_id=1, source_target_pairs={{0,6},{1,7},{2,0},{3,1},{4,2},{5,3},{6,4},{7,5},{8,14},{9,15},{10,... | collective-permute-start | bytes 1572872 | tf_op jit(solution)/shard_map/ppermute | solution.py:522
  6.3 16.8 %all-to-all-start = ((bf16[16,64,128]{2,1,0:T(8,128)(2,1)}), bf16[16,64,128]{2,1,0:T(8,128)(2,1)S(1)}, u32[]{:S(2)}, u32[]{:S(2)}) async-start(bf16[16,64,128]{2,1,0:T(8,128)(2,1)} %get-tuple-element.26), calls=%async_computation | async-start | bytes 524288 | tf_op jit(solution)/shard_map/all_to_all | solution.py:556
  23.1 32.7 %all-to-all-start.1 = ((bf16[16,64,1024]{2,1,0:T(8,128)(2,1)}), bf16[16,64,1024]{2,1,0:T(8,128)(2,1)S(1)}, u32[]{:S(2)}, u32[]{:S(2)}) async-start(bf16[16,64,1024]{2,1,0:T(8,128)(2,1)} %select_down.1), calls=%async_computation.1 | async-start | bytes 4194304 | tf_op jit(solution)/shard_map/all_to_all | solution.py:559
  26.9 3.9 %collective-permute-start.3 = (bf16[2048,128]{1,0:T(8,128)(2,1)S(1)}, bf16[2048,128]{1,0:T(8,128)(2,1)S(1)}, u32[]{:S(2)}, u32[]{:S(2)}) collective-permute-start(bf16[2048,128]{1,0:T(8,128)(2,1)S(1)} %copy-done.5), channel_id=1, source_target_pairs={{0,1},{1,0},{2,3},{3,2},{4,5},{5,4},{6,7},{7,6},{8,9},{9,8},{10,11... | collective-permute-start | bytes 1572872 | tf_op jit(solution)/shard_map/ppermute | solution.py:516
  27.0 3.9 %collective-permute-start.4 = (bf16[2048,128]{1,0:T(8,128)(2,1)S(1)}, bf16[2048,128]{1,0:T(8,128)(2,1)S(1)}, u32[]{:S(2)}, u32[]{:S(2)}) collective-permute-start(bf16[2048,128]{1,0:T(8,128)(2,1)S(1)} %collective-permute-done.refs_1_), channel_id=1, source_target_pairs={{0,1},{1,0},{2,3},{3,2},{4,5},{5,4},{6,7},{7,6},{8,9},{9,8},{10,11... | collective-permute-start | bytes 1572872 | tf_op jit(solution)/shard_map/ppermute | solution.py:516
  27.5 3.4 %collective-permute-start.5 = (bf16[2048,128]{1,0:T(8,128)(2,1)}, bf16[2048,128]{1,0:T(8,128)(2,1)S(1)}, u32[]{:S(2)}, u32[]{:S(2)}) collective-permute-start(bf16[2048,128]{1,0:T(8,128)(2,1)} %copy-done.10), channel_id=1, source_target_pairs={{0,1},{1,0},{2,3},{3,2},{4,5},{5,4},{6,7},{7,6},{8,9},{9,8},{10,11... | collective-permute-start | bytes 1572872 | tf_op jit(solution)/shard_map/ppermute | solution.py:516
  28.6 2.2 %collective-permute-start.2 = (bf16[16,64,128]{2,1,0:T(8,128)(2,1)S(1)}, bf16[16,64,128]{2,1,0:T(8,128)(2,1)S(1)}, u32[]{:S(2)}, u32[]{:S(2)}) collective-permute-start(bf16[16,64,128]{2,1,0:T(8,128)(2,1)S(1)} %back_product.1), channel_id=1, source_target_pairs={{0,1},{1,0},{2,3},{3,2},{4,5},{5,4},{6,7},{7,6},{8,9},{9,8},{10,11... | collective-permute-start | bytes 786440 | tf_op jit(solution)/shard_map/ppermute | solution.py:516
  30.9 17.4 %collective-permute-start.12 = (bf16[16,64,128]{2,1,0:T(8,128)(2,1)S(1)}, bf16[16,64,128]{2,1,0:T(8,128)(2,1)S(1)}, u32[]{:S(2)}, u32[]{:S(2)}) collective-permute-start(bf16[16,64,128]{2,1,0:T(8,128)(2,1)S(1)} %add_convert_fusion.3), channel_id=1, source_target_pairs={{0,4},{1,5},{2,6},{3,7},{4,0},{5,1},{6,2},{7,3},{8,12},{9,13},{10,... | collective-permute-start | bytes 786440 | tf_op jit(solution)/shard_map/ppermute | solution.py:522
  32.8 15.5 %collective-permute-start.11 = (bf16[16,64,128]{2,1,0:T(8,128)(2,1)S(1)}, bf16[16,64,128]{2,1,0:T(8,128)(2,1)S(1)}, u32[]{:S(2)}, u32[]{:S(2)}) collective-permute-start(bf16[16,64,128]{2,1,0:T(8,128)(2,1)S(1)} %add_convert_fusion.3), channel_id=1, source_target_pairs={{0,6},{1,7},{2,0},{3,1},{4,2},{5,3},{6,4},{7,5},{8,14},{9,15},{10,... | collective-permute-start | bytes 786440 | tf_op jit(solution)/shard_map/ppermute | solution.py:522
  33.9 14.4 %collective-permute-start.10 = (bf16[16,64,128]{2,1,0:T(8,128)(2,1)S(1)}, bf16[16,64,128]{2,1,0:T(8,128)(2,1)S(1)}, u32[]{:S(2)}, u32[]{:S(2)}) collective-permute-start(bf16[16,64,128]{2,1,0:T(8,128)(2,1)S(1)} %add_convert_fusion.3), channel_id=1, source_target_pairs={{0,2},{1,3},{2,4},{3,5},{4,6},{5,7},{6,0},{7,1},{8,10},{9,11},{10,... | collective-permute-start | bytes 786440 | tf_op jit(solution)/shard_map/ppermute | solution.py:522
  35.5 29.1 %collective-permute-start.14 = (bf16[1024,128]{1,0:T(8,128)(2,1)}, bf16[1024,128]{1,0:T(8,128)(2,1)}, u32[]{:S(2)}, u32[]{:S(2)}) collective-permute-start(bf16[1024,128]{1,0:T(8,128)(2,1)} %slice.8), channel_id=1, source_target_pairs={{0,2},{1,3},{2,4},{3,5},{4,6},{5,7},{6,0},{7,1},{8,10},{9,11},{10,... | collective-permute-start | bytes 786440 | tf_op jit(solution)/shard_map/ppermute | solution.py:522
  37.8 27.4 %collective-permute-start.15 = (bf16[1024,128]{1,0:T(8,128)(2,1)}, bf16[1024,128]{1,0:T(8,128)(2,1)}, u32[]{:S(2)}, u32[]{:S(2)}) collective-permute-start(bf16[1024,128]{1,0:T(8,128)(2,1)} %slice.9), channel_id=1, source_target_pairs={{0,6},{1,7},{2,0},{3,1},{4,2},{5,3},{6,4},{7,5},{8,14},{9,15},{10,... | collective-permute-start | bytes 786440 | tf_op jit(solution)/shard_map/ppermute | solution.py:522
  48.5 20.8 %collective-permute-start.6 = (bf16[4,2048,128]{2,1,0:T(8,128)(2,1)}, bf16[4,2048,128]{2,1,0:T(8,128)(2,1)}, u32[]{:S(2)}, u32[]{:S(2)}) collective-permute-start(bf16[4,2048,128]{2,1,0:T(8,128)(2,1)} %get-tuple-element.33), channel_id=1, source_target_pairs={{0,1},{1,0},{2,3},{3,2},{4,5},{5,4},{6,7},{7,6},{8,9},{9,8},{10,11... | collective-permute-start | bytes 6291464 | tf_op jit(solution)/shard_map/ppermute | solution.py:516
  55.9 34.4 %all-to-all-start.2 = ((bf16[16,64,1024]{2,1,0:T(8,128)(2,1)}), bf16[16,64,1024]{2,1,0:T(8,128)(2,1)}, u32[]{:S(2)}, u32[]{:S(2)}) async-start(bf16[16,64,1024]{2,1,0:T(8,128)(2,1)} %gradient_terms.1), calls=%async_computation.2 | async-start | bytes 4194304 | tf_op jit(solution)/shard_map/all_to_all | solution.py:576
  64.7 8.7 %collective-permute-start.19 = (bf16[1024,128]{1,0:T(8,128)(2,1)}, bf16[1024,128]{1,0:T(8,128)(2,1)S(1)}, u32[]{:S(2)}, u32[]{:S(2)}) collective-permute-start(bf16[1024,128]{1,0:T(8,128)(2,1)} %collective-permute-done.14.refs_3_), channel_id=1, source_target_pairs={{0,1},{1,0},{2,3},{3,2},{4,5},{5,4},{6,7},{7,6},{8,9},{9,8},{10,11... | collective-permute-start | bytes 786440 | tf_op jit(solution)/shard_map/ppermute | solution.py:516
  65.2 8.9 %collective-permute-start.20 = (bf16[1024,128]{1,0:T(8,128)(2,1)}, bf16[1024,128]{1,0:T(8,128)(2,1)S(1)}, u32[]{:S(2)}, u32[]{:S(2)}) collective-permute-start(bf16[1024,128]{1,0:T(8,128)(2,1)} %collective-permute-done.15.refs_4_), channel_id=1, source_target_pairs={{0,1},{1,0},{2,3},{3,2},{4,5},{5,4},{6,7},{7,6},{8,9},{9,8},{10,11... | collective-permute-start | bytes 786440 | tf_op jit(solution)/shard_map/ppermute | solution.py:516
  66.3 10.8 %collective-permute-start.18 = (bf16[16,64,128]{2,1,0:T(8,128)(2,1)S(1)}, bf16[16,64,128]{2,1,0:T(8,128)(2,1)S(1)}, u32[]{:S(2)}, u32[]{:S(2)}) collective-permute-start(bf16[16,64,128]{2,1,0:T(8,128)(2,1)S(1)} %add_convert_fusion.1), channel_id=1, source_target_pairs={{0,4},{1,5},{2,6},{3,7},{4,0},{5,1},{6,2},{7,3},{8,12},{9,13},{10,... | collective-permute-start | bytes 786440 | tf_op jit(solution)/shard_map/ppermute | solution.py:522
  68.2 20.0 %collective-permute-start.17 = (bf16[16,64,128]{2,1,0:T(8,128)(2,1)S(1)}, bf16[16,64,128]{2,1,0:T(8,128)(2,1)S(1)}, u32[]{:S(2)}, u32[]{:S(2)}) collective-permute-start(bf16[16,64,128]{2,1,0:T(8,128)(2,1)S(1)} %add_convert_fusion.1), channel_id=1, source_target_pairs={{0,6},{1,7},{2,0},{3,1},{4,2},{5,3},{6,4},{7,5},{8,14},{9,15},{10,... | collective-permute-start | bytes 786440 | tf_op jit(solution)/shard_map/ppermute | solution.py:522
  69.3 18.8 %collective-permute-start.16 = (bf16[16,64,128]{2,1,0:T(8,128)(2,1)S(1)}, bf16[16,64,128]{2,1,0:T(8,128)(2,1)S(1)}, u32[]{:S(2)}, u32[]{:S(2)}) collective-permute-start(bf16[16,64,128]{2,1,0:T(8,128)(2,1)S(1)} %add_convert_fusion.1), channel_id=1, source_target_pairs={{0,2},{1,3},{2,4},{3,5},{4,6},{5,7},{6,0},{7,1},{8,10},{9,11},{10,... | collective-permute-start | bytes 786440 | tf_op jit(solution)/shard_map/ppermute | solution.py:522
  73.4 27.1 %collective-permute-start.7 = (bf16[2048,128]{1,0:T(8,128)(2,1)}, bf16[2048,128]{1,0:T(8,128)(2,1)}, u32[]{:S(2)}, u32[]{:S(2)}) collective-permute-start(bf16[2048,128]{1,0:T(8,128)(2,1)} %get-tuple-element.35), channel_id=1, source_target_pairs={{0,2},{1,3},{2,4},{3,5},{4,6},{5,7},{6,0},{7,1},{8,10},{9,11},{10,... | collective-permute-start | bytes 1572872 | tf_op jit(solution)/shard_map/ppermute | solution.py:522
  74.1 26.4 %collective-permute-start.8 = (bf16[2048,128]{1,0:T(8,128)(2,1)}, bf16[2048,128]{1,0:T(8,128)(2,1)}, u32[]{:S(2)}, u32[]{:S(2)}) collective-permute-start(bf16[2048,128]{1,0:T(8,128)(2,1)} %get-tuple-element.36), channel_id=1, source_target_pairs={{0,6},{1,7},{2,0},{3,1},{4,2},{5,3},{6,4},{7,5},{8,14},{9,15},{10,... | collective-permute-start | bytes 1572872 | tf_op jit(solution)/shard_map/ppermute | solution.py:522
  77.1 27.4 %collective-permute-start.9 = (bf16[2048,128]{1,0:T(8,128)(2,1)}, bf16[2048,128]{1,0:T(8,128)(2,1)}, u32[]{:S(2)}, u32[]{:S(2)}) collective-permute-start(bf16[2048,128]{1,0:T(8,128)(2,1)} %get-tuple-element.37), channel_id=1, source_target_pairs={{0,4},{1,5},{2,6},{3,7},{4,0},{5,1},{6,2},{7,3},{8,12},{9,13},{10,... | collective-permute-start | bytes 1572872 | tf_op jit(solution)/shard_map/ppermute | solution.py:522
  90.3 17.4 %all-to-all-start.3 = ((bf16[16,64,128]{2,1,0:T(8,128)(2,1)}), bf16[16,64,128]{2,1,0:T(8,128)(2,1)S(1)}, u32[]{:S(2)}, u32[]{:S(2)}) async-start(bf16[16,64,128]{2,1,0:T(8,128)(2,1)} %narrow_terms.1), calls=%async_computation.3 | async-start | bytes 524288 | tf_op jit(solution)/shard_map/all_to_all | solution.py:586
  (17 other events, 127.3 us)

commit v5 on v4

--- a/solution.py
+++ b/solution.py
@@ -392,59 +392,24 @@
     tiles = holders.shape[0]
     rows, width = terms[0].shape
     count = len(terms)
-    middle = rows // 2
-
-    def kernel(h_ref, *refs):
-        l_hbm, up_hbm, o_hbm, t_ref, l_ref, up_ref, o_ref, term_sems, in_sems, out_sems = refs[count:]
-        spans = [pl.ds(half * middle, middle) for half in range(2)]
-        fetch = start_all(
-            [
-                pltpu.make_async_copy(source, target, in_sems.at[index])
-                for index, (source, target) in enumerate(((l_hbm, l_ref), (up_hbm, up_ref)))
-            ]
-        )
-        halves = [
-            start_all(
-                [
-                    pltpu.make_async_copy(
-                        refs[index].at[span], t_ref.at[index, span], term_sems.at[half, index]
-                    )
-                    for index in range(count)
-                ]
-            )
-            for half, span in enumerate(spans)
-        ]
-        wait_all(fetch)
-        stores = []
-        for half, span in enumerate(spans):
-            wait_all(halves[half])
-            for tile in range(half * tiles // 2, (half + 1) * tiles // 2):
-                rows_of = pl.ds(tile * TILE, TILE)
-                total = ADAPTER_SCALE * dot(l_ref[tile], up_ref[h_ref[tile]], (0, 0))
-                for index in range(count):
-                    total = total + t_ref[index, rows_of, :].astype(F32)
-                o_ref[rows_of, :] = total.astype(BF16)
-            stores += start_all([pltpu.make_async_copy(o_ref.at[span], o_hbm.at[span], out_sems.at[half])])
-        wait_all(stores)
+
+    def kernel(h_ref, l_ref, up_ref, *refs):
+        for tile in range(tiles):
+            span = pl.ds(tile * TILE, TILE)
+            total = ADAPTER_SCALE * dot(l_ref[tile], up_ref[h_ref[tile]], (0, 0))
+            for ref in refs[:count]:
+                total = total + ref[span, :].astype(F32)
+            refs[count][span, :] = total.astype(BF16)
 
     return pl.pallas_call(
         kernel,
         out_shape=jax.ShapeDtypeStruct((rows, width), BF16),
-        in_specs=[SMEM] + [ANY] * (count + 2),
-        out_specs=HBM,
-        scratch_shapes=[
-            pltpu.VMEM((count, rows, width), BF16),
-            pltpu.VMEM(lowrank.shape, BF16),
-            pltpu.VMEM(up.shape, BF16),
-            pltpu.VMEM((rows, width), BF16),
-            pltpu.SemaphoreType.DMA((2, count)),
-            pltpu.SemaphoreType.DMA((2,)),
-            pltpu.SemaphoreType.DMA((2,)),
-        ],
+        in_specs=[SMEM] + [VMEM] * (count + 2),
+        out_specs=VMEM,
         compiler_params=params(PART),
         cost_estimate=cost(),
         name="finish_projected",
-    )(holders, *terms, lowrank, up)
+    )(holders, lowrank, up, *terms)
 
 
 def input_product(holders, pieces, value_matrix, back_low, down):

time: 110 us -> 110 us (level)
  waiting for transfers between devices: 15.9 us -> 19 us
  starting transfers between devices: 44.7 us -> 42.3 us
    ppermute x13, starting transfers between devices: 19.6 us -> 16.6 us  [along_x(): lax.ppermute(array, 'tensor', [(i, (i // 2 + k) % chips * 2 + i % 2) for...]
    ppermute x13, waiting for transfers between devices: 4.28 us -> 5.87 us  [along_x(): lax.ppermute(array, 'tensor', [(i, (i // 2 + k) % chips * 2 + i % 2) for...]
    all_to_all x1, waiting for transfers between devices: 4.27 us -> 5.83 us  [shards(): lax.all_to_all(send_down, 'dp', split_axis=0, concat_axis=0, tiled=True)]
  transfers between devices with their start and end apart: 25 -> 25, of which waited for: 7 -> 8; matrix products, arithmetic and copies ran while one was open for 3% -> 3% of each run, Pallas kernels for 36% -> 35%
where the time goes in v5:
time: 110 us; the launch traced here: 109 us
  starting transfers between devices  42.3 us (38%)
  Pallas kernels  39.7 us (36%)
  waiting for transfers between devices  19 us (17%)
  local copies, waits for them, and re-layouts  6.82 us (6%)
    ppermute x13, starting transfers between devices, along_x(): lax.ppermute(array, 'tensor', [(i, (i // 2 + k) % chips * 2 + i % 2) for...  16.6 us
    pallas_call x1, Pallas kernels, input_product(): pl.pallas_call(kernel, out_shape=jax.ShapeDtypeStruct((rows, features), B...  9.23 us
    all_to_all x1, starting transfers between devices, shards(): up = lax.all_to_all(send_up, 'dp', split_axis=0, concat_axis=0, tiled=True)  8.06 us
    all_to_all x1, starting transfers between devices, shards(): lax.all_to_all(send_up_terms, 'dp', split_axis=0, concat_axis=0, tiled=True)  6.57 us
    ppermute x13, waiting for transfers between devices, along_x(): lax.ppermute(array, 'tensor', [(i, (i // 2 + k) % chips * 2 + i % 2) for...  5.87 us
    all_to_all x1, waiting for transfers between devices, shards(): lax.all_to_all(send_down, 'dp', split_axis=0, concat_axis=0, tiled=True)  5.83 us
    pallas_call x1, Pallas kernels, base_product(): pl.pallas_call(kernel, out_shape=(shape, shape), in_specs=[VMEM, VMEM], o...  5.57 us
    all_to_all x1, starting transfers between devices, shards(): lax.all_to_all(send_down, 'dp', split_axis=0, concat_axis=0, tiled=True)  4.55 us
  transfers between devices with their start and end apart: 25, of which 8 were waited for; matrix products, arithmetic and copies ran while one was open for 3% of the time, Pallas kernels for 35%

profile of v5, /device:TPU:0, one launch (start us, length us, event | category | flops | bytes accessed | tf_op | source)
XLA Modules:
  0.0 109.4 jit_solution(3428402611260201702)
XLA Ops:
  0.6 2.9 %collective-permute-start.1 = (bf16[2048,128]{1,0:T(8,128)(2,1)}, bf16[2048,128]{1,0:T(8,128)(2,1)S(1)}, u32[]{:S(2)}, u32[]{:S(2)}) collective-permute-start(bf16[2048,128]{1,0:T(8,128)(2,1)} %w_ref.3), channel_id=1, source_target_pairs={{0,6},{1,7},{2,0},{3,1},{4,2},{5,3},{6,4},{7,5},{8,14},{9,15},{10,... | collective-permute-start | bytes 1572872 | tf_op jit(solution)/shard_map/ppermute | solution.py:487
  3.5 2.4 %route_up.1 = (s32[16]{0:T(128)}, s32[16]{0:T(128)}, bf16[16,64,128]{2,1,0:T(8,128)(2,1)}) custom-call(s32[128]{0:T(128)} %usage_hbm.1, s32[256]{0:T(256)} %map_hbm.1, s32[16]{0:T(128)} %entry_hbm.1, bf16[16,64,128]{2,1,0:T(8,128)(2,1)} %up_ref.1), custom_call_target="tpu_custom_call" | custom-call | flops 1024 | bytes 1024 | tf_op jit(solution)/shard_map/route_up/pallas_call | solution.py:92
  5.9 8.1 %all-to-all-start.1 = ((bf16[16,64,128]{2,1,0:T(8,128)(2,1)}), bf16[16,64,128]{2,1,0:T(8,128)(2,1)S(1)}, u32[]{:S(2)}, u32[]{:S(2)}) async-start(bf16[16,64,128]{2,1,0:T(8,128)(2,1)} %get-tuple-element.28), calls=%async_computation.1 | async-start | bytes 524288 | tf_op jit(solution)/shard_map/all_to_all | solution.py:521
  14.0 4.0 %select_down.1 = bf16[16,64,1024]{2,1,0:T(8,128)(2,1)} custom-call(s32[16]{0:T(128)} %get-tuple-element.26.rows_ref, bf16[16,64,1024]{2,1,0:T(8,128)(2,1)} %bitcast.2), custom_call_target="tpu_custom_call" | custom-call | flops 1024 | bytes 1024 | tf_op jit(solution)/shard_map/select_down/pallas_call | solution.py:126
  18.4 4.3 %all-to-all-done.1.up_ref = bf16[16,64,128]{2,1,0:T(8,128)(2,1)S(1)} async-done(((bf16[16,64,128]{2,1,0:T(8,128)(2,1)}), bf16[16,64,128]{2,1,0:T(8,128)(2,1)S(1)}, u32[]{:S(2)}, u32[]{:S(2)}) %all-to-all-start.1) | async-done | bytes 262176 | tf_op jit(solution)/shard_map/all_to_all | solution.py:521
  22.7 4.5 %all-to-all-start = ((bf16[16,64,1024]{2,1,0:T(8,128)(2,1)}), bf16[16,64,1024]{2,1,0:T(8,128)(2,1)S(1)}, u32[]{:S(2)}, u32[]{:S(2)}) async-start(bf16[16,64,1024]{2,1,0:T(8,128)(2,1)} %select_down.1), calls=%async_computation | async-start | bytes 4194304 | tf_op jit(solution)/shard_map/all_to_all | solution.py:524
  29.4 1.7 %collective-permute-done.2 = bf16[16,64,128]{2,1,0:T(8,128)(2,1)S(1)} collective-permute-done((bf16[16,64,128]{2,1,0:T(8,128)(2,1)S(1)}, bf16[16,64,128]{2,1,0:T(8,128)(2,1)S(1)}, u32[]{:S(2)}, u32[]{:S(2)}) %collective-permute-start.2) | collective-permute-done | bytes 262176 | tf_op jit(solution)/shard_map/ppermute | solution.py:481
  35.5 2.4 %collective-permute-start.11 = (bf16[1024,128]{1,0:T(8,128)(2,1)}, bf16[1024,128]{1,0:T(8,128)(2,1)}, u32[]{:S(2)}, u32[]{:S(2)}) collective-permute-start(bf16[1024,128]{1,0:T(8,128)(2,1)} %slice.9), channel_id=1, source_target_pairs={{0,6},{1,7},{2,0},{3,1},{4,2},{5,3},{6,4},{7,5},{8,14},{9,15},{10,... | collective-permute-start | bytes 786440 | tf_op jit(solution)/shard_map/ppermute | solution.py:487
  37.9 1.7 %slice.8 = bf16[1024,128]{1,0:T(8,128)(2,1)} slice(bf16[2048,128]{1,0:T(8,128)(2,1)} %copy-done.10), slice={[0:1024], [0:128]} | slice | bytes 524288 | tf_op jit(solution)/shard_map/slice | solution.py:526
  39.7 2.2 %copy-done = bf16[2048,1024]{1,0:T(8,128)(2,1)S(1)} copy-done((bf16[2048,1024]{1,0:T(8,128)(2,1)S(1)}, bf16[2048,1024]{1,0:T(8,128)(2,1)}, u32[]{:S(2)}) %copy-start) | copy-done | bytes 4194328
  41.9 5.6 %base_product.1 = (bf16[4,2048,128]{2,1,0:T(8,128)(2,1)}, bf16[4,2048,128]{2,1,0:T(8,128)(2,1)}) custom-call(bf16[2048,1024]{1,0:T(8,128)(2,1)S(1)} %copy-done, bf16[1024,1024]{1,0:T(8,128)(2,1)S(1)} %copy-done.3), custom_call_target="tpu_custom_call" | custom-call | flops 1024 | bytes 1024 | tf_op jit(solution)/shard_map/base_product/pallas_call | solution.py:174
  47.8 3.0 %gradient_terms.1 = bf16[16,64,1024]{2,1,0:T(8,128)(2,1)} custom-call(s32[16]{0:T(128)S(1)} %copy-done.7, bf16[16,64,128]{2,1,0:T(8,128)(2,1)S(1)} %add_convert_fusion.2.r_ref.refs_11_, bf16[2048,1024]{1,0:T(8,128)(2,1)S(1)} %copy-done.1), custom_call_target="tpu_custom_call" | custom-call | flops 1024 | bytes 1024 | tf_op jit(solution)/shard_map/gradient_terms/pallas_call | solution.py:330
  50.7 5.8 %all-to-all-done.down_ref.refs_12_ = bf16[16,64,1024]{2,1,0:T(8,128)(2,1)S(1)} async-done(((bf16[16,64,1024]{2,1,0:T(8,128)(2,1)}), bf16[16,64,1024]{2,1,0:T(8,128)(2,1)S(1)}, u32[]{:S(2)}, u32[]{:S(2)}) %all-to-all-start) | async-done | bytes 2097184 | tf_op jit(solution)/shard_map/all_to_all | solution.py:524
  56.6 4.4 %all-to-all-start.2 = ((bf16[16,64,1024]{2,1,0:T(8,128)(2,1)}), bf16[16,64,1024]{2,1,0:T(8,128)(2,1)}, u32[]{:S(2)}, u32[]{:S(2)}) async-start(bf16[16,64,1024]{2,1,0:T(8,128)(2,1)} %gradient_terms.1), calls=%async_computation.2 | async-start | bytes 4194304 | tf_op jit(solution)/shard_map/all_to_all | solution.py:541
  61.0 2.2 %copy-done.2 = bf16[2048,1024]{1,0:T(8,128)(2,1)S(1)} copy-done((bf16[2048,1024]{1,0:T(8,128)(2,1)S(1)}, bf16[2048,1024]{1,0:T(8,128)(2,1)}, u32[]{:S(2)}) %copy-start.2) | copy-done | bytes 4194328
  63.2 2.1 %low_product.1 = bf16[16,64,128]{2,1,0:T(8,128)(2,1)S(1)} custom-call(s32[16]{0:T(128)S(1)} %copy-done.7, bf16[16,64,1024]{2,1,0:T(8,128)(2,1)S(1)} %all-to-all-done.down_ref.refs_12_, bf16[2048,1024]{1,0:T(8,128)(2,1)S(1)} %copy-done.2), custom_call_target="tpu_custom_call" | custom-call | flops 1099511627776 | bytes 1024 | tf_op jit(solution)/shard_map/low_product/pallas_call | solution.py:255
  70.2 3.2 %add_cores.1 = (bf16[2048,128]{1,0:T(8,128)(2,1)S(1)}, bf16[2048,128]{1,0:T(8,128)(2,1)}, bf16[2048,128]{1,0:T(8,128)(2,1)}, bf16[2048,128]{1,0:T(8,128)(2,1)}) custom-call(bf16[4,2048,128]{2,1,0:T(8,128)(2,1)} %get-tuple-element.32.own_hbm, bf16[4,2048,128]{2,1,0:T(8,128)(2,1)} %collective-permute-done.17.other_hbm), custom_call_target="tpu_custom_call" | custom-call | flops 1024 | bytes 1024 | tf_op jit(solution)/shard_map/add_cores/pallas_call | solution.py:212
  73.4 1.9 %collective-permute-start.18 = (bf16[2048,128]{1,0:T(8,128)(2,1)}, bf16[2048,128]{1,0:T(8,128)(2,1)}, u32[]{:S(2)}, u32[]{:S(2)}) collective-permute-start(bf16[2048,128]{1,0:T(8,128)(2,1)} %get-tuple-element.40), channel_id=1, source_target_pairs={{0,2},{1,3},{2,4},{3,5},{4,6},{5,7},{6,0},{7,1},{8,10},{9,11},{10,... | collective-permute-start | bytes 1572872 | tf_op jit(solution)/shard_map/ppermute | solution.py:487
  78.9 9.2 %input_product.1 = bf16[2048,1024]{1,0:T(8,128)(2,1)} custom-call(s32[16]{0:T(128)S(1)} %copy-done.7, bf16[2048,128]{1,0:T(8,128)(2,1)} %w_ref.3, bf16[2048,128]{1,0:T(8,128)(2,1)} %copy-done.10, bf16[2048,128]{1,0:T(8,128)(2,1)} %copy-done.9, bf16[1024,128]{1,0:T(8,128)(2,1)} %collective-permute-done.10.refs_3_, ...), custom_call_target="tpu_custom_call" | custom-call | flops 1024 | bytes 1024 | tf_op jit(solution)/shard_map/input_product/pallas_call | solution.py:462
  88.4 1.6 %narrow_terms.1 = bf16[16,64,128]{2,1,0:T(8,128)(2,1)} custom-call(s32[16]{0:T(128)S(1)} %copy-done.7, bf16[16,64,128]{2,1,0:T(8,128)(2,1)S(1)} %add_convert_fusion.l_ref.r_ref, bf16[2048,128]{1,0:T(8,128)(2,1)S(1)} %copy-done.6), custom_call_target="tpu_custom_call" | custom-call | flops 1024 | bytes 1024 | tf_op jit(solution)/shard_map/narrow_terms/pallas_call | solution.py:276
  90.5 6.6 %all-to-all-start.3 = ((bf16[16,64,128]{2,1,0:T(8,128)(2,1)}), bf16[16,64,128]{2,1,0:T(8,128)(2,1)S(1)}, u32[]{:S(2)}, u32[]{:S(2)}) async-start(bf16[16,64,128]{2,1,0:T(8,128)(2,1)} %narrow_terms.1), calls=%async_computation.3 | async-start | bytes 524288 | tf_op jit(solution)/shard_map/all_to_all | solution.py:551
  97.1 3.6 %combine.1 = bf16[16,64,1024]{2,1,0:T(8,128)(2,1)} custom-call(s32[16]{0:T(128)S(1)} %copy-done.8, bf16[16,64,1024]{2,1,0:T(8,128)(2,1)} %all-to-all-done.2.r_hbm), custom_call_target="tpu_custom_call" | custom-call | flops 1024 | bytes 1024 | tf_op jit(solution)/shard_map/combine/pallas_call | solution.py:373
  100.6 4.5 %collective-permute-done.20.refs_3_ = bf16[2048,128]{1,0:T(8,128)(2,1)} collective-permute-done((bf16[2048,128]{1,0:T(8,128)(2,1)}, bf16[2048,128]{1,0:T(8,128)(2,1)}, u32[]{:S(2)}, u32[]{:S(2)}) %collective-permute-start.20) | collective-permute-done | bytes 524320 | tf_op jit(solution)/shard_map/ppermute | solution.py:487
  105.2 2.7 %finish_projected.1 = bf16[2048,128]{1,0:T(8,128)(2,1)} custom-call(s32[16]{0:T(128)S(1)} %copy-done.7, bf16[16,64,128]{2,1,0:T(8,128)(2,1)S(1)} %add_convert_fusion.l_ref.r_ref, bf16[16,64,128]{2,1,0:T(8,128)(2,1)S(1)} %all-to-all-done.1.up_ref, bf16[2048,128]{1,0:T(8,128)(2,1)S(1)} %get-tuple-element.39.refs_0_, ...), custom_call_target="tpu_custom_call" | custom-call | flops 1024 | bytes 1024 | tf_op jit(solution)/shard_map/finish_projected/pallas_call | solution.py:404
  (76 shorter events, 18.0 us)
Async XLA Ops:
  0.6 17.4 %collective-permute-start.1 = (bf16[2048,128]{1,0:T(8,128)(2,1)}, bf16[2048,128]{1,0:T(8,128)(2,1)S(1)}, u32[]{:S(2)}, u32[]{:S(2)}) collective-permute-start(bf16[2048,128]{1,0:T(8,128)(2,1)} %w_ref.3), channel_id=1, source_target_pairs={{0,6},{1,7},{2,0},{3,1},{4,2},{5,3},{6,4},{7,5},{8,14},{9,15},{10,... | collective-permute-start | bytes 1572872 | tf_op jit(solution)/shard_map/ppermute | solution.py:487
  3.5 14.8 %collective-permute-start = (bf16[2048,128]{1,0:T(8,128)(2,1)}, bf16[2048,128]{1,0:T(8,128)(2,1)S(1)}, u32[]{:S(2)}, u32[]{:S(2)}) collective-permute-start(bf16[2048,128]{1,0:T(8,128)(2,1)} %w_ref.3), channel_id=1, source_target_pairs={{0,2},{1,3},{2,4},{3,5},{4,6},{5,7},{6,0},{7,1},{8,10},{9,11},{10,... | collective-permute-start | bytes 1572872 | tf_op jit(solution)/shard_map/ppermute | solution.py:487
  5.9 16.8 %all-to-all-start.1 = ((bf16[16,64,128]{2,1,0:T(8,128)(2,1)}), bf16[16,64,128]{2,1,0:T(8,128)(2,1)S(1)}, u32[]{:S(2)}, u32[]{:S(2)}) async-start(bf16[16,64,128]{2,1,0:T(8,128)(2,1)} %get-tuple-element.28), calls=%async_computation.1 | async-start | bytes 524288 | tf_op jit(solution)/shard_map/all_to_all | solution.py:521
  22.7 33.9 %all-to-all-start = ((bf16[16,64,1024]{2,1,0:T(8,128)(2,1)}), bf16[16,64,1024]{2,1,0:T(8,128)(2,1)S(1)}, u32[]{:S(2)}, u32[]{:S(2)}) async-start(bf16[16,64,1024]{2,1,0:T(8,128)(2,1)} %select_down.1), calls=%async_computation | async-start | bytes 4194304 | tf_op jit(solution)/shard_map/all_to_all | solution.py:524
  27.2 3.9 %collective-permute-start.3 = (bf16[2048,128]{1,0:T(8,128)(2,1)S(1)}, bf16[2048,128]{1,0:T(8,128)(2,1)S(1)}, u32[]{:S(2)}, u32[]{:S(2)}) collective-permute-start(bf16[2048,128]{1,0:T(8,128)(2,1)S(1)} %copy-done.5), channel_id=1, source_target_pairs={{0,1},{1,0},{2,3},{3,2},{4,5},{5,4},{6,7},{7,6},{8,9},{9,8},{10,11... | collective-permute-start | bytes 1572872 | tf_op jit(solution)/shard_map/ppermute | solution.py:481
  27.3 3.9 %collective-permute-start.5 = (bf16[2048,128]{1,0:T(8,128)(2,1)S(1)}, bf16[2048,128]{1,0:T(8,128)(2,1)S(1)}, u32[]{:S(2)}, u32[]{:S(2)}) collective-permute-start(bf16[2048,128]{1,0:T(8,128)(2,1)S(1)} %collective-permute-done.1.refs_2_), channel_id=1, source_target_pairs={{0,1},{1,0},{2,3},{3,2},{4,5},{5,4},{6,7},{7,6},{8,9},{9,8},{10,11... | collective-permute-start | bytes 1572872 | tf_op jit(solution)/shard_map/ppermute | solution.py:481
  27.8 3.4 %collective-permute-start.4 = (bf16[2048,128]{1,0:T(8,128)(2,1)}, bf16[2048,128]{1,0:T(8,128)(2,1)S(1)}, u32[]{:S(2)}, u32[]{:S(2)}) collective-permute-start(bf16[2048,128]{1,0:T(8,128)(2,1)} %copy-done.10), channel_id=1, source_target_pairs={{0,1},{1,0},{2,3},{3,2},{4,5},{5,4},{6,7},{7,6},{8,9},{9,8},{10,11... | collective-permute-start | bytes 1572872 | tf_op jit(solution)/shard_map/ppermute | solution.py:481
  28.9 2.2 %collective-permute-start.2 = (bf16[16,64,128]{2,1,0:T(8,128)(2,1)S(1)}, bf16[16,64,128]{2,1,0:T(8,128)(2,1)S(1)}, u32[]{:S(2)}, u32[]{:S(2)}) collective-permute-start(bf16[16,64,128]{2,1,0:T(8,128)(2,1)S(1)} %back_product.1), channel_id=1, source_target_pairs={{0,1},{1,0},{2,3},{3,2},{4,5},{5,4},{6,7},{7,6},{8,9},{9,8},{10,11... | collective-permute-start | bytes 786440 | tf_op jit(solution)/shard_map/ppermute | solution.py:481
  31.2 16.2 %collective-permute-start.8 = (bf16[16,64,128]{2,1,0:T(8,128)(2,1)S(1)}, bf16[16,64,128]{2,1,0:T(8,128)(2,1)S(1)}, u32[]{:S(2)}, u32[]{:S(2)}) collective-permute-start(bf16[16,64,128]{2,1,0:T(8,128)(2,1)S(1)} %add_convert_fusion.3), channel_id=1, source_target_pairs={{0,4},{1,5},{2,6},{3,7},{4,0},{5,1},{6,2},{7,3},{8,12},{9,13},{10,... | collective-permute-start | bytes 786440 | tf_op jit(solution)/shard_map/ppermute | solution.py:487
  32.8 14.7 %collective-permute-start.7 = (bf16[16,64,128]{2,1,0:T(8,128)(2,1)S(1)}, bf16[16,64,128]{2,1,0:T(8,128)(2,1)S(1)}, u32[]{:S(2)}, u32[]{:S(2)}) collective-permute-start(bf16[16,64,128]{2,1,0:T(8,128)(2,1)S(1)} %add_convert_fusion.3), channel_id=1, source_target_pairs={{0,6},{1,7},{2,0},{3,1},{4,2},{5,3},{6,4},{7,5},{8,14},{9,15},{10,... | collective-permute-start | bytes 786440 | tf_op jit(solution)/shard_map/ppermute | solution.py:487
  33.9 13.5 %collective-permute-start.6 = (bf16[16,64,128]{2,1,0:T(8,128)(2,1)S(1)}, bf16[16,64,128]{2,1,0:T(8,128)(2,1)S(1)}, u32[]{:S(2)}, u32[]{:S(2)}) collective-permute-start(bf16[16,64,128]{2,1,0:T(8,128)(2,1)S(1)} %add_convert_fusion.3), channel_id=1, source_target_pairs={{0,2},{1,3},{2,4},{3,5},{4,6},{5,7},{6,0},{7,1},{8,10},{9,11},{10,... | collective-permute-start | bytes 786440 | tf_op jit(solution)/shard_map/ppermute | solution.py:487
  35.5 29.8 %collective-permute-start.11 = (bf16[1024,128]{1,0:T(8,128)(2,1)}, bf16[1024,128]{1,0:T(8,128)(2,1)}, u32[]{:S(2)}, u32[]{:S(2)}) collective-permute-start(bf16[1024,128]{1,0:T(8,128)(2,1)} %slice.9), channel_id=1, source_target_pairs={{0,6},{1,7},{2,0},{3,1},{4,2},{5,3},{6,4},{7,5},{8,14},{9,15},{10,... | collective-permute-start | bytes 786440 | tf_op jit(solution)/shard_map/ppermute | solution.py:487
  39.6 26.3 %collective-permute-start.10 = (bf16[1024,128]{1,0:T(8,128)(2,1)}, bf16[1024,128]{1,0:T(8,128)(2,1)}, u32[]{:S(2)}, u32[]{:S(2)}) collective-permute-start(bf16[1024,128]{1,0:T(8,128)(2,1)} %slice.8), channel_id=1, source_target_pairs={{0,2},{1,3},{2,4},{3,5},{4,6},{5,7},{6,0},{7,1},{8,10},{9,11},{10,... | collective-permute-start | bytes 786440 | tf_op jit(solution)/shard_map/ppermute | solution.py:487
  47.7 21.7 %collective-permute-start.17 = (bf16[4,2048,128]{2,1,0:T(8,128)(2,1)}, bf16[4,2048,128]{2,1,0:T(8,128)(2,1)}, u32[]{:S(2)}, u32[]{:S(2)}) collective-permute-start(bf16[4,2048,128]{2,1,0:T(8,128)(2,1)} %get-tuple-element.38), channel_id=1, source_target_pairs={{0,1},{1,0},{2,3},{3,2},{4,5},{5,4},{6,7},{7,6},{8,9},{9,8},{10,11... | collective-permute-start | bytes 6291464 | tf_op jit(solution)/shard_map/ppermute | solution.py:481
  56.6 33.9 %all-to-all-start.2 = ((bf16[16,64,1024]{2,1,0:T(8,128)(2,1)}), bf16[16,64,1024]{2,1,0:T(8,128)(2,1)}, u32[]{:S(2)}, u32[]{:S(2)}) async-start(bf16[16,64,1024]{2,1,0:T(8,128)(2,1)} %gradient_terms.1), calls=%async_computation.2 | async-start | bytes 4194304 | tf_op jit(solution)/shard_map/all_to_all | solution.py:541
  65.4 8.0 %collective-permute-start.16 = (bf16[1024,128]{1,0:T(8,128)(2,1)}, bf16[1024,128]{1,0:T(8,128)(2,1)S(1)}, u32[]{:S(2)}, u32[]{:S(2)}) collective-permute-start(bf16[1024,128]{1,0:T(8,128)(2,1)} %collective-permute-done.11.refs_4_), channel_id=1, source_target_pairs={{0,1},{1,0},{2,3},{3,2},{4,5},{5,4},{6,7},{7,6},{8,9},{9,8},{10,11... | collective-permute-start | bytes 786440 | tf_op jit(solution)/shard_map/ppermute | solution.py:481
  65.9 9.4 %collective-permute-start.15 = (bf16[1024,128]{1,0:T(8,128)(2,1)}, bf16[1024,128]{1,0:T(8,128)(2,1)S(1)}, u32[]{:S(2)}, u32[]{:S(2)}) collective-permute-start(bf16[1024,128]{1,0:T(8,128)(2,1)} %collective-permute-done.10.refs_3_), channel_id=1, source_target_pairs={{0,1},{1,0},{2,3},{3,2},{4,5},{5,4},{6,7},{7,6},{8,9},{9,8},{10,11... | collective-permute-start | bytes 786440 | tf_op jit(solution)/shard_map/ppermute | solution.py:481
  67.0 10.8 %collective-permute-start.14 = (bf16[16,64,128]{2,1,0:T(8,128)(2,1)S(1)}, bf16[16,64,128]{2,1,0:T(8,128)(2,1)S(1)}, u32[]{:S(2)}, u32[]{:S(2)}) collective-permute-start(bf16[16,64,128]{2,1,0:T(8,128)(2,1)S(1)} %add_convert_fusion.1), channel_id=1, source_target_pairs={{0,4},{1,5},{2,6},{3,7},{4,0},{5,1},{6,2},{7,3},{8,12},{9,13},{10,... | collective-permute-start | bytes 786440 | tf_op jit(solution)/shard_map/ppermute | solution.py:487
  68.2 20.0 %collective-permute-start.13 = (bf16[16,64,128]{2,1,0:T(8,128)(2,1)S(1)}, bf16[16,64,128]{2,1,0:T(8,128)(2,1)S(1)}, u32[]{:S(2)}, u32[]{:S(2)}) collective-permute-start(bf16[16,64,128]{2,1,0:T(8,128)(2,1)S(1)} %add_convert_fusion.1), channel_id=1, source_target_pairs={{0,6},{1,7},{2,0},{3,1},{4,2},{5,3},{6,4},{7,5},{8,14},{9,15},{10,... | collective-permute-start | bytes 786440 | tf_op jit(solution)/shard_map/ppermute | solution.py:487
  69.4 18.8 %collective-permute-start.12 = (bf16[16,64,128]{2,1,0:T(8,128)(2,1)S(1)}, bf16[16,64,128]{2,1,0:T(8,128)(2,1)S(1)}, u32[]{:S(2)}, u32[]{:S(2)}) collective-permute-start(bf16[16,64,128]{2,1,0:T(8,128)(2,1)S(1)} %add_convert_fusion.1), channel_id=1, source_target_pairs={{0,2},{1,3},{2,4},{3,5},{4,6},{5,7},{6,0},{7,1},{8,10},{9,11},{10,... | collective-permute-start | bytes 786440 | tf_op jit(solution)/shard_map/ppermute | solution.py:487
  73.4 27.2 %collective-permute-start.18 = (bf16[2048,128]{1,0:T(8,128)(2,1)}, bf16[2048,128]{1,0:T(8,128)(2,1)}, u32[]{:S(2)}, u32[]{:S(2)}) collective-permute-start(bf16[2048,128]{1,0:T(8,128)(2,1)} %get-tuple-element.40), channel_id=1, source_target_pairs={{0,2},{1,3},{2,4},{3,5},{4,6},{5,7},{6,0},{7,1},{8,10},{9,11},{10,... | collective-permute-start | bytes 1572872 | tf_op jit(solution)/shard_map/ppermute | solution.py:487
  75.3 25.3 %collective-permute-start.19 = (bf16[2048,128]{1,0:T(8,128)(2,1)}, bf16[2048,128]{1,0:T(8,128)(2,1)}, u32[]{:S(2)}, u32[]{:S(2)}) collective-permute-start(bf16[2048,128]{1,0:T(8,128)(2,1)} %get-tuple-element.41), channel_id=1, source_target_pairs={{0,6},{1,7},{2,0},{3,1},{4,2},{5,3},{6,4},{7,5},{8,14},{9,15},{10,... | collective-permute-start | bytes 1572872 | tf_op jit(solution)/shard_map/ppermute | solution.py:487
  77.8 27.4 %collective-permute-start.20 = (bf16[2048,128]{1,0:T(8,128)(2,1)}, bf16[2048,128]{1,0:T(8,128)(2,1)}, u32[]{:S(2)}, u32[]{:S(2)}) collective-permute-start(bf16[2048,128]{1,0:T(8,128)(2,1)} %get-tuple-element.42), channel_id=1, source_target_pairs={{0,4},{1,5},{2,6},{3,7},{4,0},{5,1},{6,2},{7,3},{8,12},{9,13},{10,... | collective-permute-start | bytes 1572872 | tf_op jit(solution)/shard_map/ppermute | solution.py:487
  90.5 17.4 %all-to-all-start.3 = ((bf16[16,64,128]{2,1,0:T(8,128)(2,1)}), bf16[16,64,128]{2,1,0:T(8,128)(2,1)S(1)}, u32[]{:S(2)}, u32[]{:S(2)}) async-start(bf16[16,64,128]{2,1,0:T(8,128)(2,1)} %narrow_terms.1), calls=%async_computation.3 | async-start | bytes 524288 | tf_op jit(solution)/shard_map/all_to_all | solution.py:551
  (17 other events, 130.1 us)
